TPU v7x, 128 devices: a whole 4x4x4 slice. The times are simulated.
128 devices in a mesh: sector: 32 (over y, x, z_lo), blk: 4 (over z_hi, core).
Axes of the slice: x: 4, y: 4, z: 4 (z_hi: 2, z_lo: 2; z = z_hi * 2 + z_lo), core: 2. Of those that a mesh axis runs over, the one named last changes fastest.
Arguments:
- features: bfloat16 [512, 64, 2048], P('sector', 'blk'), may hold values from -6 to 6
- residual_first: bfloat16 [3, 3, 64, 64], replicated, may hold values from -0.25 to 0.25
- residual_second: bfloat16 [3, 3, 64, 64], replicated, may hold values from -0.25 to 0.25
- shortcut_first: bfloat16 [3, 3, 64, 64], replicated, may hold values from -0.25 to 0.25
- shortcut_second: bfloat16 [3, 3, 64, 64], replicated, may hold values from -0.25 to 0.25
- first_reduce_weight: bfloat16 [3, 3, 3, 64, 128], replicated, may hold values from -0.15625 to 0.15625
- second_reduce_weight: bfloat16 [3, 3, 3, 128, 256], replicated, may hold values from -0.109375 to 0.109375
- coarse_kernel: bfloat16 [3, 3, 3, 256, 256], P(None, None, None, None, 'blk'), may hold values from -0.078125 to 0.078125
Outputs:
- coarse: bfloat16 [128, 16, 2048], P('sector', None, 'blk')
All inputs are finite; a program needn't handle non-finite values.
Results may differ from a plain program's by a relative error of at most 0.009.
Values may be sent and summed in bfloat16 or wider, within the bound.
No kernel may reach another device: no remote copies, remote signals or barrier semaphores. Data moves between devices by JAX's collectives and lax.ppermute only.
A program may use at most 128 MiB of HBM per device.

v0:
```python
import jax
import jax.numpy as jnp
from jax import lax
from jax.sharding import PartitionSpec as P


def padded_2(block, sides, width):
    for axis, dim in sides:
        count = lax.axis_size(axis)
        forward = [(i, i + 1) for i in range(count - 1)]
        forward.append((count - 1, 0))
        backward = [(target, source) for source, target in forward]
        low = lax.ppermute(
            lax.slice_in_dim(block, block.shape[dim] - width, None, axis=dim), axis, forward
        )
        high = lax.ppermute(lax.slice_in_dim(block, 0, width, axis=dim), axis, backward)
        block = jnp.concatenate([low, block, high], axis=dim)
    return block


def passed_along(x, axis, by):
    devices = lax.axis_size(axis)
    return lax.ppermute(x, axis, [(i, (i + by) % devices) for i in range(devices)])


def passed_along_2(x, axis, by):
    devices = lax.axis_size(axis)
    pairs = [(i, i + by) for i in range(devices) if 0 <= i + by < devices]
    return lax.ppermute(x, axis, pairs)


def leaky_relu(values):
    return jnp.where(values > 0, values, 0.01 * values)


def pad_pairs(source, before, after):
    return jnp.pad(source, ((0, 0), (0, 0), (before, after), (0, 0)))


def pair_weights(filter_weight):
    zero_block = jnp.zeros((3,) + filter_weight.shape[2:], filter_weight.dtype)
    per_offset = []
    for offset_pair in (-1, 0, 1):
        row_blocks = []
        for slot_in in range(2):
            col_blocks = []
            for slot_out in range(2):
                tap_index = 2 * offset_pair + slot_in - slot_out + 1
                if 0 <= tap_index <= 2:
                    col_blocks.append(filter_weight[:, tap_index])
                else:
                    col_blocks.append(zero_block)
            row_blocks.append(jnp.concatenate(col_blocks, axis=2))
        per_offset.append(jnp.concatenate(row_blocks, axis=1))
    return jnp.stack(per_offset, axis=1)


def pair_conv(padded, weights, along, first_len, second_len, pairs):
    summed = None
    for spatial in range(3):
        for offset in range(3):
            if along == 0:
                portion = padded[
                    spatial : spatial + first_len, 0:second_len, offset : offset + pairs
                ]
            else:
                portion = padded[
                    0:first_len, spatial : spatial + second_len, offset : offset + pairs
                ]
            summand = jnp.einsum(
                "pqhc,cd->pqhd",
                portion,
                weights[spatial, offset],
                preferred_element_type=jnp.float32,
            )
            summed = summand if summed is None else summed + summand
    return summed


def context_block(features, residual_first, residual_second, shortcut_first, shortcut_second):
    azimuth, radius, flat = features.shape
    channels = residual_first.shape[-1]
    pairs = flat // (2 * channels)
    extended = padded_2(features, (("sector", 0), ("blk", 1)), 1)
    band_index = lax.axis_index("blk")
    band_count = lax.axis_size("blk")
    row_ids = jnp.arange(radius + 2)
    outside = (row_ids == 0) & (band_index == 0) | (row_ids == radius + 1) & (
        band_index == band_count - 1
    )
    extended = jnp.where(outside[None, :, None], jnp.zeros((), extended.dtype), extended)
    padded = pad_pairs(extended.reshape(azimuth + 2, radius + 2, pairs, 2 * channels), 1, 1)
    first_res = leaky_relu(
        pair_conv(padded, pair_weights(residual_first), 0, azimuth, radius + 2, pairs)
    ).astype(jnp.bfloat16)
    first_short = leaky_relu(
        pair_conv(padded, pair_weights(shortcut_first), 1, azimuth + 2, radius, pairs)
    ).astype(jnp.bfloat16)
    res_part = leaky_relu(
        pair_conv(
            pad_pairs(first_res, 1, 1), pair_weights(residual_second), 1, azimuth, radius, pairs
        )
    )
    short_part = leaky_relu(
        pair_conv(
            pad_pairs(first_short, 1, 1), pair_weights(shortcut_second), 0, azimuth, radius, pairs
        )
    )
    return (res_part + short_part).astype(jnp.bfloat16)


def reduce_grid(feature_volume, filter_weight):
    azimuth, radius, pairs, packed = feature_volume.shape
    lower_rim = passed_along(
        feature_volume[azimuth - 1 :].reshape(1, radius, pairs * packed), "sector", 1
    )
    widened = jnp.concatenate([lower_rim.reshape(1, radius, pairs, packed), feature_volume], axis=0)
    radial_rim = passed_along_2(
        widened[:, radius - 1 :].reshape(azimuth + 1, 1, pairs * packed), "blk", 1
    )
    widened = jnp.concatenate([radial_rim.reshape(azimuth + 1, 1, pairs, packed), widened], axis=1)
    previous = pad_pairs(widened, 1, 0)[:, :, 0:pairs]
    current_weight = jnp.concatenate([filter_weight[:, :, 1], filter_weight[:, :, 2]], axis=2)
    previous_weight = jnp.concatenate(
        [jnp.zeros_like(filter_weight[:, :, 0]), filter_weight[:, :, 0]], axis=2
    )
    summed = None
    for along in range(3):
        for across in range(3):
            current_part = widened[along : along + azimuth : 2, across : across + radius : 2]
            previous_part = previous[along : along + azimuth : 2, across : across + radius : 2]
            summand = jnp.einsum(
                "pqhc,cd->pqhd",
                current_part,
                current_weight[along, across],
                preferred_element_type=jnp.float32,
            )
            summand = summand + jnp.einsum(
                "pqhc,cd->pqhd",
                previous_part,
                previous_weight[along, across],
                preferred_element_type=jnp.float32,
            )
            summed = summand if summed is None else summed + summand
    return leaky_relu(summed).astype(jnp.bfloat16)


def per_device(
    features,
    residual_first,
    residual_second,
    shortcut_first,
    shortcut_second,
    first_reduce_weight,
    second_reduce_weight,
    coarse_kernel,
):
    finer_features = context_block(
        features, residual_first, residual_second, shortcut_first, shortcut_second
    )
    halved_features = reduce_grid(finer_features, first_reduce_weight)
    half_az, half_rad, half_hgt, half_ch = halved_features.shape
    halved_features = halved_features.reshape(half_az, half_rad, half_hgt // 2, 2 * half_ch)
    quartered_features = reduce_grid(halved_features, second_reduce_weight)
    azimuth, band_rows, height, channels = quartered_features.shape
    width_out = coarse_kernel.shape[-1]
    slab_rows = band_rows * lax.axis_size("blk")
    first_channel = lax.axis_index("blk") * width_out
    whole_slab = lax.all_gather(quartered_features, "blk", axis=1, tiled=True)
    extended = padded_2(whole_slab, (("sector", 0),), 1)
    extended = jnp.pad(extended, ((0, 0), (1, 1), (1, 1), (0, 0)))
    summed = None
    for along in range(3):
        for across in range(3):
            for level_tap in range(3):
                portion = extended[
                    along : along + azimuth,
                    across : across + slab_rows,
                    level_tap : level_tap + height,
                ]
                summand = jnp.einsum(
                    "pqhc,cd->pqhd",
                    portion,
                    coarse_kernel[along, across, level_tap],
                    preferred_element_type=jnp.float32,
                )
                summed = summand if summed is None else summed + summand
    own_part = lax.dynamic_slice_in_dim(whole_slab, first_channel, width_out, 3)
    result = (own_part.astype(jnp.float32) + leaky_relu(summed)).astype(jnp.bfloat16)
    return jnp.transpose(result, (0, 1, 3, 2)).reshape(azimuth, slab_rows, width_out * height)


def solution(mesh):
    in_specs = (
        P("sector", "blk", None),
        P(),
        P(),
        P(),
        P(),
        P(),
        P(),
        P(None, None, None, None, "blk"),
    )
    out_specs = P("sector", None, "blk")
    return jax.shard_map(
        per_device, mesh=mesh, in_specs=in_specs, out_specs=out_specs, check_vma=False
    )
```

profile of v0, /device:TPU:1, one launch (start us, length us, event | category | flops | bytes accessed | tf_op | source)
XLA Modules:
  0.0 147.9 jit_solution(896843233312937414)
XLA Ops:
  0.0 1.9 %copy.49 = bf16[16,16,2048]{2,0,1:T(8,128)(2,1)S(1)} copy(bf16[16,16,2048]{2,1,0:T(8,128)(2,1)} %param.8) | data formatting | bytes 2097152 | tf_op args[0]
  2.8 2.5 %collective-permute-start = (bf16[1,16,2048]{2,0,1:T(2,128)(2,1)}, bf16[1,16,2048]{2,0,1:T(2,128)(2,1)}, u32[]{:S(2)}, u32[]{:S(2)}) collective-permute-start(bf16[1,16,2048]{2,0,1:T(2,128)(2,1)} %get-tuple-element.10), channel_id=1, source_target_pairs={{0,4},{4,8},{8,12},{12,16},{16,20},{20,24},{24,28},{28,32},{32,36}... | collective-permute-start | bytes 196616 | tf_op jit(solution)/shard_map/ppermute | solution.py:13
  5.3 4.6 %collective-permute-start.1 = (bf16[1,16,2048]{2,0,1:T(2,128)(2,1)}, bf16[1,16,2048]{2,0,1:T(2,128)(2,1)}, u32[]{:S(2)}, u32[]{:S(2)}) collective-permute-start(bf16[1,16,2048]{2,0,1:T(2,128)(2,1)} %get-tuple-element.11), channel_id=1, source_target_pairs={{4,0},{8,4},{12,8},{16,12},{20,16},{24,20},{28,24},{32,28},{36,32}... | collective-permute-start | bytes 196616 | tf_op jit(solution)/shard_map/ppermute | solution.py:16
  18.3 4.1 %collective-permute-start.2 = (bf16[18,1,2048]{2,0,1:T(8,128)(2,1)}, bf16[18,1,2048]{2,0,1:T(8,128)(2,1)}, u32[]{:S(2)}, u32[]{:S(2)}) collective-permute-start(bf16[18,1,2048]{2,0,1:T(8,128)(2,1)} %get-tuple-element.8), channel_id=1, source_target_pairs={{0,1},{1,2},{2,3},{3,0},{4,5},{5,6},{6,7},{7,4},{8,9},{9,10},{10,1... | collective-permute-start | bytes 221192 | tf_op jit(solution)/shard_map/ppermute | solution.py:13
  22.5 2.6 %reshape.226 = bf16[18,16,16,128]{3,2,0,1:T(8,128)(2,1)S(1)} reshape(bf16[18,16,2048]{2,0,1:T(8,128)(2,1)} %copy-done.3) | data formatting | bytes 2359296 | tf_op jit(solution)/shard_map/concatenate | solution.py:17
  26.1 2.2 %collective-permute-done.3 = bf16[18,1,2048]{2,0,1:T(8,128)(2,1)} collective-permute-done((bf16[18,1,2048]{2,0,1:T(8,128)(2,1)}, bf16[18,1,2048]{2,0,1:T(8,128)(2,1)}, u32[]{:S(2)}, u32[]{:S(2)}) %collective-permute-start.3) | collective-permute-done | bytes 73760 | tf_op jit(solution)/shard_map/ppermute | solution.py:16
  38.6 1.8 %fusion.39 = f32[16,16,16,128]{3,2,1,0:T(8,128)} fusion(bf16[16,18,16,128]{3,2,1,0:T(8,128)(2,1)S(1)} %fusion, bf16[3,64,64]{2,1,0:T(8,128)(2,1)S(1)} %copy-done.15), kind=kOutput, calls=%fused_computation.147 | convolution fusion | flops 134217728 | bytes 3301376 | tf_op jit(solution)/shard_map/pqhc,cd->pqhd/dot_general | solution.py:70
  40.5 1.8 %fusion.40 = f32[16,16,16,128]{3,2,1,0:T(8,128)} fusion(bf16[16,18,16,128]{3,2,1,0:T(8,128)(2,1)S(1)} %fusion, bf16[3,64,64]{2,1,0:T(8,128)(2,1)S(1)} %copy-done.13), kind=kOutput, calls=%fused_computation.148 | convolution fusion | flops 134217728 | bytes 3301376 | tf_op jit(solution)/shard_map/pqhc,cd->pqhd/dot_general | solution.py:70
  44.0 1.9 %fusion.42 = f32[16,16,16,128]{3,2,1,0:T(8,128)} fusion(bf16[16,18,16,128]{3,2,1,0:T(8,128)(2,1)S(1)} %fusion, bf16[3,64,64]{2,1,0:T(8,128)(2,1)S(1)} %copy-done.13), kind=kOutput, calls=%fused_computation.150 | convolution fusion | flops 134217728 | bytes 3301376 | tf_op jit(solution)/shard_map/pqhc,cd->pqhd/dot_general | solution.py:70
  45.9 1.8 %fusion.43 = f32[16,16,16,128]{3,2,1,0:T(8,128)} fusion(bf16[16,18,16,128]{3,2,1,0:T(8,128)(2,1)S(1)} %fusion, bf16[3,64,64]{2,1,0:T(8,128)(2,1)S(1)} %copy-done.15), kind=kOutput, calls=%fused_computation.151 | convolution fusion | flops 134217728 | bytes 3301376 | tf_op jit(solution)/shard_map/pqhc,cd->pqhd/dot_general | solution.py:70
  47.7 1.8 %fusion.44 = f32[16,16,16,128]{3,2,1,0:T(8,128)} fusion(bf16[16,18,16,128]{3,2,1,0:T(8,128)(2,1)S(1)} %fusion, bf16[3,64,64]{2,1,0:T(8,128)(2,1)S(1)} %copy-done.13), kind=kOutput, calls=%fused_computation.152 | convolution fusion | flops 134217728 | bytes 3301376 | tf_op jit(solution)/shard_map/pqhc,cd->pqhd/dot_general | solution.py:70
  53.7 1.9 %convert_reduce_fusion = (u32[16,16,128]{2,1,0:T(8,128)S(1)}, f32[18,16,16,128]{3,2,1,0:T(8,128)S(1)}) fusion(bf16[3,64,64]{2,1,0:T(8,128)(2,1)S(1)} %copy-done.17, bf16[18,18,16,128]{3,2,1,0:T(8,128)(2,1)S(1)} %maximum_select_fusion, f32[18,16,16,128]{3,2,1,0:T(8,128)S(1)} %fusion.275, f32[18,16,16,128]{3,2,1,0:T(8,128)S(1)} %fusion.24, ...), kind=kOutput, calls=%fused_computation.32 | convolution fusion | flops 158040064 | bytes 22716416 | tf_op jit(solution)/shard_map/pqhc,cd->pqhd/dot_general | solution.py:70
  61.7 1.9 %fusion.46 = f32[16,16,16,128]{3,2,1,0:T(8,128)} fusion(bf16[18,16,16,128]{3,2,1,0:T(8,128)(2,1)S(1)} %fusion.1, bf16[3,64,64]{2,1,0:T(8,128)(2,1)S(1)} %get-tuple-element.25), kind=kOutput, calls=%fused_computation.154 | convolution fusion | flops 134217728 | bytes 3301376 | tf_op jit(solution)/shard_map/pqhc,cd->pqhd/dot_general | solution.py:70
  65.4 1.9 %fusion.48 = f32[16,16,16,128]{3,2,1,0:T(8,128)} fusion(bf16[18,16,16,128]{3,2,1,0:T(8,128)(2,1)S(1)} %fusion.1, bf16[3,64,64]{2,1,0:T(8,128)(2,1)S(1)} %get-tuple-element.25), kind=kOutput, calls=%fused_computation.156 | convolution fusion | flops 134217728 | bytes 3301376 | tf_op jit(solution)/shard_map/pqhc,cd->pqhd/dot_general | solution.py:70
  67.3 1.8 %fusion.49 = f32[16,16,16,128]{3,2,1,0:T(8,128)} fusion(bf16[18,16,16,128]{3,2,1,0:T(8,128)(2,1)S(1)} %fusion.1, bf16[3,64,64]{2,1,0:T(8,128)(2,1)S(1)} %copy-done.11), kind=kOutput, calls=%fused_computation.157 | convolution fusion | flops 134217728 | bytes 3301376 | tf_op jit(solution)/shard_map/pqhc,cd->pqhd/dot_general | solution.py:70
  69.1 1.8 %fusion.50 = f32[16,16,16,128]{3,2,1,0:T(8,128)} fusion(bf16[18,16,16,128]{3,2,1,0:T(8,128)(2,1)S(1)} %fusion.1, bf16[3,64,64]{2,1,0:T(8,128)(2,1)S(1)} %get-tuple-element.25), kind=kOutput, calls=%fused_computation.158 | convolution fusion | flops 134217728 | bytes 3301376 | tf_op jit(solution)/shard_map/pqhc,cd->pqhd/dot_general | solution.py:70
  71.8 9.5 %fusion.3 = bf16[16,16,16,128]{3,2,1,0:T(8,128)(2,1)S(1)} fusion(f32[16,16,16,128]{3,2,1,0:T(8,128)} %fusion.50, f32[16,16,16,128]{3,2,1,0:T(8,128)} %fusion.49, f32[16,16,16,128]{3,2,1,0:T(8,128)} %fusion.48, f32[16,16,16,128]{3,2,1,0:T(8,128)} %fusion.273, f32[16,16,16,128]{3,2,1,0:T(8,128)} %fusion.47, f32[16,16,16,128]{3,2,1,0:T(8,128)} %fusion.46, ...), kind=kOutput, calls=%fused_computation.66 | convolution fusion | flops 146800640 | bytes 37912576 | tf_op jit(solution)/shard_map/pqhc,cd->pqhd/dot_general | solution.py:70
  85.5 6.3 %collective-permute-done.4 = bf16[1,16,2048]{2,1,0:T(8,128)(2,1)S(1)} collective-permute-done((bf16[1,16,2048]{2,1,0:T(8,128)(2,1)S(1)}, bf16[1,16,2048]{2,1,0:T(8,128)(2,1)S(1)}, u32[]{:S(2)}, u32[]{:S(2)}) %collective-permute-start.4) | collective-permute-done | bytes 65568 | tf_op jit(solution)/shard_map/ppermute | solution.py:23
  94.0 4.7 %collective-permute-start.5 = (bf16[17,1,2048]{2,0,1:T(8,128)(2,1)S(1)}, bf16[17,1,2048]{2,0,1:T(8,128)(2,1)S(1)}, u32[]{:S(2)}, u32[]{:S(2)}) collective-permute-start(bf16[17,1,2048]{2,0,1:T(8,128)(2,1)S(1)} %reshape.119), channel_id=1, source_target_pairs={{0,1},{1,2},{2,3},{4,5},{5,6},{6,7},{8,9},{9,10},{10,11},{12,13},{... | collective-permute-start | bytes 208904 | tf_op jit(solution)/shard_map/ppermute | solution.py:29
  106.3 6.8 %collective-permute-done.6 = bf16[1,8,2048]{2,1,0:T(8,128)(2,1)S(1)} collective-permute-done((bf16[1,8,2048]{2,1,0:T(8,128)(2,1)S(1)}, bf16[1,8,2048]{2,1,0:T(8,128)(2,1)S(1)}, u32[]{:S(2)}, u32[]{:S(2)}) %collective-permute-start.6) | collective-permute-done | bytes 32800 | tf_op jit(solution)/shard_map/ppermute | solution.py:23
  113.3 7.0 %collective-permute-start.7 = (bf16[9,1,2048]{2,0,1:T(8,128)(2,1)S(1)}, bf16[9,1,2048]{2,0,1:T(8,128)(2,1)S(1)}, u32[]{:S(2)}, u32[]{:S(2)}) collective-permute-start(bf16[9,1,2048]{2,0,1:T(8,128)(2,1)S(1)} %reshape.124), channel_id=1, source_target_pairs={{0,1},{1,2},{2,3},{4,5},{5,6},{6,7},{8,9},{9,10},{10,11},{12,13},{... | collective-permute-start | bytes 110600 | tf_op jit(solution)/shard_map/ppermute | solution.py:29
  123.9 8.5 %all_gather.3 = bf16[4,16,8,256]{3,2,1,0:T(8,128)(2,1)S(1)} all-gather(bf16[4,4,8,256]{3,2,1,0:T(8,128)(2,1)S(1)} %fusion.122), channel_id=1, replica_groups=mesh['sector'=32,'blk'=4] {'blk'}, dimensions={1}, use_global_device_ids=true | all-gather | bytes 327680 | tf_op jit(solution)/shard_map/all_gather | solution.py:169
  132.5 5.7 %collective-permute-start.9 = (bf16[1,16,8,256]{3,2,1,0:T(8,128)(2,1)S(1)}, bf16[1,16,8,256]{3,2,1,0:T(8,128)(2,1)S(1)}, u32[]{:S(2)}, u32[]{:S(2)}) collective-permute-start(bf16[1,16,8,256]{3,2,1,0:T(8,128)(2,1)S(1)} %get-tuple-element.16), channel_id=1, source_target_pairs={{4,0},{8,4},{12,8},{16,12},{20,16},{24,20},{28,24},{32,28},{36,32}... | collective-permute-start | bytes 196616 | tf_op jit(solution)/shard_map/ppermute | solution.py:16
  138.2 2.1 %collective-permute-done.8 = bf16[1,16,8,256]{3,2,1,0:T(8,128)(2,1)S(1)} collective-permute-done((bf16[1,16,8,256]{3,2,1,0:T(8,128)(2,1)S(1)}, bf16[1,16,8,256]{3,2,1,0:T(8,128)(2,1)S(1)}, u32[]{:S(2)}, u32[]{:S(2)}) %collective-permute-start.8) | collective-permute-done | bytes 65568 | tf_op jit(solution)/shard_map/ppermute | solution.py:13
  (203 shorter events, 60.1 us)
Async XLA Ops:
  0.0 10.0 %copy-start.26 = (bf16[3,3,64,64]{3,2,1,0:T(8,128)(2,1)S(1)}, bf16[3,3,64,64]{3,2,1,0:T(8,128)(2,1)}, u32[]{:S(2)}) copy-start(bf16[3,3,64,64]{3,2,1,0:T(8,128)(2,1)} %param.9) | copy-start | bytes 221188
  0.0 10.0 %copy-start.27 = (bf16[3,3,64,64]{3,2,1,0:T(8,128)(2,1)S(1)}, bf16[3,3,64,64]{3,2,1,0:T(8,128)(2,1)}, u32[]{:S(2)}) copy-start(bf16[3,3,64,64]{3,2,1,0:T(8,128)(2,1)} %param.10) | copy-start | bytes 221188
  0.0 10.0 %copy-start.28 = (bf16[3,3,64,64]{3,2,1,0:T(8,128)(2,1)S(1)}, bf16[3,3,64,64]{3,2,1,0:T(8,128)(2,1)}, u32[]{:S(2)}) copy-start(bf16[3,3,64,64]{3,2,1,0:T(8,128)(2,1)} %param.11) | copy-start | bytes 221188
  0.0 10.1 %copy-start.29 = (bf16[3,3,64,64]{3,2,1,0:T(8,128)(2,1)S(1)}, bf16[3,3,64,64]{3,2,1,0:T(8,128)(2,1)}, u32[]{:S(2)}) copy-start(bf16[3,3,64,64]{3,2,1,0:T(8,128)(2,1)} %param.12) | copy-start | bytes 221188
  0.0 10.1 %copy-start.21 = (bf16[3,3,3,64,128]{4,3,2,1,0:T(8,128)(2,1)S(1)}, bf16[3,3,3,64,128]{4,3,2,1,0:T(8,128)(2,1)}, u32[]{:S(2)}) copy-start(bf16[3,3,3,64,128]{4,3,2,1,0:T(8,128)(2,1)} %param.13) | copy-start | bytes 1327108
  2.8 11.9 %collective-permute-start = (bf16[1,16,2048]{2,0,1:T(2,128)(2,1)}, bf16[1,16,2048]{2,0,1:T(2,128)(2,1)}, u32[]{:S(2)}, u32[]{:S(2)}) collective-permute-start(bf16[1,16,2048]{2,0,1:T(2,128)(2,1)} %get-tuple-element.10), channel_id=1, source_target_pairs={{0,4},{4,8},{8,12},{12,16},{16,20},{20,24},{24,28},{28,32},{32,36}... | collective-permute-start | bytes 196616 | tf_op jit(solution)/shard_map/ppermute | solution.py:13
  5.3 9.4 %collective-permute-start.1 = (bf16[1,16,2048]{2,0,1:T(2,128)(2,1)}, bf16[1,16,2048]{2,0,1:T(2,128)(2,1)}, u32[]{:S(2)}, u32[]{:S(2)}) collective-permute-start(bf16[1,16,2048]{2,0,1:T(2,128)(2,1)} %get-tuple-element.11), channel_id=1, source_target_pairs={{4,0},{8,4},{12,8},{16,12},{20,16},{24,20},{28,24},{32,28},{36,32}... | collective-permute-start | bytes 196616 | tf_op jit(solution)/shard_map/ppermute | solution.py:16
  10.0 2.4 %copy-start.12 = (bf16[3,64,64]{2,1,0:T(8,128)(2,1)}, bf16[3,64,64]{2,1,0:T(8,128)(2,1)S(1)}, u32[]{:S(2)}) copy-start(bf16[3,64,64]{2,1,0:T(8,128)(2,1)S(1)} %get-tuple-element.19) | copy-start | bytes 73732
  10.0 2.4 %copy-start.14 = (bf16[3,64,64]{2,1,0:T(8,128)(2,1)}, bf16[3,64,64]{2,1,0:T(8,128)(2,1)S(1)}, u32[]{:S(2)}) copy-start(bf16[3,64,64]{2,1,0:T(8,128)(2,1)S(1)} %get-tuple-element.17) | copy-start | bytes 73732
  10.1 3.1 %copy-start.16 = (bf16[3,64,64]{2,1,0:T(8,128)(2,1)}, bf16[3,64,64]{2,1,0:T(8,128)(2,1)S(1)}, u32[]{:S(2)}) copy-start(bf16[3,64,64]{2,1,0:T(8,128)(2,1)S(1)} %get-tuple-element.28) | copy-start | bytes 73732
  10.1 3.8 %copy-start.10 = (bf16[3,64,64]{2,1,0:T(8,128)(2,1)}, bf16[3,64,64]{2,1,0:T(8,128)(2,1)S(1)}, u32[]{:S(2)}) copy-start(bf16[3,64,64]{2,1,0:T(8,128)(2,1)S(1)} %get-tuple-element.24) | copy-start | bytes 73732
  18.3 6.8 %collective-permute-start.2 = (bf16[18,1,2048]{2,0,1:T(8,128)(2,1)}, bf16[18,1,2048]{2,0,1:T(8,128)(2,1)}, u32[]{:S(2)}, u32[]{:S(2)}) collective-permute-start(bf16[18,1,2048]{2,0,1:T(8,128)(2,1)} %get-tuple-element.8), channel_id=1, source_target_pairs={{0,1},{1,2},{2,3},{3,0},{4,5},{5,6},{6,7},{7,4},{8,9},{9,10},{10,1... | collective-permute-start | bytes 221192 | tf_op jit(solution)/shard_map/ppermute | solution.py:13
  22.5 5.9 %collective-permute-start.3 = (bf16[18,1,2048]{2,0,1:T(8,128)(2,1)}, bf16[18,1,2048]{2,0,1:T(8,128)(2,1)}, u32[]{:S(2)}, u32[]{:S(2)}) collective-permute-start(bf16[18,1,2048]{2,0,1:T(8,128)(2,1)} %get-tuple-element.9), channel_id=1, source_target_pairs={{1,0},{2,1},{3,2},{0,3},{5,4},{6,5},{7,6},{4,7},{9,8},{10,9},{11,1... | collective-permute-start | bytes 221192 | tf_op jit(solution)/shard_map/ppermute | solution.py:16
  25.1 4.5 %copy-start.24 = (bf16[3,128,128]{2,1,0:T(8,128)(2,1)S(1)}, bf16[3,128,128]{2,1,0:T(8,128)(2,1)}, u32[]{:S(2)}) copy-start(bf16[3,128,128]{2,1,0:T(8,128)(2,1)} %maximum_maximum_fusion.1) | copy-start | bytes 294916
  67.3 3.6 %copy-start.1 = (f32[16,16,16,128]{3,2,1,0:T(8,128)S(1)}, f32[16,16,16,128]{3,2,1,0:T(8,128)}, u32[]{:S(2)}) copy-start(f32[16,16,16,128]{3,2,1,0:T(8,128)} %fusion.39) | copy-start | bytes 6291460
  67.3 3.6 %copy-start.2 = (f32[16,16,16,128]{3,2,1,0:T(8,128)S(1)}, f32[16,16,16,128]{3,2,1,0:T(8,128)}, u32[]{:S(2)}) copy-start(f32[16,16,16,128]{3,2,1,0:T(8,128)} %fusion.40) | copy-start | bytes 6291460
  69.1 2.7 %copy-start = (f32[16,16,16,128]{3,2,1,0:T(8,128)S(1)}, f32[16,16,16,128]{3,2,1,0:T(8,128)}, u32[]{:S(2)}) copy-start(f32[16,16,16,128]{3,2,1,0:T(8,128)} %fusion.280) | copy-start | bytes 6291460
  84.4 7.4 %collective-permute-start.4 = (bf16[1,16,2048]{2,1,0:T(8,128)(2,1)S(1)}, bf16[1,16,2048]{2,1,0:T(8,128)(2,1)S(1)}, u32[]{:S(2)}, u32[]{:S(2)}) collective-permute-start(bf16[1,16,2048]{2,1,0:T(8,128)(2,1)S(1)} %reshape.117), channel_id=1, source_target_pairs={{0,4},{4,8},{8,12},{12,16},{16,20},{20,24},{24,28},{28,32},{32,36}... | collective-permute-start | bytes 196616 | tf_op jit(solution)/shard_map/ppermute | solution.py:23
  94.0 6.4 %collective-permute-start.5 = (bf16[17,1,2048]{2,0,1:T(8,128)(2,1)S(1)}, bf16[17,1,2048]{2,0,1:T(8,128)(2,1)S(1)}, u32[]{:S(2)}, u32[]{:S(2)}) collective-permute-start(bf16[17,1,2048]{2,0,1:T(8,128)(2,1)S(1)} %reshape.119), channel_id=1, source_target_pairs={{0,1},{1,2},{2,3},{4,5},{5,6},{6,7},{8,9},{9,10},{10,11},{12,13},{... | collective-permute-start | bytes 208904 | tf_op jit(solution)/shard_map/ppermute | solution.py:29
  106.0 7.1 %collective-permute-start.6 = (bf16[1,8,2048]{2,1,0:T(8,128)(2,1)S(1)}, bf16[1,8,2048]{2,1,0:T(8,128)(2,1)S(1)}, u32[]{:S(2)}, u32[]{:S(2)}) collective-permute-start(bf16[1,8,2048]{2,1,0:T(8,128)(2,1)S(1)} %reshape.121), channel_id=1, source_target_pairs={{0,4},{4,8},{8,12},{12,16},{16,20},{20,24},{24,28},{28,32},{32,36}... | collective-permute-start | bytes 98312 | tf_op jit(solution)/shard_map/ppermute | solution.py:23
  113.3 8.3 %collective-permute-start.7 = (bf16[9,1,2048]{2,0,1:T(8,128)(2,1)S(1)}, bf16[9,1,2048]{2,0,1:T(8,128)(2,1)S(1)}, u32[]{:S(2)}, u32[]{:S(2)}) collective-permute-start(bf16[9,1,2048]{2,0,1:T(8,128)(2,1)S(1)} %reshape.124), channel_id=1, source_target_pairs={{0,1},{1,2},{2,3},{4,5},{5,6},{6,7},{8,9},{9,10},{10,11},{12,13},{... | collective-permute-start | bytes 110600 | tf_op jit(solution)/shard_map/ppermute | solution.py:29
  123.7 16.9 %copy-start.20 = (bf16[3,3,3,256,64]{3,4,2,1,0:T(8,128)(2,1)S(1)}, bf16[3,3,3,256,64]{3,4,2,1,0:T(8,128)(2,1)}, u32[]{:S(2)}) copy-start(bf16[3,3,3,256,64]{3,4,2,1,0:T(8,128)(2,1)} %param.15) | copy-start | bytes 2654212
  132.4 7.8 %collective-permute-start.8 = (bf16[1,16,8,256]{3,2,1,0:T(8,128)(2,1)S(1)}, bf16[1,16,8,256]{3,2,1,0:T(8,128)(2,1)S(1)}, u32[]{:S(2)}, u32[]{:S(2)}) collective-permute-start(bf16[1,16,8,256]{3,2,1,0:T(8,128)(2,1)S(1)} %get-tuple-element.15), channel_id=1, source_target_pairs={{0,4},{4,8},{8,12},{12,16},{16,20},{20,24},{24,28},{28,32},{32,36}... | collective-permute-start | bytes 196616 | tf_op jit(solution)/shard_map/ppermute | solution.py:13
  132.5 7.8 %collective-permute-start.9 = (bf16[1,16,8,256]{3,2,1,0:T(8,128)(2,1)S(1)}, bf16[1,16,8,256]{3,2,1,0:T(8,128)(2,1)S(1)}, u32[]{:S(2)}, u32[]{:S(2)}) collective-permute-start(bf16[1,16,8,256]{3,2,1,0:T(8,128)(2,1)S(1)} %get-tuple-element.16), channel_id=1, source_target_pairs={{4,0},{8,4},{12,8},{16,12},{20,16},{24,20},{28,24},{32,28},{36,32}... | collective-permute-start | bytes 196616 | tf_op jit(solution)/shard_map/ppermute | solution.py:16
  (16 other events, 19.8 us)
where the time goes:
time: 149 us; the launch traced here: 148 us
  matrix products  66.3 us (44%)
  starting transfers between devices  28.9 us (19%)
  waiting for transfers between devices  19 us (13%)
  local copies, waits for them, and re-layouts  17.9 us (12%)
  blocking collectives  8.48 us (6%)
  other arithmetic  6.54 us (4%)
    dot_general x36, matrix products, pair_conv(): jnp.einsum('pqhc,cd->pqhd', portion, weights[spatial, offset], preferred_...  48.3 us
    ppermute x2, waiting for transfers between devices, passed_along(): lax.ppermute(x, axis, [(i, (i + by) % devices) for i in range(devices)])  13.1 us
    ppermute x2, starting transfers between devices, passed_along_2(): return lax.ppermute(x, axis, pairs)  11.7 us
    ppermute x3, starting transfers between devices, padded_2(): lax.ppermute(lax.slice_in_dim(block, 0, width, axis=dim), axis, backward)  10.3 us
    unnamed x67, local copies, waits for them, and re-layouts  10.1 us
    all_gather x1, blocking collectives, per_device(): whole_slab = lax.all_gather(quartered_features, 'blk', axis=1, tiled=True)  8.48 us
    dot_general x18, matrix products, reduce_grid(): jnp.einsum('pqhc,cd->pqhd', current_part, current_weight[along, across],...  8.37 us
    ppermute x3, starting transfers between devices, padded_2(): lax.ppermute(lax.slice_in_dim(block, block.shape[dim] - width, None, axis...  6.69 us
  transfers between devices with their start and end apart: 10, of which 6 were waited for; matrix products, arithmetic and copies ran while one was open for 7% of the time, Pallas kernels for 0%

commit v1 on v0

v1 whole, which is shorter than its diff:
```python
import jax
import jax.numpy as jnp
from jax import lax
from jax.experimental import pallas as pl
from jax.experimental.pallas import tpu as pltpu
from jax.sharding import PartitionSpec as P

BF = jnp.bfloat16
F32 = jnp.float32
EDGE = 5
VMEM = pl.BlockSpec(memory_space=pltpu.VMEM)


def leaky_relu(values):
    return jnp.maximum(values, 0.01 * values)


def beside(tiles):
    gap = jnp.zeros(tiles.shape[:-2] + (1, tiles.shape[-1]), tiles.dtype)
    after = jnp.concatenate([tiles[..., 1:, :], gap], axis=-2)
    before = jnp.concatenate([gap, tiles[..., :-1, :]], axis=-2)
    lane = lax.broadcasted_iota(jnp.int32, tiles.shape, tiles.ndim - 1)
    return jnp.where(lane < 64, after, before)


def put(ref, index, tiles):
    ref[index + (slice(None), slice(0, 128))] = tiles
    ref[index + (slice(None), slice(128, 256))] = beside(tiles)


def flat(tiles):
    return tiles.reshape(-1, tiles.shape[-1])


def pair_dot(source, weights, slots):
    total = None
    for slot in range(4):
        term = jnp.dot(flat(source(slot)), weights[slot], preferred_element_type=F32)
        total = term if total is None else total + term
    return leaky_relu(total)


def tiles_kernel(x_ref, tiles_ref, sector_ref, band_ref, corner_ref):
    for a in range(x_ref.shape[0]):
        tiles = x_ref[a].reshape(x_ref.shape[1], 16, 128)
        tiles_ref[a] = tiles
        band_ref[a] = tiles[:EDGE]
        if a < EDGE:
            sector_ref[a] = tiles
            corner_ref[a] = tiles[:EDGE]


def weights_kernel(*refs):
    convs, first_ref, coarse_ref = refs[:4], refs[4], refs[5]
    conv_outs, first_out, coarse_out, spread_out = refs[6:10], refs[10], refs[11], refs[12]
    zero = jnp.zeros((64, 64), BF)
    heights = (0, 1, 2, -1)
    for ref, out in zip(convs, conv_outs):
        for slot in range(4):
            for block, height in enumerate(heights):
                for side in range(2):
                    tap = slot - side
                    parts = []
                    for own in range(2):
                        k = height - own + 1
                        inside = 0 <= tap <= 2 and 0 <= k <= 2
                        parts.append(ref[tap, k] if inside else zero)
                    out[slot, 64 * block : 64 * block + 64, 128 * side : 128 * side + 128] = (
                        jnp.concatenate(parts, axis=1)
                    )
    for i in range(3):
        for j in range(3):
            first_out[i, j, 0:64] = first_ref[i, j, 1]
            first_out[i, j, 64:128] = first_ref[i, j, 2]
            first_out[i, j, 128:192] = jnp.zeros((64, 128), BF)
            first_out[i, j, 192:256] = first_ref[i, j, 0]
    band = lax.axis_index("blk")
    row = lax.broadcasted_iota(jnp.int32, (256, 64), 0)
    col = lax.broadcasted_iota(jnp.int32, (256, 64), 1)
    own = jnp.where(row == col + 64 * band, 1.0, 0.0).astype(BF)
    none = jnp.zeros((256, 64), BF)
    for i in range(3):
        for k in range(3):
            last = own if i == 1 and k == 1 else none
            cols = [coarse_ref[i, 0, k], coarse_ref[i, 1, k], coarse_ref[i, 2, k], last]
            coarse_out[i, k] = jnp.concatenate(cols, axis=1)
    row = lax.broadcasted_iota(jnp.int32, (64, 512), 0)
    col = lax.broadcasted_iota(jnp.int32, (64, 512), 1)
    for h in range(8):
        spread_out[h] = jnp.where(col == row * 8 + h, 1.0, 0.0).astype(BF)


def down_kernel(
    tiles_ref, sector_ref, band_ref, corner_ref,
    wp_ref, wp2_ref, wq_ref, wq2_ref, w1_ref, w2_ref,
    y_ref, xx, pp, qq, ff, part, gg,
):
    own = tiles_ref.shape[0]
    blank = jnp.zeros((1, 16, 256), BF)
    for a in range(22):
        xx[a, 0:1] = blank
    xx[0] = jnp.zeros((22, 16, 256), BF)
    for a in range(own):
        put(xx, (a + 1, slice(1, own + 1)), tiles_ref[a])
        put(xx, (a + 1, slice(own + 1, own + 1 + EDGE)), band_ref[a])
    for a in range(EDGE):
        put(xx, (own + a + 1, slice(1, own + 1)), sector_ref[a])
        put(xx, (own + a + 1, slice(own + 1, own + 1 + EDGE)), corner_ref[a])
    for a in range(20):
        pp[a, 0:1] = blank
    for pair in range(10):
        total = pair_dot(lambda s: xx[2 * pair + s, 1:22], wp_ref, 4)
        for side in range(2):
            tiles = total[:, 128 * side : 128 * side + 128].astype(BF).reshape(21, 16, 128)
            put(pp, (2 * pair + side, slice(1, 22)), tiles)
    qq[0] = jnp.zeros((20, 16, 256), BF)
    for pair in range(10):
        total = pair_dot(lambda s: xx[1:22, 2 * pair + s], wq_ref, 4)
        for side in range(2):
            tiles = total[:, 128 * side : 128 * side + 128].astype(BF).reshape(21, 16, 128)
            put(qq, (slice(1, 22), 2 * pair + side), tiles)
    for pair in range(10):
        total = pair_dot(lambda s: pp[0:20, 2 * pair + s], wp2_ref, 4)
        for side in range(2):
            part[:, 2 * pair + side] = total[:, 128 * side : 128 * side + 128].reshape(20, 16, 128)
    for a in range(20):
        ff[a, 0:1] = blank
    for pair in range(10):
        total = pair_dot(lambda s: qq[2 * pair + s], wq2_ref, 4)
        for side in range(2):
            a = 2 * pair + side
            tiles = total[:, 128 * side : 128 * side + 128].reshape(20, 16, 128)
            put(ff, (a, slice(1, 21)), (part[a] + tiles).astype(BF))
    for a in range(9):
        gg[a, 0:1] = jnp.zeros((1, 16, 128), F32)
    for a in range(9):
        total = None
        for i in range(3):
            for j in range(3):
                rows = jnp.stack([ff[2 * a + 1 + i, j + 2 * r] for r in range(10)])
                term = jnp.dot(flat(rows), w1_ref[i, j], preferred_element_type=F32)
                total = term if total is None else total + term
        total = leaky_relu(total).astype(BF).astype(F32)
        gg[a, 1:11] = total.reshape(10, 16, 128)
    gap = jnp.zeros((1, 128), F32)
    cells = {}
    for a in range(9):
        for r in range(11):
            even = gg[a, r, pl.ds(0, 8, stride=2), :]
            odd = gg[a, r, pl.ds(1, 8, stride=2), :]
            under = jnp.concatenate([gap, odd[:-1]], axis=0)
            cells[a, r] = jnp.concatenate([even, odd, under], axis=1)
    total = None
    for i in range(3):
        for j in range(3):
            rows = jnp.concatenate([cells[2 * a + i, 2 * r + j] for a in range(4) for r in range(5)], axis=0).astype(BF)
            term = jnp.dot(rows[:, 0:256], w2_ref[i, j, 1:3].reshape(256, 256), preferred_element_type=F32)
            term = term + jnp.dot(rows[:, 256:384], w2_ref[i, j, 0], preferred_element_type=F32)
            total = term if total is None else total + term
    y_ref[...] = leaky_relu(total).astype(BF)


def coarse_kernel_body(own_ref, near_ref, far_ref, wc_ref, spread_ref, out_ref, slab, moved):
    band = lax.axis_index("blk")
    for place, ref, index in ((0, own_ref, None), (1, near_ref, None), (2, far_ref, 0), (3, far_ref, 1)):
        other = jnp.bitwise_xor(band, place)
        block = (ref[...] if index is None else ref[index]).astype(F32).reshape(6, 5, 8, 256)
        slab[:, pl.ds(4 * other + 1, 4)] = block[:, 1:5]

        @pl.when(other == 0)
        def _():
            slab[:, 0:1] = block[:, 0:1]

    for a in range(4):
        rows = [slab[a + i, 0:16].astype(BF).reshape(128, 256) for i in range(3)]
        tall = None
        for k in range(3):
            total = None
            for i in range(3):
                term = jnp.dot(rows[i], wc_ref[i, k], preferred_element_type=F32)
                total = term if total is None else total + term
            total = total.reshape(16, 8, 256)
            gap = jnp.zeros((16, 1, 256), F32)
            if k == 0:
                total = jnp.concatenate([gap, total[:, :-1]], axis=1)
            elif k == 2:
                total = jnp.concatenate([total[:, 1:], gap], axis=1)
            else:
                kept = total[:, :, 192:256]
            tall = total if tall is None else tall + total
        gap = jnp.zeros((1, 8, 64), F32)
        total = (
            jnp.concatenate([gap, tall[:-1, :, 0:64]], axis=0)
            + tall[:, :, 64:128]
            + jnp.concatenate([tall[1:, :, 128:192], gap], axis=0)
        )
        moved[128 * a : 128 * a + 128, 0:64] = (kept + leaky_relu(total)).reshape(128, 64)
    total = None
    for h in range(8):
        rows = moved[pl.ds(h, 64, stride=8), :].astype(BF)
        term = jnp.dot(rows[:, 0:64], spread_ref[h], preferred_element_type=F32)
        total = term if total is None else total + term
    out_ref[...] = total.astype(BF).reshape(4, 16, 512)


def moved_by(x, sectors, band_of):
    count, bands = lax.axis_size("sector"), lax.axis_size("blk")
    pairs = []
    for s in range(count):
        for b in range(bands):
            if 0 <= band_of(b) < bands:
                pairs.append((s * bands + b, (s + sectors) % count * bands + band_of(b)))
    return lax.ppermute(x, ("sector", "blk"), pairs)


def shaped(*dims, dtype=BF):
    return jax.ShapeDtypeStruct(dims, dtype)


def run(kernel, outs, scratch, flops, name, *args):
    return pl.pallas_call(
        kernel,
        out_shape=outs,
        in_specs=[VMEM] * len(args),
        out_specs=jax.tree.map(lambda _: VMEM, outs),
        scratch_shapes=scratch,
        compiler_params=pltpu.CompilerParams(vmem_limit_bytes=40 << 20),
        cost_estimate=pl.CostEstimate(flops=flops, bytes_accessed=1 << 20, transcendentals=0),
        name=name,
    )(*args)


def per_device(features, residual_first, residual_second, shortcut_first, shortcut_second,
               first_reduce_weight, second_reduce_weight, coarse_kernel):
    tiles, sector_edge, band_edge, corner = run(
        tiles_kernel,
        (shaped(16, 16, 16, 128), shaped(EDGE, 16, 16, 128), shaped(16, EDGE, 16, 128), shaped(EDGE, EDGE, 16, 128)),
        (), 1 << 30, "tiles", features,
    )
    sector_edge = moved_by(sector_edge, -1, lambda b: b)
    band_edge = moved_by(band_edge, 0, lambda b: b - 1)
    corner = moved_by(corner, -1, lambda b: b - 1)
    *convs, w1, wc, spread = run(
        weights_kernel,
        (shaped(4, 256, 256),) * 4 + (shaped(3, 3, 256, 128), shaped(3, 3, 256, 256), shaped(8, 64, 512)),
        (), 1 << 30, "weights",
        residual_first, residual_second, shortcut_first, shortcut_second, first_reduce_weight, coarse_kernel,
    )
    y = run(
        down_kernel,
        shaped(160, 256),
        (
            pltpu.VMEM((22, 22, 16, 256), BF),
            pltpu.VMEM((20, 22, 16, 256), BF),
            pltpu.VMEM((22, 20, 16, 256), BF),
            pltpu.VMEM((20, 21, 16, 256), BF),
            pltpu.VMEM((20, 20, 16, 128), F32),
            pltpu.VMEM((9, 11, 16, 128), F32),
        ),
        10 << 30, "down", tiles, sector_edge, band_edge, corner, *convs, w1, second_reduce_weight,
    )
    y = jnp.concatenate([moved_by(y[80:160], 1, lambda b: b), y], axis=0)
    far = moved_by(y, 0, lambda b: b ^ 2)
    both = jnp.stack([y, far])
    other = moved_by(both, 0, lambda b: b ^ 1)
    return run(
        coarse_kernel_body,
        shaped(4, 16, 512),
        (pltpu.VMEM((6, 18, 8, 256), F32), pltpu.VMEM((512, 128), F32)),
        2 << 30, "coarse", y, other[0], jnp.stack([far, other[1]]), wc, spread,
    )


def solution(mesh):
    in_specs = (P("sector", "blk", None),) + (P(),) * 6 + (P(None, None, None, None, "blk"),)
    return jax.shard_map(
        per_device, mesh=mesh, in_specs=in_specs, out_specs=P("sector", None, "blk"), check_vma=False
    )
```

time: 149 us -> 52.9 us (0.36)
  matrix products: 66.3 us -> 0 us
  Pallas kernels: 0 us -> 14.7 us
  starting transfers between devices: 28.9 us -> 16.2 us
  local copies, waits for them, and re-layouts: 17.9 us -> 7.76 us
  blocking collectives: 8.48 us -> 0 us
  other arithmetic: 6.54 us -> 0.07 us
  waiting for transfers between devices: 19 us -> 13.7 us
    dot_general x99 -> x0, matrix products: 66.3 us -> none  [the longest x36 48.3 us: pair_conv(): jnp.einsum('pqhc,cd->pqhd', portion, weights[spatial, offset], preferred_...]
    pallas_call x0 -> x4, Pallas kernels: none -> 14.7 us  [run(): pl.pallas_call(kernel, out_shape=outs, in_specs=[VMEM] * len(args), out_s...]
    ppermute x10 -> x6, starting transfers between devices: 28.9 us -> 16.2 us  [moved_by(): return lax.ppermute(x, ('sector', 'blk'), pairs)]
    all_gather x1 -> x0, blocking collectives: 8.48 us -> none  [per_device(): whole_slab = lax.all_gather(quartered_features, 'blk', axis=1, tiled=True)]
    concatenate x10 -> x0, other arithmetic: 5.35 us -> none  [the longest x4 2.96 us: pair_weights(): per_offset.append(jnp.concatenate(row_blocks, axis=1))]
    ppermute x10 -> x6, waiting for transfers between devices: 19 us -> 13.7 us  [moved_by(): return lax.ppermute(x, ('sector', 'blk'), pairs)]
    concatenate x3 -> x0, local copies, waits for them, and re-layouts: 2.66 us -> none  [the longest x2 2.64 us: padded_2(): block = jnp.concatenate([low, block, high], axis=dim)]
    unnamed x67 -> x19, local copies, waits for them, and re-layouts: 10.1 us -> 7.74 us
  transfers between devices with their start and end apart: 10 -> 6, of which waited for: 6 -> 4; matrix products, arithmetic and copies ran while one was open for 7% -> 4% of each run, Pallas kernels for 0% -> 1%
where the time goes in v1:
time: 52.9 us; the launch traced here: 52.6 us
  starting transfers between devices  16.2 us (31%)
  Pallas kernels  14.7 us (28%)
  waiting for transfers between devices  13.7 us (26%)
  local copies, waits for them, and re-layouts  7.76 us (15%)
    ppermute x6, starting transfers between devices, moved_by(): return lax.ppermute(x, ('sector', 'blk'), pairs)  16.2 us
    pallas_call x4, Pallas kernels, run(): pl.pallas_call(kernel, out_shape=outs, in_specs=[VMEM] * len(args), out_s...  14.7 us
    ppermute x6, waiting for transfers between devices, moved_by(): return lax.ppermute(x, ('sector', 'blk'), pairs)  13.7 us
    unnamed x19, local copies, waits for them, and re-layouts  7.74 us
  transfers between devices with their start and end apart: 6, of which 4 were waited for; matrix products, arithmetic and copies ran while one was open for 4% of the time, Pallas kernels for 1%

profile of v1, /device:TPU:1, one launch (start us, length us, event | category | flops | bytes accessed | tf_op | source)
XLA Modules:
  0.0 52.6 jit_solution(9425572812286625881)
XLA Ops:
  0.0 1.2 %copy-done.1 = bf16[16,16,2048]{2,1,0:T(8,128)(2,1)S(1)} copy-done((bf16[16,16,2048]{2,1,0:T(8,128)(2,1)S(1)}, bf16[16,16,2048]{2,1,0:T(8,128)(2,1)}, u32[]{:S(2)}) %copy-start.1) | copy-done | bytes 1048600
  1.2 0.7 %tiles.1 = (bf16[16,16,16,128]{3,2,1,0:T(8,128)(2,1)S(1)}, bf16[5,16,16,128]{3,2,1,0:T(8,128)(2,1)S(1)}, bf16[16,5,16,128]{3,2,1,0:T(8,128)(2,1)S(1)}, bf16[5,5,16,128]{3,2,1,0:T(8,128)(2,1)}) custom-call(bf16[16,16,2048]{2,1,0:T(8,128)(2,1)S(1)} %copy-done.1), custom_call_target="tpu_custom_call" | custom-call | flops 1073741824 | bytes 1048576 | tf_op jit(solution)/shard_map/tiles/pallas_call | solution.py:221
  2.0 1.0 %copy-done.7 = bf16[16,16,16,128]{3,2,1,0:T(8,128)(2,1)} copy-done((bf16[16,16,16,128]{3,2,1,0:T(8,128)(2,1)}, bf16[16,16,16,128]{3,2,1,0:T(8,128)(2,1)S(1)}, u32[]{:S(2)}) %copy-start.7) | copy-done | bytes 1048600
  2.9 7.1 %collective-permute-start = (bf16[5,16,16,128]{3,2,1,0:T(8,128)(2,1)S(1)}, bf16[5,16,16,128]{3,2,1,0:T(8,128)(2,1)S(1)}, u32[]{:S(2)}, u32[]{:S(2)}) collective-permute-start(bf16[5,16,16,128]{3,2,1,0:T(8,128)(2,1)S(1)} %get-tuple-element.17), channel_id=1, source_target_pairs={{0,124},{1,125},{2,126},{3,127},{4,0},{5,1},{6,2},{7,3},{8,4},{9,5... | collective-permute-start | bytes 983048 | tf_op jit(solution)/shard_map/ppermute | solution.py:213
  10.1 2.9 %collective-permute-start.1 = (bf16[16,5,16,128]{3,2,1,0:T(8,128)(2,1)S(1)}, bf16[16,5,16,128]{3,2,1,0:T(8,128)(2,1)S(1)}, u32[]{:S(2)}, u32[]{:S(2)}) collective-permute-start(bf16[16,5,16,128]{3,2,1,0:T(8,128)(2,1)S(1)} %get-tuple-element.18), channel_id=1, source_target_pairs={{1,0},{2,1},{3,2},{5,4},{6,5},{7,6},{9,8},{10,9},{11,10},{13,12},{... | collective-permute-start | bytes 983048 | tf_op jit(solution)/shard_map/ppermute | solution.py:213
  12.9 1.9 %collective-permute-start.2 = (bf16[5,5,16,128]{3,2,1,0:T(8,128)(2,1)}, bf16[5,5,16,128]{3,2,1,0:T(8,128)(2,1)}, u32[]{:S(2)}, u32[]{:S(2)}) collective-permute-start(bf16[5,5,16,128]{3,2,1,0:T(8,128)(2,1)} %get-tuple-element.19), channel_id=1, source_target_pairs={{1,124},{2,125},{3,126},{5,0},{6,1},{7,2},{9,4},{10,5},{11,6},{13,... | collective-permute-start | bytes 307208 | tf_op jit(solution)/shard_map/ppermute | solution.py:213
  14.8 1.9 %copy.9.refs_5_ = bf16[3,3,3,256,64]{4,3,2,1,0:T(8,128)(2,1)S(1)} copy(bf16[3,3,3,256,64]{3,4,2,1,0:T(8,128)(2,1)} %param.15) | data formatting | bytes 1769472 | tf_op args[7]
  16.8 0.0 copy-start.3
  16.8 0.9 %copy-done.3 = bf16[3,3,64,64]{3,2,1,0:T(8,128)(2,1)S(1)} copy-done((bf16[3,3,64,64]{3,2,1,0:T(8,128)(2,1)S(1)}, bf16[3,3,64,64]{3,2,1,0:T(8,128)(2,1)}, u32[]{:S(2)}) %copy-start.3) | copy-done | bytes 73752
  17.7 0.9 %copy-done.4 = bf16[3,3,64,64]{3,2,1,0:T(8,128)(2,1)S(1)} copy-done((bf16[3,3,64,64]{3,2,1,0:T(8,128)(2,1)S(1)}, bf16[3,3,64,64]{3,2,1,0:T(8,128)(2,1)}, u32[]{:S(2)}) %copy-start.4) | copy-done | bytes 73752
  18.6 0.9 %copy-done.5 = bf16[3,3,64,64]{3,2,1,0:T(8,128)(2,1)S(1)} copy-done((bf16[3,3,64,64]{3,2,1,0:T(8,128)(2,1)S(1)}, bf16[3,3,64,64]{3,2,1,0:T(8,128)(2,1)}, u32[]{:S(2)}) %copy-start.5) | copy-done | bytes 73752
  19.5 0.9 %copy-done.6 = bf16[3,3,64,64]{3,2,1,0:T(8,128)(2,1)S(1)} copy-done((bf16[3,3,64,64]{3,2,1,0:T(8,128)(2,1)S(1)}, bf16[3,3,64,64]{3,2,1,0:T(8,128)(2,1)}, u32[]{:S(2)}) %copy-start.6) | copy-done | bytes 73752
  20.4 0.7 %weights.1 = (bf16[4,256,256]{2,1,0:T(8,128)(2,1)S(1)}, bf16[4,256,256]{2,1,0:T(8,128)(2,1)S(1)}, bf16[4,256,256]{2,1,0:T(8,128)(2,1)S(1)}, bf16[4,256,256]{2,1,...) custom-call(bf16[3,3,64,64]{3,2,1,0:T(8,128)(2,1)S(1)} %copy-done.3,, ...), custom_call_target="tpu_custom_call" | custom-call | flops 1073741824 | bytes 1048576 | tf_op jit(solution)/shard_map/weights/pallas_call | solution.py:221
  21.1 2.2 %collective-permute-done.2.corner_ref = bf16[5,5,16,128]{3,2,1,0:T(8,128)(2,1)} collective-permute-done((bf16[5,5,16,128]{3,2,1,0:T(8,128)(2,1)}, bf16[5,5,16,128]{3,2,1,0:T(8,128)(2,1)}, u32[]{:S(2)}, u32[]{:S(2)}) %collective-permute-start.2) | collective-permute-done | bytes 102432 | tf_op jit(solution)/shard_map/ppermute | solution.py:213
  23.4 0.0 collective-permute-done.sector_ref
  23.4 0.0 collective-permute-done.1.band_ref
  23.4 11.3 %down.1 = bf16[160,256]{1,0:T(8,128)(2,1)S(1)} custom-call(bf16[16,16,16,128]{3,2,1,0:T(8,128)(2,1)S(1)} %copy-done.8, bf16[5,16,16,128]{3,2,1,0:T(8,128)(2,1)S(1)} %collective-permute-done.sector_ref, bf16[16,5,16,128]{3,2,1,0:T(8,128)(2,1)S(1)} %collective-permute-done.1.band_ref, bf16[5,5,16,128]{3,2,1,0:T(8,128)(2,1)} %collective-permute-done.2.corner_ref, ...), custom_call_target="tpu_custom_call" | custom-call | flops 10737418240 | bytes 1048576 | tf_op jit(solution)/shard_map/down/pallas_call | solution.py:221
  34.7 0.1 collective-permute-start.3
  34.8 7.1 %collective-permute-done.3 = bf16[80,256]{1,0:T(8,128)(2,1)S(1)} collective-permute-done((bf16[80,256]{1,0:T(8,128)(2,1)S(1)}, bf16[80,256]{1,0:T(8,128)(2,1)S(1)}, u32[]{:S(2)}, u32[]{:S(2)}) %collective-permute-start.3) | collective-permute-done | bytes 40992 | tf_op jit(solution)/shard_map/ppermute | solution.py:213
  41.9 3.2 %collective-permute-start.4 = (bf16[240,256]{1,0:T(8,128)(2,1)S(1)}, bf16[240,256]{1,0:T(8,128)(2,1)S(1)}, u32[]{:S(2)}, u32[]{:S(2)}) collective-permute-start(bf16[240,256]{1,0:T(8,128)(2,1)S(1)} %get-tuple-element.30.own_ref), channel_id=1, source_target_pairs={{0,2},{1,3},{2,0},{3,1},{4,6},{5,7},{6,4},{7,5},{8,10},{9,11},{10,... | collective-permute-start | bytes 368648 | tf_op jit(solution)/shard_map/ppermute | solution.py:213
  45.1 3.3 %collective-permute-done.4 = bf16[240,256]{1,0:T(8,128)(2,1)S(1)} collective-permute-done((bf16[240,256]{1,0:T(8,128)(2,1)S(1)}, bf16[240,256]{1,0:T(8,128)(2,1)S(1)}, u32[]{:S(2)}, u32[]{:S(2)}) %collective-permute-start.4) | collective-permute-done | bytes 122912 | tf_op jit(solution)/shard_map/ppermute | solution.py:213
  48.3 1.1 %collective-permute-start.5 = (bf16[2,240,256]{2,1,0:T(8,128)(2,1)S(1)}, bf16[2,240,256]{2,1,0:T(8,128)(2,1)S(1)}, u32[]{:S(2)}, u32[]{:S(2)}) collective-permute-start(bf16[2,240,256]{2,1,0:T(8,128)(2,1)S(1)} %pad_maximum_fusion), channel_id=1, source_target_pairs={{0,1},{1,0},{2,3},{3,2},{4,5},{5,4},{6,7},{7,6},{8,9},{9,8},{10,11... | collective-permute-start | bytes 737288 | tf_op jit(solution)/shard_map/ppermute | solution.py:213
  49.4 1.1 %collective-permute-done.5 = bf16[2,240,256]{2,1,0:T(8,128)(2,1)S(1)} collective-permute-done((bf16[2,240,256]{2,1,0:T(8,128)(2,1)S(1)}, bf16[2,240,256]{2,1,0:T(8,128)(2,1)S(1)}, u32[]{:S(2)}, u32[]{:S(2)}) %collective-permute-start.5) | collective-permute-done | bytes 245792 | tf_op jit(solution)/shard_map/ppermute | solution.py:213
  50.6 2.0 %coarse.1 = bf16[4,16,512]{2,1,0:T(8,128)(2,1)} custom-call(bf16[240,256]{1,0:T(8,128)(2,1)S(1)} %get-tuple-element.30.own_ref, bf16[240,256]{1,0:T(8,128)(2,1)S(1)} %get-tuple-element.28.near_ref, bf16[2,240,256]{2,1,0:T(8,128)(2,1)S(1)} %pad_maximum_fusion.1.far_ref, bf16[3,3,256,256]{3,2,1,0:T(8,128)(2,1)S(1)} %get-tuple-element.25.wc_ref, ...), custom_call_target="tpu_custom_call" | custom-call | flops 2147483648 | bytes 1048576 | tf_op jit(solution)/shard_map/coarse/pallas_call | solution.py:221
  (16 shorter events, 0.1 us)
Async XLA Ops:
  0.0 1.2 %copy-start.1 = (bf16[16,16,2048]{2,1,0:T(8,128)(2,1)S(1)}, bf16[16,16,2048]{2,1,0:T(8,128)(2,1)}, u32[]{:S(2)}) copy-start(bf16[16,16,2048]{2,1,0:T(8,128)(2,1)} %x_ref.1) | copy-start | bytes 3145732
  2.0 1.0 %copy-start.7 = (bf16[16,16,16,128]{3,2,1,0:T(8,128)(2,1)}, bf16[16,16,16,128]{3,2,1,0:T(8,128)(2,1)S(1)}, u32[]{:S(2)}) copy-start(bf16[16,16,16,128]{3,2,1,0:T(8,128)(2,1)S(1)} %get-tuple-element.16.tiles_ref) | copy-start | bytes 3145732
  2.9 13.8 %copy-start.2 = (bf16[3,3,3,64,128]{4,3,2,1,0:T(8,128)(2,1)S(1)}, bf16[3,3,3,64,128]{4,3,2,1,0:T(8,128)(2,1)}, u32[]{:S(2)}) copy-start(bf16[3,3,3,64,128]{4,3,2,1,0:T(8,128)(2,1)} %refs_4_.1) | copy-start | bytes 1327108
  2.9 20.5 %collective-permute-start = (bf16[5,16,16,128]{3,2,1,0:T(8,128)(2,1)S(1)}, bf16[5,16,16,128]{3,2,1,0:T(8,128)(2,1)S(1)}, u32[]{:S(2)}, u32[]{:S(2)}) collective-permute-start(bf16[5,16,16,128]{3,2,1,0:T(8,128)(2,1)S(1)} %get-tuple-element.17), channel_id=1, source_target_pairs={{0,124},{1,125},{2,126},{3,127},{4,0},{5,1},{6,2},{7,3},{8,4},{9,5... | collective-permute-start | bytes 983048 | tf_op jit(solution)/shard_map/ppermute | solution.py:213
  10.1 13.3 %collective-permute-start.1 = (bf16[16,5,16,128]{3,2,1,0:T(8,128)(2,1)S(1)}, bf16[16,5,16,128]{3,2,1,0:T(8,128)(2,1)S(1)}, u32[]{:S(2)}, u32[]{:S(2)}) collective-permute-start(bf16[16,5,16,128]{3,2,1,0:T(8,128)(2,1)S(1)} %get-tuple-element.18), channel_id=1, source_target_pairs={{1,0},{2,1},{3,2},{5,4},{6,5},{7,6},{9,8},{10,9},{11,10},{13,12},{... | collective-permute-start | bytes 983048 | tf_op jit(solution)/shard_map/ppermute | solution.py:213
  12.9 10.5 %collective-permute-start.2 = (bf16[5,5,16,128]{3,2,1,0:T(8,128)(2,1)}, bf16[5,5,16,128]{3,2,1,0:T(8,128)(2,1)}, u32[]{:S(2)}, u32[]{:S(2)}) collective-permute-start(bf16[5,5,16,128]{3,2,1,0:T(8,128)(2,1)} %get-tuple-element.19), channel_id=1, source_target_pairs={{1,124},{2,125},{3,126},{5,0},{6,1},{7,2},{9,4},{10,5},{11,6},{13,... | collective-permute-start | bytes 307208 | tf_op jit(solution)/shard_map/ppermute | solution.py:213
  16.8 0.9 %copy-start.3 = (bf16[3,3,64,64]{3,2,1,0:T(8,128)(2,1)S(1)}, bf16[3,3,64,64]{3,2,1,0:T(8,128)(2,1)}, u32[]{:S(2)}) copy-start(bf16[3,3,64,64]{3,2,1,0:T(8,128)(2,1)} %refs_0_.1) | copy-start | bytes 221188
  17.7 0.9 %copy-start.4 = (bf16[3,3,64,64]{3,2,1,0:T(8,128)(2,1)S(1)}, bf16[3,3,64,64]{3,2,1,0:T(8,128)(2,1)}, u32[]{:S(2)}) copy-start(bf16[3,3,64,64]{3,2,1,0:T(8,128)(2,1)} %refs_1_.1) | copy-start | bytes 221188
  18.6 0.9 %copy-start.5 = (bf16[3,3,64,64]{3,2,1,0:T(8,128)(2,1)S(1)}, bf16[3,3,64,64]{3,2,1,0:T(8,128)(2,1)}, u32[]{:S(2)}) copy-start(bf16[3,3,64,64]{3,2,1,0:T(8,128)(2,1)} %refs_2_.1) | copy-start | bytes 221188
  19.5 0.9 %copy-start.6 = (bf16[3,3,64,64]{3,2,1,0:T(8,128)(2,1)S(1)}, bf16[3,3,64,64]{3,2,1,0:T(8,128)(2,1)}, u32[]{:S(2)}) copy-start(bf16[3,3,64,64]{3,2,1,0:T(8,128)(2,1)} %refs_3_.1) | copy-start | bytes 221188
  20.4 3.0 %copy-start = (bf16[3,3,3,128,256]{4,3,2,1,0:T(8,128)(2,1)S(1)}, bf16[3,3,3,128,256]{4,3,2,1,0:T(8,128)(2,1)}, u32[]{:S(2)}) copy-start(bf16[3,3,3,128,256]{4,3,2,1,0:T(8,128)(2,1)} %w2_ref.1) | copy-start | bytes 5308420
  20.4 3.0 %copy-start.8 = (bf16[16,16,16,128]{3,2,1,0:T(8,128)(2,1)S(1)}, bf16[16,16,16,128]{3,2,1,0:T(8,128)(2,1)}, u32[]{:S(2)}) copy-start(bf16[16,16,16,128]{3,2,1,0:T(8,128)(2,1)} %copy-done.7) | copy-start | bytes 3145732
  34.7 7.1 %collective-permute-start.3 = (bf16[80,256]{1,0:T(8,128)(2,1)S(1)}, bf16[80,256]{1,0:T(8,128)(2,1)S(1)}, u32[]{:S(2)}, u32[]{:S(2)}) collective-permute-start(bf16[80,256]{1,0:T(8,128)(2,1)S(1)} %slice.12), channel_id=1, source_target_pairs={{0,4},{1,5},{2,6},{3,7},{4,8},{5,9},{6,10},{7,11},{8,12},{9,13},{1... | collective-permute-start | bytes 122888 | tf_op jit(solution)/shard_map/ppermute | solution.py:213
  41.9 6.4 %collective-permute-start.4 = (bf16[240,256]{1,0:T(8,128)(2,1)S(1)}, bf16[240,256]{1,0:T(8,128)(2,1)S(1)}, u32[]{:S(2)}, u32[]{:S(2)}) collective-permute-start(bf16[240,256]{1,0:T(8,128)(2,1)S(1)} %get-tuple-element.30.own_ref), channel_id=1, source_target_pairs={{0,2},{1,3},{2,0},{3,1},{4,6},{5,7},{6,4},{7,5},{8,10},{9,11},{10,... | collective-permute-start | bytes 368648 | tf_op jit(solution)/shard_map/ppermute | solution.py:213
  48.3 2.2 %collective-permute-start.5 = (bf16[2,240,256]{2,1,0:T(8,128)(2,1)S(1)}, bf16[2,240,256]{2,1,0:T(8,128)(2,1)S(1)}, u32[]{:S(2)}, u32[]{:S(2)}) collective-permute-start(bf16[2,240,256]{2,1,0:T(8,128)(2,1)S(1)} %pad_maximum_fusion), channel_id=1, source_target_pairs={{0,1},{1,0},{2,3},{3,2},{4,5},{5,4},{6,7},{7,6},{8,9},{9,8},{10,11... | collective-permute-start | bytes 737288 | tf_op jit(solution)/shard_map/ppermute | solution.py:213

commit v2 on v1

v2 whole, which is shorter than its diff:
```python
import jax
import jax.numpy as jnp
from jax import lax
from jax.experimental import pallas as pl
from jax.experimental.pallas import tpu as pltpu
from jax.sharding import PartitionSpec as P

BF = jnp.bfloat16
F32 = jnp.float32
EDGE = 5
VMEM = pl.BlockSpec(memory_space=pltpu.VMEM)


def leaky_relu(values):
    return jnp.maximum(values, 0.01 * values)


def beside(tiles):
    gap = jnp.zeros(tiles.shape[:-2] + (1, tiles.shape[-1]), tiles.dtype)
    after = jnp.concatenate([tiles[..., 1:, :], gap], axis=-2)
    before = jnp.concatenate([gap, tiles[..., :-1, :]], axis=-2)
    lane = lax.broadcasted_iota(jnp.int32, tiles.shape, tiles.ndim - 1)
    return jnp.where(lane < 64, after, before)


def under(tiles):
    gap = jnp.zeros(tiles.shape[:-2] + (1, tiles.shape[-1]), tiles.dtype)
    return jnp.concatenate([gap, tiles[..., :-1, :]], axis=-2)


def put(ref, index, tiles, second=beside):
    ref[index + (slice(None), slice(0, 128))] = tiles
    ref[index + (slice(None), slice(128, 256))] = second(tiles)


def flat(tiles):
    return tiles.reshape(-1, tiles.shape[-1])


def spaced(ref, a, rows, a_step, r, cols, r_step):
    lines = []
    for n in range(rows):
        if r_step == 1:
            lines.append(ref[a + a_step * n, r : r + cols])
        else:
            lines.append(jnp.stack([ref[a + a_step * n, r + r_step * m] for m in range(cols)]))
    return jnp.stack(lines)


def pair_dot(source, weights):
    total = None
    for slot in range(4):
        term = jnp.dot(flat(source(slot)), weights[slot], preferred_element_type=F32)
        total = term if total is None else total + term
    return leaky_relu(total)


def along_a(source, weights, a, pairs, r, count):
    total = pair_dot(lambda s: spaced(source, a - 1 + s, pairs, 2, r, count, 1), weights)
    return total.reshape(pairs, count, 16, 256)


def along_r(source, weights, a, count, r, pairs):
    total = pair_dot(lambda s: spaced(source, a, count, 1, r + s, pairs, 2), weights)
    return total.reshape(count, pairs, 16, 256)


def fill_p(xx, pp, weights, a, pairs, r, count):
    total = along_a(xx, weights, a, pairs, r + 1, count).astype(BF)
    for pair in range(pairs):
        for side in range(2):
            put(pp, (a + 2 * pair + side, slice(r + 1, r + 1 + count)), total[pair, :, :, 128 * side : 128 * side + 128])


def fill_q(xx, qq, weights, a, count, r, pairs):
    total = along_r(xx, weights, a, count, r, pairs).astype(BF)
    for pair in range(pairs):
        for side in range(2):
            put(qq, (slice(a, a + count), r + 2 * pair + side), total[:, pair, :, 128 * side : 128 * side + 128])


def fill_f(pp, qq, ff, part, wp, wq, a, a_pairs, r, r_pairs):
    count, span = 2 * a_pairs, 2 * r_pairs
    total = along_r(pp, wp, a, count, r, r_pairs)
    for pair in range(r_pairs):
        for side in range(2):
            part[0:count, 2 * pair + side] = total[:, pair, :, 128 * side : 128 * side + 128]
    total = along_a(qq, wq, a, a_pairs, r, span)
    for pair in range(a_pairs):
        for side in range(2):
            tiles = total[pair, :, :, 128 * side : 128 * side + 128] + part[2 * pair + side, 0:span]
            put(ff, (a + 2 * pair + side, slice(r + 1, r + 1 + span)), tiles.astype(BF), under)


def fill_g(ff, gg, w_oo, w_oe, w_eo, w_ee, a, rows, r, cols):
    def product(first_a, na, first_r, nr, weights):
        tiles = spaced(ff, first_a, na, 2, first_r + 1, nr, 2)
        total = jnp.dot(flat(tiles), weights[...], preferred_element_type=F32)
        return total.reshape(na, nr, 16, -1)

    odd = product(2 * a - 1, rows + 1, 2 * r - 1, cols + 1, w_oo)
    total = odd[:rows, :cols, :, 0:128] + odd[:rows, 1:, :, 128:256]
    total = total + (odd[1:, :cols, :, 256:384] + odd[1:, 1:, :, 384:512])
    mixed = product(2 * a - 1, rows + 1, 2 * r, cols, w_oe)
    total = total + (mixed[:rows, :, :, 0:128] + mixed[1:, :, :, 128:256])
    mixed = product(2 * a, rows, 2 * r - 1, cols + 1, w_eo)
    total = total + (mixed[:, :cols, :, 0:128] + mixed[:, 1:, :, 128:256])
    total = total + product(2 * a, rows, 2 * r, cols, w_ee)
    gg[a - 1 : a - 1 + rows, r + 1 : r + 1 + cols] = leaky_relu(total).astype(BF).astype(F32)


def tiles_kernel(x_hbm, tiles_ref, sector_ref, band_ref, corner_ref, x_ref, sems):
    rows = x_hbm.shape[0]
    copies = []
    for part in range(8):
        at = pl.ds(rows // 8 * part, rows // 8)
        copies.append(pltpu.make_async_copy(x_hbm.at[at], x_ref.at[at], sems.at[part]))
        copies[-1].start()
    for a in range(rows):
        if a % (rows // 8) == 0:
            copies[a // (rows // 8)].wait()
        tiles = x_ref[a].reshape(x_ref.shape[1], 16, 128)
        tiles_ref[a] = tiles
        band_ref[a] = tiles[:EDGE]
        if a < EDGE:
            sector_ref[a] = tiles
            corner_ref[a] = tiles[:EDGE]


def inner_kernel(
    tiles_ref, wp_hbm, wp2_hbm, wq_hbm, wq2_hbm, w1_hbm,
    wp, wp2, wq, wq2, w_oo, w_oe, w_eo, w_ee, xx, pp, qq, ff, gg,
    raw, raw1, part, sems,
):
    copies = [pltpu.make_async_copy(w, raw.at[n], sems.at[n]) for n, w in enumerate((wp_hbm, wq_hbm, wp2_hbm, wq2_hbm))]
    copies.append(pltpu.make_async_copy(w1_hbm, raw1, sems.at[4]))
    for copy in copies:
        copy.start()
    own = tiles_ref.shape[0]
    blank = jnp.zeros((1, 16, 256), BF)
    for a in range(own):
        put(xx, (a, slice(1, own + 1)), tiles_ref[a])
    for a in range(own + EDGE):
        xx[a, 0:1] = blank
        pp[a, 0:1] = blank
        ff[a, 0:1] = blank
    for a in range(9):
        gg[a, 0:1] = jnp.zeros((1, 16, 128), F32)
    xx[own + EDGE] = jnp.zeros(xx.shape[1:], BF)
    qq[own + EDGE] = jnp.zeros(qq.shape[1:], BF)

    zero = jnp.zeros((64, 64), BF)
    for n, out in enumerate((wp, wq, wp2, wq2)):
        copies[n].wait()
        for slot in range(4):
            for block, height in enumerate((0, 1, 2, -1)):
                for side in range(2):
                    tap = slot - side
                    parts = []
                    for upper in range(2):
                        k = height - upper + 1
                        inside = 0 <= tap <= 2 and 0 <= k <= 2
                        parts.append(raw[n, tap, k] if inside else zero)
                    out[slot, 64 * block : 64 * block + 64, 128 * side : 128 * side + 128] = (
                        jnp.concatenate(parts, axis=1)
                    )
    copies[4].wait()
    taps = (
        (w_oo, ((0, 0), (0, 2), (2, 0), (2, 2))), (w_oe, ((0, 1), (2, 1))), (w_eo, ((1, 0), (1, 2))), (w_ee, ((1, 1),)),
    )
    for out, pairs in taps:
        for n, (i, j) in enumerate(pairs):
            at = slice(128 * n, 128 * n + 128)
            out[0:64, at] = raw1[i, j, 1]
            out[64:128, at] = raw1[i, j, 2]
            out[128:192, at] = jnp.zeros((64, 128), BF)
            out[192:256, at] = raw1[i, j, 0]

    fill_p(xx, pp, wp, 1, 7, 0, 16)
    fill_q(xx, qq, wq, 0, 16, 0, 7)
    fill_f(pp, qq, ff, part, wp2, wq2, 1, 7, 0, 7)
    fill_g(ff, gg, w_oo, w_oe, w_eo, w_ee, 1, 6, 0, 7)


def outer_kernel(
    xx_in, pp_in, qq_in, ff_in, gg_in, sector_ref, band_ref, corner_ref,
    wp, wp2, wq, wq2, w_oo, w_oe, w_eo, w_ee, w2_ref,
    y_ref, xx, pp, qq, ff, gg, part, cells,
):
    own = band_ref.shape[0]
    for a in range(own):
        put(xx, (a, slice(own + 1, own + 1 + EDGE)), band_ref[a])
    for a in range(EDGE):
        put(xx, (own + a, slice(1, own + 1)), sector_ref[a])
        put(xx, (own + a, slice(own + 1, own + 1 + EDGE)), corner_ref[a])
    fill_p(xx, pp, wp, 1, 7, 16, 5)
    fill_p(xx, pp, wp, 15, 3, 0, 21)
    fill_q(xx, qq, wq, 0, 16, 14, 3)
    fill_q(xx, qq, wq, 16, 5, 0, 10)
    fill_f(pp, qq, ff, part, wp2, wq2, 1, 7, 14, 3)
    fill_f(pp, qq, ff, part, wp2, wq2, 15, 3, 0, 10)
    fill_g(ff, gg, w_oo, w_oe, w_eo, w_ee, 1, 6, 7, 3)
    fill_g(ff, gg, w_oo, w_oe, w_eo, w_ee, 7, 3, 0, 10)

    even = gg[:, :, pl.ds(0, 8, stride=2), :]
    odd = gg[:, :, pl.ds(1, 8, stride=2), :]
    cells[:, :, :, 0:128] = even
    cells[:, :, :, 128:256] = odd
    cells[:, :, :, 256:384] = under(odd)
    total = None
    for i in range(3):
        for j in range(3):
            rows = flat(spaced(cells, i, 4, 2, j, 5, 2)).astype(BF)
            term = jnp.dot(rows[:, 0:256], w2_ref[i, j, 1:3].reshape(256, 256), preferred_element_type=F32)
            term = term + jnp.dot(rows[:, 256:384], w2_ref[i, j, 0], preferred_element_type=F32)
            total = term if total is None else total + term
    y_ref[...] = leaky_relu(total).astype(BF)


def late_kernel(y_ref, coarse_hbm, coarse_out, spread_out, raw, sem):
    copy = pltpu.make_async_copy(coarse_hbm, raw, sem)
    copy.start()
    row = lax.broadcasted_iota(jnp.int32, (64, 512), 0)
    col = lax.broadcasted_iota(jnp.int32, (64, 512), 1)
    for h in range(8):
        spread_out[h] = jnp.where(col == row * 8 + h, 1.0, 0.0).astype(BF)
    band = lax.axis_index("blk")
    row = lax.broadcasted_iota(jnp.int32, (64, 256), 0)
    col = lax.broadcasted_iota(jnp.int32, (64, 256), 1)
    own = jnp.where(col == row + 64 * band, 1.0, 0.0).astype(BF)
    copy.wait()
    for i in range(3):
        for k in range(3):
            for j in range(3):
                coarse_out[i, k, 64 * j : 64 * j + 64] = raw[i, j, k]
            coarse_out[i, k, 192:256] = own if i == 1 and k == 1 else jnp.zeros((64, 256), BF)


def coarse_kernel_body(
    own_ref, near_ref, halo_ref, far_ref, far_halo_ref, last_ref, wc_ref, spread_ref, out_ref, slab, moved,
):
    band = lax.axis_index("blk")
    blocks = (
        (0, 2, own_ref[...]), (0, 0, halo_ref[...]), (1, 2, near_ref[...]), (1, 0, last_ref[0:80]),
        (2, 2, far_ref[...]), (2, 0, far_halo_ref[...]), (3, 2, last_ref[80:240]), (3, 0, last_ref[240:320]),
    )
    for place, first, block in blocks:
        other = jnp.bitwise_xor(band, place)
        block = block.astype(F32).reshape(-1, 5, 8, 256)
        at = slice(first, first + block.shape[0])
        slab[at, pl.ds(4 * other + 1, 4)] = block[:, 1:5]

        @pl.when(other == 0)
        def _():
            slab[at, 0:1] = block[:, 0:1]

    for a in range(4):
        rows = [slab[a + i, 0:16].astype(BF).reshape(128, 256) for i in range(3)]
        tall = None
        for k in range(3):
            total = None
            for i in range(3):
                term = lax.dot_general(rows[i], wc_ref[i, k], (((1,), (1,)), ((), ())), preferred_element_type=F32)
                total = term if total is None else total + term
            total = total.reshape(16, 8, 256)
            gap = jnp.zeros((16, 1, 256), F32)
            if k == 0:
                total = jnp.concatenate([gap, total[:, :-1]], axis=1)
            elif k == 2:
                total = jnp.concatenate([total[:, 1:], gap], axis=1)
            else:
                kept = total[:, :, 192:256]
            tall = total if tall is None else tall + total
        gap = jnp.zeros((1, 8, 64), F32)
        total = (
            jnp.concatenate([gap, tall[:-1, :, 0:64]], axis=0)
            + tall[:, :, 64:128]
            + jnp.concatenate([tall[1:, :, 128:192], gap], axis=0)
        )
        moved[128 * a : 128 * a + 128, 0:64] = (kept + leaky_relu(total)).reshape(128, 64)
    total = None
    for h in range(8):
        rows = moved[pl.ds(h, 64, stride=8), :].astype(BF)
        term = jnp.dot(rows[:, 0:64], spread_ref[h], preferred_element_type=F32)
        total = term if total is None else total + term
    out_ref[...] = total.astype(BF).reshape(4, 16, 512)


def moved_by(x, sectors, band_of):
    count, bands = lax.axis_size("sector"), lax.axis_size("blk")
    pairs = []
    for s in range(count):
        for b in range(bands):
            if 0 <= band_of(b) < bands:
                pairs.append((s * bands + b, (s + sectors) % count * bands + band_of(b)))
    return lax.ppermute(x, ("sector", "blk"), pairs)


def shaped(*dims, dtype=BF):
    return jax.ShapeDtypeStruct(dims, dtype)


def run(kernel, outs, scratch, flops, name, *args, limit=24, hbm=(), aliases=None):
    return pl.pallas_call(
        kernel,
        out_shape=outs,
        in_specs=[pl.BlockSpec(memory_space=pl.ANY) if n in hbm else VMEM for n in range(len(args))],
        out_specs=jax.tree.map(lambda _: VMEM, outs),
        scratch_shapes=scratch,
        input_output_aliases=aliases or {},
        compiler_params=pltpu.CompilerParams(vmem_limit_bytes=limit << 20),
        cost_estimate=pl.CostEstimate(flops=flops, bytes_accessed=1 << 20, transcendentals=0),
        name=name,
    )(*args)


def per_device(features, residual_first, residual_second, shortcut_first, shortcut_second,
               first_reduce_weight, second_reduce_weight, coarse_kernel):
    tiles, sector_edge, band_edge, corner = run(
        tiles_kernel,
        (shaped(16, 16, 16, 128), shaped(EDGE, 16, 16, 128), shaped(16, EDGE, 16, 128), shaped(EDGE, EDGE, 16, 128)),
        (pltpu.VMEM((16, 16, 2048), BF), pltpu.SemaphoreType.DMA((8,))),
        1 << 30, "tiles", features, limit=8, hbm=(0,),
    )
    sector_edge = moved_by(sector_edge, -1, lambda b: b)
    band_edge = moved_by(band_edge, 0, lambda b: b - 1)
    corner = moved_by(corner, -1, lambda b: b - 1)
    held = (
        shaped(22, 22, 16, 256), shaped(21, 22, 16, 256), shaped(22, 20, 16, 256), shaped(21, 21, 16, 256),
        shaped(9, 11, 16, 128, dtype=F32),
    )
    made = run(
        inner_kernel,
        (shaped(4, 256, 256),) * 4 + (shaped(256, 512), shaped(256, 256), shaped(256, 256), shaped(256, 128)) + held,
        (
            pltpu.VMEM((4, 3, 3, 64, 64), BF),
            pltpu.VMEM((3, 3, 3, 64, 128), BF),
            pltpu.VMEM((14, 14, 16, 128), F32),
            pltpu.SemaphoreType.DMA((5,)),
        ),
        6 << 30, "inner", tiles,
        residual_first, residual_second, shortcut_first, shortcut_second, first_reduce_weight,
        hbm=(1, 2, 3, 4, 5),
    )
    weights, levels = made[:8], made[8:]
    y, *_ = run(
        outer_kernel,
        (shaped(160, 256),) + held,
        (pltpu.VMEM((14, 20, 16, 128), F32), pltpu.VMEM((9, 11, 8, 384), F32)),
        6 << 30, "outer", *levels, sector_edge, band_edge, corner, *weights, second_reduce_weight,
        aliases={n: n + 1 for n in range(5)},
    )
    halo = moved_by(y[80:160], 1, lambda b: b)
    far = moved_by(y, 0, lambda b: b ^ 2)
    near = moved_by(y, 0, lambda b: b ^ 1)
    far_halo = moved_by(halo, 0, lambda b: b ^ 2)
    last = moved_by(jnp.concatenate([halo, far, far_halo], axis=0), 0, lambda b: b ^ 1)
    wc, spread = run(
        late_kernel,
        (shaped(3, 3, 256, 256), shaped(8, 64, 512)),
        (pltpu.VMEM((3, 3, 3, 64, 256), BF), pltpu.SemaphoreType.DMA),
        1 << 30, "late", y, jnp.swapaxes(coarse_kernel, 3, 4), limit=8, hbm=(1,),
    )
    return run(
        coarse_kernel_body,
        shaped(4, 16, 512),
        (pltpu.VMEM((6, 18, 8, 256), F32), pltpu.VMEM((512, 128), F32)),
        2 << 30, "coarse", y, near, halo, far, far_halo, last, wc, spread, limit=16,
    )


def solution(mesh):
    in_specs = (P("sector", "blk", None),) + (P(),) * 6 + (P(None, None, None, None, "blk"),)
    return jax.shard_map(
        per_device, mesh=mesh, in_specs=in_specs, out_specs=P("sector", None, "blk"), check_vma=False
    )
```

time: 52.9 us -> 47.6 us (0.90)
  local copies, waits for them, and re-layouts: 7.76 us -> 1.26 us
  Pallas kernels: 14.7 us -> 18.8 us
  waiting for transfers between devices: 13.7 us -> 11.2 us
    unnamed x19 -> x16, local copies, waits for them, and re-layouts: 7.74 us -> 1.25 us
    pallas_call x4 -> x5, Pallas kernels: 14.7 us -> 18.8 us  [run(): pl.pallas_call(kernel, out_shape=outs, in_specs=[pl.BlockSpec(memory_spac...]
    ppermute x6 -> x8, waiting for transfers between devices: 13.7 us -> 11.2 us  [moved_by(): return lax.ppermute(x, ('sector', 'blk'), pairs)]
    ppermute x6 -> x8, starting transfers between devices: 16.2 us -> 16.1 us  [moved_by(): return lax.ppermute(x, ('sector', 'blk'), pairs)]
  transfers between devices with their start and end apart: 6 -> 8, of which waited for: 4 -> 4; matrix products, arithmetic and copies ran while one was open for 4% -> 0% of each run, Pallas kernels for 1% -> 18%
where the time goes in v2:
time: 47.6 us; the launch traced here: 47.5 us
  Pallas kernels  18.8 us (39%)
  starting transfers between devices  16.1 us (34%)
  waiting for transfers between devices  11.2 us (24%)
  local copies, waits for them, and re-layouts  1.26 us (3%)
    pallas_call x5, Pallas kernels, run(): pl.pallas_call(kernel, out_shape=outs, in_specs=[pl.BlockSpec(memory_spac...  18.8 us
    ppermute x8, starting transfers between devices, moved_by(): return lax.ppermute(x, ('sector', 'blk'), pairs)  16.1 us
    ppermute x8, waiting for transfers between devices, moved_by(): return lax.ppermute(x, ('sector', 'blk'), pairs)  11.2 us
    unnamed x16, local copies, waits for them, and re-layouts  1.25 us
  transfers between devices with their start and end apart: 8, of which 4 were waited for; matrix products, arithmetic and copies ran while one was open for 0% of the time, Pallas kernels for 18%

profile of v2, /device:TPU:1, one launch (start us, length us, event | category | flops | bytes accessed | tf_op | source)
XLA Modules:
  0.0 47.5 jit_solution(468329706945207826)
XLA Ops:
  0.0 1.2 %copy-done.1 = bf16[16,16,2048]{2,1,0:T(8,128)(2,1)S(1)} copy-done((bf16[16,16,2048]{2,1,0:T(8,128)(2,1)S(1)}, bf16[16,16,2048]{2,1,0:T(8,128)(2,1)}, u32[]{:S(2)}) %copy-start.1) | copy-done | bytes 1048600
  1.2 0.0 copy-start.7
  1.2 1.8 %tiles.1 = (bf16[16,16,16,128]{3,2,1,0:T(8,128)(2,1)S(1)}, bf16[5,16,16,128]{3,2,1,0:T(8,128)(2,1)S(1)}, bf16[16,5,16,128]{3,2,1,0:T(8,128)(2,1)S(1)}, bf16[5,5,16,128]{3,2,1,0:T(8,128)(2,1)S(1)}) custom-call(bf16[16,16,2048]{2,1,0:T(8,128)(2,1)S(1)} %copy-done.1), custom_call_target="tpu_custom_call" | custom-call | flops 1073741824 | bytes 1048576 | tf_op jit(solution)/shard_map/tiles/pallas_call | solution.py:304
  3.0 9.6 %collective-permute-start.2 = (bf16[5,5,16,128]{3,2,1,0:T(8,128)(2,1)S(1)}, bf16[5,5,16,128]{3,2,1,0:T(8,128)(2,1)S(1)}, u32[]{:S(2)}, u32[]{:S(2)}) collective-permute-start(bf16[5,5,16,128]{3,2,1,0:T(8,128)(2,1)S(1)} %get-tuple-element.33), channel_id=1, source_target_pairs={{1,124},{2,125},{3,126},{5,0},{6,1},{7,2},{9,4},{10,5},{11,6},{13,... | collective-permute-start | bytes 307208 | tf_op jit(solution)/shard_map/ppermute | solution.py:296
  12.6 0.1 collective-permute-start
  12.7 1.9 %collective-permute-start.1 = (bf16[16,5,16,128]{3,2,1,0:T(8,128)(2,1)S(1)}, bf16[16,5,16,128]{3,2,1,0:T(8,128)(2,1)S(1)}, u32[]{:S(2)}, u32[]{:S(2)}) collective-permute-start(bf16[16,5,16,128]{3,2,1,0:T(8,128)(2,1)S(1)} %get-tuple-element.32), channel_id=1, source_target_pairs={{1,0},{2,1},{3,2},{5,4},{6,5},{7,6},{9,8},{10,9},{11,10},{13,12},{... | collective-permute-start | bytes 983048 | tf_op jit(solution)/shard_map/ppermute | solution.py:296
  14.7 0.0 copy-start
  14.7 8.0 %inner.1 = (bf16[4,256,256]{2,1,0:T(8,128)(2,1)S(1)}, bf16[4,256,256]{2,1,0:T(8,128)(2,1)S(1)}, bf16[4,256,256]{2,1,0:T(8,128)(2,1)S(1)}, bf16[4,256,256]{2,1,0:...) custom-call(bf16[16,16,16,128]{3,2,1,0:T(8,128)(2,1)S(1)} %get-tuple, ...), custom_call_target="tpu_custom_call" | custom-call | flops 6442450944 | bytes 1048576 | tf_op jit(solution)/shard_map/inner/pallas_call | solution.py:304
  22.7 0.0 collective-permute-done.2.corner_ref
  22.7 0.0 collective-permute-done.sector_ref
  22.8 2.1 %collective-permute-done.1.band_ref = bf16[16,5,16,128]{3,2,1,0:T(8,128)(2,1)S(1)} collective-permute-done((bf16[16,5,16,128]{3,2,1,0:T(8,128)(2,1)S(1)}, bf16[16,5,16,128]{3,2,1,0:T(8,128)(2,1)S(1)}, u32[]{:S(2)}, u32[]{:S(2)}) %collective-permute-start.1) | collective-permute-done | bytes 327712 | tf_op jit(solution)/shard_map/ppermute | solution.py:296
  24.8 5.8 %outer.1 = (bf16[160,256]{1,0:T(8,128)(2,1)S(1)}, bf16[22,22,16,256]{3,2,1,0:T(8,128)(2,1)S(1)}, bf16[21,22,16,256]{3,2,1,0:T(8,128)(2,1)S(1)}, bf16[22,20,16,25...) custom-call(bf16[22,22,16,256]{3,2,1,0:T(8,128)(2,1)S(1)} %get-tuple, ...), custom_call_target="tpu_custom_call", output_to_operand_aliasing={{1}: (0, {}), {2}: (1, {}), {3}: (2, {}), {4}: (3, {}), {5}... | custom-call | flops 6442450944 | bytes 1048576 | tf_op jit(solution)/shard_map/outer/pallas_call | solution.py:304
  30.6 2.4 %collective-permute-start.4 = (bf16[80,256]{1,0:T(8,128)(2,1)S(1)}, bf16[80,256]{1,0:T(8,128)(2,1)S(1)}, u32[]{:S(2)}, u32[]{:S(2)}) collective-permute-start(bf16[80,256]{1,0:T(8,128)(2,1)S(1)} %slice.3), channel_id=1, source_target_pairs={{0,4},{1,5},{2,6},{3,7},{4,8},{5,9},{6,10},{7,11},{8,12},{9,13},{1... | collective-permute-start | bytes 122888 | tf_op jit(solution)/shard_map/ppermute | solution.py:296
  32.9 0.0 collective-permute-start.5
  32.9 4.9 %collective-permute-done.4.halo_ref = bf16[80,256]{1,0:T(8,128)(2,1)S(1)} collective-permute-done((bf16[80,256]{1,0:T(8,128)(2,1)S(1)}, bf16[80,256]{1,0:T(8,128)(2,1)S(1)}, u32[]{:S(2)}, u32[]{:S(2)}) %collective-permute-start.4) | collective-permute-done | bytes 40992 | tf_op jit(solution)/shard_map/ppermute | solution.py:296
  37.8 1.6 %collective-permute-start.6 = (bf16[80,256]{1,0:T(8,128)(2,1)S(1)}, bf16[80,256]{1,0:T(8,128)(2,1)S(1)}, u32[]{:S(2)}, u32[]{:S(2)}) collective-permute-start(bf16[80,256]{1,0:T(8,128)(2,1)S(1)} %collective-permute-done.4.halo_ref), channel_id=1, source_target_pairs={{0,2},{1,3},{2,0},{3,1},{4,6},{5,7},{6,4},{7,5},{8,10},{9,11},{10,... | collective-permute-start | bytes 122888 | tf_op jit(solution)/shard_map/ppermute | solution.py:296
  39.4 3.4 %collective-permute-done.6.far_halo_ref = bf16[80,256]{1,0:T(8,128)(2,1)S(1)} collective-permute-done((bf16[80,256]{1,0:T(8,128)(2,1)S(1)}, bf16[80,256]{1,0:T(8,128)(2,1)S(1)}, u32[]{:S(2)}, u32[]{:S(2)}) %collective-permute-start.6) | collective-permute-done | bytes 40992 | tf_op jit(solution)/shard_map/ppermute | solution.py:296
  42.9 0.0 collective-permute-done.5.far_ref
  42.9 0.5 collective-permute-start.7
  43.4 0.1 collective-permute-start.3
  43.5 0.4 late.1
  43.8 0.8 %collective-permute-done.3.near_ref = bf16[160,256]{1,0:T(8,128)(2,1)S(1)} collective-permute-done((bf16[160,256]{1,0:T(8,128)(2,1)S(1)}, bf16[160,256]{1,0:T(8,128)(2,1)S(1)}, u32[]{:S(2)}, u32[]{:S(2)}) %collective-permute-start.3) | collective-permute-done | bytes 81952 | tf_op jit(solution)/shard_map/ppermute | solution.py:296
  44.6 0.0 collective-permute-done.7.last_ref
  44.6 2.8 %coarse.1 = bf16[4,16,512]{2,1,0:T(8,128)(2,1)} custom-call(bf16[160,256]{1,0:T(8,128)(2,1)S(1)} %get-tuple-element.42.y_ref.own_ref, bf16[160,256]{1,0:T(8,128)(2,1)S(1)} %collective-permute-done.3.near_ref, bf16[80,256]{1,0:T(8,128)(2,1)S(1)} %collective-permute-done.4.halo_ref, bf16[160,256]{1,0:T(8,128)(2,1)S(1)} %collective-permute-done.5.far_ref, ...), custom_call_target="tpu_custom_call" | custom-call | flops 2147483648 | bytes 1048576 | tf_op jit(solution)/shard_map/coarse/pallas_call | solution.py:304
  (15 shorter events, 0.0 us)
Async XLA Ops:
  0.0 1.2 %copy-start.1 = (bf16[16,16,2048]{2,1,0:T(8,128)(2,1)S(1)}, bf16[16,16,2048]{2,1,0:T(8,128)(2,1)}, u32[]{:S(2)}) copy-start(bf16[16,16,2048]{2,1,0:T(8,128)(2,1)} %x_hbm.1) | copy-start | bytes 3145732
  1.2 13.4 %copy-start.3 = (bf16[3,3,3,64,128]{4,3,2,1,0:T(8,128)(2,1)S(1)}, bf16[3,3,3,64,128]{4,3,2,1,0:T(8,128)(2,1)}, u32[]{:S(2)}) copy-start(bf16[3,3,3,64,128]{4,3,2,1,0:T(8,128)(2,1)} %w1_hbm.1) | copy-start | bytes 1327108
  1.2 13.4 %copy-start.4 = (bf16[3,3,64,64]{3,2,1,0:T(8,128)(2,1)S(1)}, bf16[3,3,64,64]{3,2,1,0:T(8,128)(2,1)}, u32[]{:S(2)}) copy-start(bf16[3,3,64,64]{3,2,1,0:T(8,128)(2,1)} %wp_hbm.1) | copy-start | bytes 221188
  1.2 13.4 %copy-start.5 = (bf16[3,3,64,64]{3,2,1,0:T(8,128)(2,1)S(1)}, bf16[3,3,64,64]{3,2,1,0:T(8,128)(2,1)}, u32[]{:S(2)}) copy-start(bf16[3,3,64,64]{3,2,1,0:T(8,128)(2,1)} %wp2_hbm.1) | copy-start | bytes 221188
  1.2 13.4 %copy-start.6 = (bf16[3,3,64,64]{3,2,1,0:T(8,128)(2,1)S(1)}, bf16[3,3,64,64]{3,2,1,0:T(8,128)(2,1)}, u32[]{:S(2)}) copy-start(bf16[3,3,64,64]{3,2,1,0:T(8,128)(2,1)} %wq_hbm.1) | copy-start | bytes 221188
  1.2 13.4 %copy-start.7 = (bf16[3,3,64,64]{3,2,1,0:T(8,128)(2,1)S(1)}, bf16[3,3,64,64]{3,2,1,0:T(8,128)(2,1)}, u32[]{:S(2)}) copy-start(bf16[3,3,64,64]{3,2,1,0:T(8,128)(2,1)} %wq2_hbm.1) | copy-start | bytes 221188
  3.0 19.7 %collective-permute-start.2 = (bf16[5,5,16,128]{3,2,1,0:T(8,128)(2,1)S(1)}, bf16[5,5,16,128]{3,2,1,0:T(8,128)(2,1)S(1)}, u32[]{:S(2)}, u32[]{:S(2)}) collective-permute-start(bf16[5,5,16,128]{3,2,1,0:T(8,128)(2,1)S(1)} %get-tuple-element.33), channel_id=1, source_target_pairs={{1,124},{2,125},{3,126},{5,0},{6,1},{7,2},{9,4},{10,5},{11,6},{13,... | collective-permute-start | bytes 307208 | tf_op jit(solution)/shard_map/ppermute | solution.py:296
  12.6 10.1 %collective-permute-start = (bf16[5,16,16,128]{3,2,1,0:T(8,128)(2,1)S(1)}, bf16[5,16,16,128]{3,2,1,0:T(8,128)(2,1)S(1)}, u32[]{:S(2)}, u32[]{:S(2)}) collective-permute-start(bf16[5,16,16,128]{3,2,1,0:T(8,128)(2,1)S(1)} %get-tuple-element.31), channel_id=1, source_target_pairs={{0,124},{1,125},{2,126},{3,127},{4,0},{5,1},{6,2},{7,3},{8,4},{9,5... | collective-permute-start | bytes 983048 | tf_op jit(solution)/shard_map/ppermute | solution.py:296
  12.7 12.1 %collective-permute-start.1 = (bf16[16,5,16,128]{3,2,1,0:T(8,128)(2,1)S(1)}, bf16[16,5,16,128]{3,2,1,0:T(8,128)(2,1)S(1)}, u32[]{:S(2)}, u32[]{:S(2)}) collective-permute-start(bf16[16,5,16,128]{3,2,1,0:T(8,128)(2,1)S(1)} %get-tuple-element.32), channel_id=1, source_target_pairs={{1,0},{2,1},{3,2},{5,4},{6,5},{7,6},{9,8},{10,9},{11,10},{13,12},{... | collective-permute-start | bytes 983048 | tf_op jit(solution)/shard_map/ppermute | solution.py:296
  14.7 10.1 %copy-start = (bf16[3,3,3,128,256]{4,3,2,1,0:T(8,128)(2,1)S(1)}, bf16[3,3,3,128,256]{4,3,2,1,0:T(8,128)(2,1)}, u32[]{:S(2)}) copy-start(bf16[3,3,3,128,256]{4,3,2,1,0:T(8,128)(2,1)} %w2_ref.1) | copy-start | bytes 5308420
  24.8 18.7 %copy-start.2 = (bf16[3,3,3,256,64]{3,4,2,1,0:T(8,128)(2,1)S(1)}, bf16[3,3,3,256,64]{3,4,2,1,0:T(8,128)(2,1)}, u32[]{:S(2)}) copy-start(bf16[3,3,3,256,64]{3,4,2,1,0:T(8,128)(2,1)} %param.15) | copy-start | bytes 2654212
  30.6 7.2 %collective-permute-start.4 = (bf16[80,256]{1,0:T(8,128)(2,1)S(1)}, bf16[80,256]{1,0:T(8,128)(2,1)S(1)}, u32[]{:S(2)}, u32[]{:S(2)}) collective-permute-start(bf16[80,256]{1,0:T(8,128)(2,1)S(1)} %slice.3), channel_id=1, source_target_pairs={{0,4},{1,5},{2,6},{3,7},{4,8},{5,9},{6,10},{7,11},{8,12},{9,13},{1... | collective-permute-start | bytes 122888 | tf_op jit(solution)/shard_map/ppermute | solution.py:296
  32.9 9.9 %collective-permute-start.5 = (bf16[160,256]{1,0:T(8,128)(2,1)S(1)}, bf16[160,256]{1,0:T(8,128)(2,1)S(1)}, u32[]{:S(2)}, u32[]{:S(2)}) collective-permute-start(bf16[160,256]{1,0:T(8,128)(2,1)S(1)} %get-tuple-element.42.y_ref.own_ref), channel_id=1, source_target_pairs={{0,2},{1,3},{2,0},{3,1},{4,6},{5,7},{6,4},{7,5},{8,10},{9,11},{10,... | collective-permute-start | bytes 245768 | tf_op jit(solution)/shard_map/ppermute | solution.py:296
  37.8 5.0 %collective-permute-start.6 = (bf16[80,256]{1,0:T(8,128)(2,1)S(1)}, bf16[80,256]{1,0:T(8,128)(2,1)S(1)}, u32[]{:S(2)}, u32[]{:S(2)}) collective-permute-start(bf16[80,256]{1,0:T(8,128)(2,1)S(1)} %collective-permute-done.4.halo_ref), channel_id=1, source_target_pairs={{0,2},{1,3},{2,0},{3,1},{4,6},{5,7},{6,4},{7,5},{8,10},{9,11},{10,... | collective-permute-start | bytes 122888 | tf_op jit(solution)/shard_map/ppermute | solution.py:296
  42.9 1.8 %collective-permute-start.7 = (bf16[320,256]{1,0:T(8,128)(2,1)S(1)}, bf16[320,256]{1,0:T(8,128)(2,1)S(1)}, u32[]{:S(2)}, u32[]{:S(2)}) collective-permute-start(bf16[320,256]{1,0:T(8,128)(2,1)S(1)} %pad_maximum_fusion), channel_id=1, source_target_pairs={{0,1},{1,0},{2,3},{3,2},{4,5},{5,4},{6,7},{7,6},{8,9},{9,8},{10,11... | collective-permute-start | bytes 491528 | tf_op jit(solution)/shard_map/ppermute | solution.py:296
  43.4 1.3 %collective-permute-start.3 = (bf16[160,256]{1,0:T(8,128)(2,1)S(1)}, bf16[160,256]{1,0:T(8,128)(2,1)S(1)}, u32[]{:S(2)}, u32[]{:S(2)}) collective-permute-start(bf16[160,256]{1,0:T(8,128)(2,1)S(1)} %get-tuple-element.42.y_ref.own_ref), channel_id=1, source_target_pairs={{0,1},{1,0},{2,3},{3,2},{4,5},{5,4},{6,7},{7,6},{8,9},{9,8},{10,11... | collective-permute-start | bytes 245768 | tf_op jit(solution)/shard_map/ppermute | solution.py:296

commit v3 on v2

--- a/solution.py
+++ b/solution.py
@@ -109,37 +109,24 @@
     gg[a - 1 : a - 1 + rows, r + 1 : r + 1 + cols] = leaky_relu(total).astype(BF).astype(F32)
 
 
-def tiles_kernel(x_hbm, tiles_ref, sector_ref, band_ref, corner_ref, x_ref, sems):
-    rows = x_hbm.shape[0]
-    copies = []
-    for part in range(8):
-        at = pl.ds(rows // 8 * part, rows // 8)
-        copies.append(pltpu.make_async_copy(x_hbm.at[at], x_ref.at[at], sems.at[part]))
-        copies[-1].start()
-    for a in range(rows):
-        if a % (rows // 8) == 0:
-            copies[a // (rows // 8)].wait()
-        tiles = x_ref[a].reshape(x_ref.shape[1], 16, 128)
-        tiles_ref[a] = tiles
-        band_ref[a] = tiles[:EDGE]
-        if a < EDGE:
-            sector_ref[a] = tiles
-            corner_ref[a] = tiles[:EDGE]
+def band_edge_kernel(x_ref, band_ref):
+    for a in range(x_ref.shape[0]):
+        band_ref[a] = x_ref[a, 0:8].reshape(8, 16, 128)[:EDGE]
+
+
+def sector_edge_kernel(x_ref, band_ref, sector_ref, corner_ref):
+    for a in range(EDGE):
+        sector_ref[a] = x_ref[a].reshape(x_ref.shape[1], 16, 128)
+        corner_ref[a] = band_ref[a]
 
 
 def inner_kernel(
-    tiles_ref, wp_hbm, wp2_hbm, wq_hbm, wq2_hbm, w1_hbm,
+    x_ref, wp_raw, wp2_raw, wq_raw, wq2_raw, w1_raw,
     wp, wp2, wq, wq2, w_oo, w_oe, w_eo, w_ee, xx, pp, qq, ff, gg,
-    raw, raw1, part, sems,
+    part,
 ):
-    copies = [pltpu.make_async_copy(w, raw.at[n], sems.at[n]) for n, w in enumerate((wp_hbm, wq_hbm, wp2_hbm, wq2_hbm))]
-    copies.append(pltpu.make_async_copy(w1_hbm, raw1, sems.at[4]))
-    for copy in copies:
-        copy.start()
-    own = tiles_ref.shape[0]
+    own = x_ref.shape[0]
     blank = jnp.zeros((1, 16, 256), BF)
-    for a in range(own):
-        put(xx, (a, slice(1, own + 1)), tiles_ref[a])
     for a in range(own + EDGE):
         xx[a, 0:1] = blank
         pp[a, 0:1] = blank
@@ -148,10 +135,11 @@
         gg[a, 0:1] = jnp.zeros((1, 16, 128), F32)
     xx[own + EDGE] = jnp.zeros(xx.shape[1:], BF)
     qq[own + EDGE] = jnp.zeros(qq.shape[1:], BF)
+    for a in range(own):
+        put(xx, (a, slice(1, own + 1)), x_ref[a].reshape(own, 16, 128))
 
     zero = jnp.zeros((64, 64), BF)
-    for n, out in enumerate((wp, wq, wp2, wq2)):
-        copies[n].wait()
+    for raw, out in ((wp_raw, wp), (wq_raw, wq), (wp2_raw, wp2), (wq2_raw, wq2)):
         for slot in range(4):
             for block, height in enumerate((0, 1, 2, -1)):
                 for side in range(2):
@@ -160,21 +148,20 @@
                     for upper in range(2):
                         k = height - upper + 1
                         inside = 0 <= tap <= 2 and 0 <= k <= 2
-                        parts.append(raw[n, tap, k] if inside else zero)
+                        parts.append(raw[tap, k] if inside else zero)
                     out[slot, 64 * block : 64 * block + 64, 128 * side : 128 * side + 128] = (
                         jnp.concatenate(parts, axis=1)
                     )
-    copies[4].wait()
     taps = (
         (w_oo, ((0, 0), (0, 2), (2, 0), (2, 2))), (w_oe, ((0, 1), (2, 1))), (w_eo, ((1, 0), (1, 2))), (w_ee, ((1, 1),)),
     )
     for out, pairs in taps:
         for n, (i, j) in enumerate(pairs):
             at = slice(128 * n, 128 * n + 128)
-            out[0:64, at] = raw1[i, j, 1]
-            out[64:128, at] = raw1[i, j, 2]
+            out[0:64, at] = w1_raw[i, j, 1]
+            out[64:128, at] = w1_raw[i, j, 2]
             out[128:192, at] = jnp.zeros((64, 128), BF)
-            out[192:256, at] = raw1[i, j, 0]
+            out[192:256, at] = w1_raw[i, j, 0]
 
     fill_p(xx, pp, wp, 1, 7, 0, 16)
     fill_q(xx, qq, wq, 0, 16, 0, 7)
@@ -182,24 +169,32 @@
     fill_g(ff, gg, w_oo, w_oe, w_eo, w_ee, 1, 6, 0, 7)
 
 
-def outer_kernel(
-    xx_in, pp_in, qq_in, ff_in, gg_in, sector_ref, band_ref, corner_ref,
-    wp, wp2, wq, wq2, w_oo, w_oe, w_eo, w_ee, w2_ref,
-    y_ref, xx, pp, qq, ff, gg, part, cells,
+def band_kernel(
+    xx_in, pp_in, qq_in, ff_in, gg_in, band_ref,
+    wp, wp2, wq, wq2, w_oo, w_oe, w_eo, w_ee,
+    xx, pp, qq, ff, gg, part,
 ):
     own = band_ref.shape[0]
     for a in range(own):
         put(xx, (a, slice(own + 1, own + 1 + EDGE)), band_ref[a])
+    fill_p(xx, pp, wp, 1, 7, 16, 5)
+    fill_q(xx, qq, wq, 0, 16, 14, 3)
+    fill_f(pp, qq, ff, part, wp2, wq2, 1, 7, 14, 3)
+    fill_g(ff, gg, w_oo, w_oe, w_eo, w_ee, 1, 6, 7, 3)
+
+
+def outer_kernel(
+    xx_in, pp_in, qq_in, ff_in, gg_in, sector_ref, corner_ref,
+    wp, wp2, wq, wq2, w_oo, w_oe, w_eo, w_ee, w2_ref,
+    y_ref, xx, pp, qq, ff, gg, part, cells,
+):
+    own = sector_ref.shape[1]
     for a in range(EDGE):
         put(xx, (own + a, slice(1, own + 1)), sector_ref[a])
         put(xx, (own + a, slice(own + 1, own + 1 + EDGE)), corner_ref[a])
-    fill_p(xx, pp, wp, 1, 7, 16, 5)
     fill_p(xx, pp, wp, 15, 3, 0, 21)
-    fill_q(xx, qq, wq, 0, 16, 14, 3)
     fill_q(xx, qq, wq, 16, 5, 0, 10)
-    fill_f(pp, qq, ff, part, wp2, wq2, 1, 7, 14, 3)
     fill_f(pp, qq, ff, part, wp2, wq2, 15, 3, 0, 10)
-    fill_g(ff, gg, w_oo, w_oe, w_eo, w_ee, 1, 6, 7, 3)
     fill_g(ff, gg, w_oo, w_oe, w_eo, w_ee, 7, 3, 0, 10)
 
     even = gg[:, :, pl.ds(0, 8, stride=2), :]
@@ -217,9 +212,7 @@
     y_ref[...] = leaky_relu(total).astype(BF)
 
 
-def late_kernel(y_ref, coarse_hbm, coarse_out, spread_out, raw, sem):
-    copy = pltpu.make_async_copy(coarse_hbm, raw, sem)
-    copy.start()
+def late_kernel(y_ref, raw, coarse_out, spread_out):
     row = lax.broadcasted_iota(jnp.int32, (64, 512), 0)
     col = lax.broadcasted_iota(jnp.int32, (64, 512), 1)
     for h in range(8):
@@ -228,12 +221,10 @@
     row = lax.broadcasted_iota(jnp.int32, (64, 256), 0)
     col = lax.broadcasted_iota(jnp.int32, (64, 256), 1)
     own = jnp.where(col == row + 64 * band, 1.0, 0.0).astype(BF)
-    copy.wait()
     for i in range(3):
         for k in range(3):
-            for j in range(3):
-                coarse_out[i, k, 64 * j : 64 * j + 64] = raw[i, j, k]
-            coarse_out[i, k, 192:256] = own if i == 1 and k == 1 else jnp.zeros((64, 256), BF)
+            last = own if i == 1 and k == 1 else jnp.zeros((64, 256), BF)
+            coarse_out[i, k] = jnp.concatenate([raw[i, 0, k], raw[i, 1, k], raw[i, 2, k], last], axis=0).T
 
 
 def coarse_kernel_body(
@@ -260,7 +251,7 @@
         for k in range(3):
             total = None
             for i in range(3):
-                term = lax.dot_general(rows[i], wc_ref[i, k], (((1,), (1,)), ((), ())), preferred_element_type=F32)
+                term = jnp.dot(rows[i], wc_ref[i, k], preferred_element_type=F32)
                 total = term if total is None else total + term
             total = total.reshape(16, 8, 256)
             gap = jnp.zeros((16, 1, 256), F32)
@@ -304,7 +295,7 @@
     return pl.pallas_call(
         kernel,
         out_shape=outs,
-        in_specs=[pl.BlockSpec(memory_space=pl.ANY) if n in hbm else VMEM for n in range(len(args))],
+        in_specs=[pl.BlockSpec(memory_space=pltpu.HBM) if n in hbm else VMEM for n in range(len(args))],
         out_specs=jax.tree.map(lambda _: VMEM, outs),
         scratch_shapes=scratch,
         input_output_aliases=aliases or {},
@@ -316,14 +307,13 @@
 
 def per_device(features, residual_first, residual_second, shortcut_first, shortcut_second,
                first_reduce_weight, second_reduce_weight, coarse_kernel):
-    tiles, sector_edge, band_edge, corner = run(
-        tiles_kernel,
-        (shaped(16, 16, 16, 128), shaped(EDGE, 16, 16, 128), shaped(16, EDGE, 16, 128), shaped(EDGE, EDGE, 16, 128)),
-        (pltpu.VMEM((16, 16, 2048), BF), pltpu.SemaphoreType.DMA((8,))),
-        1 << 30, "tiles", features, limit=8, hbm=(0,),
+    own_band = run(band_edge_kernel, shaped(16, EDGE, 16, 128), (), 2 << 30, "band_edge", features)
+    band_edge = moved_by(own_band, 0, lambda b: b - 1)
+    sector_edge, corner = run(
+        sector_edge_kernel, (shaped(EDGE, 16, 16, 128), shaped(EDGE, EDGE, 16, 128)), (), 4 << 30,
+        "sector_edge", features, own_band,
     )
     sector_edge = moved_by(sector_edge, -1, lambda b: b)
-    band_edge = moved_by(band_edge, 0, lambda b: b - 1)
     corner = moved_by(corner, -1, lambda b: b - 1)
     held = (
         shaped(22, 22, 16, 256), shaped(21, 22, 16, 256), shaped(22, 20, 16, 256), shaped(21, 21, 16, 256),
@@ -333,34 +323,36 @@
         inner_kernel,
         (shaped(4, 256, 256),) * 4 + (shaped(256, 512), shaped(256, 256), shaped(256, 256), shaped(256, 128)) + held,
         (
-            pltpu.VMEM((4, 3, 3, 64, 64), BF),
-            pltpu.VMEM((3, 3, 3, 64, 128), BF),
             pltpu.VMEM((14, 14, 16, 128), F32),
-            pltpu.SemaphoreType.DMA((5,)),
         ),
-        6 << 30, "inner", tiles,
+        6 << 30, "inner", features,
         residual_first, residual_second, shortcut_first, shortcut_second, first_reduce_weight,
-        hbm=(1, 2, 3, 4, 5),
     )
     weights, levels = made[:8], made[8:]
+    levels = run(
+        band_kernel, held, (pltpu.VMEM((14, 6, 16, 128), F32),),
+        3 << 30, "band", *levels, band_edge, *weights,
+        aliases={n: n for n in range(5)},
+    )
+    *levels, sector_edge, corner = lax.optimization_barrier((*levels, sector_edge, corner))
     y, *_ = run(
         outer_kernel,
         (shaped(160, 256),) + held,
-        (pltpu.VMEM((14, 20, 16, 128), F32), pltpu.VMEM((9, 11, 8, 384), F32)),
-        6 << 30, "outer", *levels, sector_edge, band_edge, corner, *weights, second_reduce_weight,
+        (pltpu.VMEM((6, 20, 16, 128), F32), pltpu.VMEM((9, 11, 8, 384), F32)),
+        4 << 30, "outer", *levels, sector_edge, corner, *weights, second_reduce_weight,
         aliases={n: n + 1 for n in range(5)},
     )
+    far = moved_by(y, 0, lambda b: b ^ 2)
     halo = moved_by(y[80:160], 1, lambda b: b)
-    far = moved_by(y, 0, lambda b: b ^ 2)
+    far_halo = moved_by(y[80:160], 1, lambda b: b ^ 2)
     near = moved_by(y, 0, lambda b: b ^ 1)
-    far_halo = moved_by(halo, 0, lambda b: b ^ 2)
-    last = moved_by(jnp.concatenate([halo, far, far_halo], axis=0), 0, lambda b: b ^ 1)
     wc, spread = run(
         late_kernel,
         (shaped(3, 3, 256, 256), shaped(8, 64, 512)),
-        (pltpu.VMEM((3, 3, 3, 64, 256), BF), pltpu.SemaphoreType.DMA),
-        1 << 30, "late", y, jnp.swapaxes(coarse_kernel, 3, 4), limit=8, hbm=(1,),
-    )
+        (), 4 << 30, "late", y, jnp.swapaxes(coarse_kernel, 3, 4), limit=8,
+    )
+    far, near, halo, far_halo, wc, spread = lax.optimization_barrier((far, near, halo, far_halo, wc, spread))
+    last = moved_by(jnp.concatenate([halo, far, far_halo], axis=0), 0, lambda b: b ^ 1)
     return run(
         coarse_kernel_body,
         shaped(4, 16, 512),

time: 47.6 us -> 44.2 us (0.929)
  Pallas kernels: 18.8 us -> 15.3 us
  starting transfers between devices: 16.1 us -> 18.3 us
  waiting for transfers between devices: 11.2 us -> 9.08 us
    pallas_call x5 -> x7, Pallas kernels: 18.8 us -> 15.3 us  [run(): pl.pallas_call(kernel, out_shape=outs, in_specs=[pl.BlockSpec(memory_spac...]
    ppermute x8, starting transfers between devices: 16.1 us -> 18.3 us  [moved_by(): return lax.ppermute(x, ('sector', 'blk'), pairs)]
    ppermute x8, waiting for transfers between devices: 11.2 us -> 9.08 us  [moved_by(): return lax.ppermute(x, ('sector', 'blk'), pairs)]
  transfers between devices with their start and end apart: 8 -> 8, of which waited for: 4 -> 4; matrix products, arithmetic and copies ran while one was open for 0% -> 0% of each run, Pallas kernels for 18% -> 20%
where the time goes in v3:
time: 44.2 us; the launch traced here: 44.1 us
  starting transfers between devices  18.3 us (41%)
  Pallas kernels  15.3 us (35%)
  waiting for transfers between devices  9.08 us (21%)
  local copies, waits for them, and re-layouts  1.27 us (3%)
    ppermute x8, starting transfers between devices, moved_by(): return lax.ppermute(x, ('sector', 'blk'), pairs)  18.3 us
    pallas_call x7, Pallas kernels, run(): pl.pallas_call(kernel, out_shape=outs, in_specs=[pl.BlockSpec(memory_spac...  15.3 us
    ppermute x8, waiting for transfers between devices, moved_by(): return lax.ppermute(x, ('sector', 'blk'), pairs)  9.08 us
    unnamed x16, local copies, waits for them, and re-layouts  1.27 us
  transfers between devices with their start and end apart: 8, of which 4 were waited for; matrix products, arithmetic and copies ran while one was open for 0% of the time, Pallas kernels for 20%

profile of v3, /device:TPU:1, one launch (start us, length us, event | category | flops | bytes accessed | tf_op | source)
XLA Modules:
  0.0 44.1 jit_solution(10983410804181667221)
XLA Ops:
  0.0 1.2 %copy-done.1 = bf16[16,16,2048]{2,1,0:T(8,128)(2,1)S(1)} copy-done((bf16[16,16,2048]{2,1,0:T(8,128)(2,1)S(1)}, bf16[16,16,2048]{2,1,0:T(8,128)(2,1)}, u32[]{:S(2)}) %copy-start.1) | copy-done | bytes 1048600
  1.2 0.1 band_edge.1.band_ref
  1.4 0.0 copy-start.3
  1.4 0.0 copy-start.4
  1.4 0.0 copy-start.5
  1.4 0.0 copy-start.6
  1.4 3.5 %collective-permute-start = (bf16[16,5,16,128]{3,2,1,0:T(8,128)(2,1)S(1)}, bf16[16,5,16,128]{3,2,1,0:T(8,128)(2,1)S(1)}, u32[]{:S(2)}, u32[]{:S(2)}) collective-permute-start(bf16[16,5,16,128]{3,2,1,0:T(8,128)(2,1)S(1)} %band_edge.1.band_ref), channel_id=1, source_target_pairs={{1,0},{2,1},{3,2},{5,4},{6,5},{7,6},{9,8},{10,9},{11,10},{13,12},{... | collective-permute-start | bytes 983048 | tf_op jit(solution)/shard_map/ppermute | solution.py:287
  4.9 0.1 sector_edge.1
  5.0 6.4 %collective-permute-start.1 = (bf16[5,16,16,128]{3,2,1,0:T(8,128)(2,1)S(1)}, bf16[5,16,16,128]{3,2,1,0:T(8,128)(2,1)S(1)}, u32[]{:S(2)}, u32[]{:S(2)}) collective-permute-start(bf16[5,16,16,128]{3,2,1,0:T(8,128)(2,1)S(1)} %get-tuple-element.59), channel_id=1, source_target_pairs={{0,124},{1,125},{2,126},{3,127},{4,0},{5,1},{6,2},{7,3},{8,4},{9,5... | collective-permute-start | bytes 983048 | tf_op jit(solution)/shard_map/ppermute | solution.py:287
  11.4 1.9 %collective-permute-start.2 = (bf16[5,5,16,128]{3,2,1,0:T(8,128)(2,1)S(1)}, bf16[5,5,16,128]{3,2,1,0:T(8,128)(2,1)S(1)}, u32[]{:S(2)}, u32[]{:S(2)}) collective-permute-start(bf16[5,5,16,128]{3,2,1,0:T(8,128)(2,1)S(1)} %get-tuple-element.60), channel_id=1, source_target_pairs={{1,124},{2,125},{3,126},{5,0},{6,1},{7,2},{9,4},{10,5},{11,6},{13,... | collective-permute-start | bytes 307208 | tf_op jit(solution)/shard_map/ppermute | solution.py:287
  13.4 6.3 %inner.1 = (bf16[4,256,256]{2,1,0:T(8,128)(2,1)S(1)}, bf16[4,256,256]{2,1,0:T(8,128)(2,1)S(1)}, bf16[4,256,256]{2,1,0:T(8,128)(2,1)S(1)}, bf16[4,256,256]{2,1,0:...) custom-call(bf16[16,16,2048]{2,1,0:T(8,128)(2,1)S(1)} %copy-done.1, ...), custom_call_target="tpu_custom_call" | custom-call | flops 6442450944 | bytes 1048576 | tf_op jit(solution)/shard_map/inner/pallas_call | solution.py:295
  19.7 1.7 %collective-permute-done.band_ref = bf16[16,5,16,128]{3,2,1,0:T(8,128)(2,1)S(1)} collective-permute-done((bf16[16,5,16,128]{3,2,1,0:T(8,128)(2,1)S(1)}, bf16[16,5,16,128]{3,2,1,0:T(8,128)(2,1)S(1)}, u32[]{:S(2)}, u32[]{:S(2)}) %collective-permute-start) | collective-permute-done | bytes 327712 | tf_op jit(solution)/shard_map/ppermute | solution.py:287
  21.3 2.2 %band.1 = (bf16[22,22,16,256]{3,2,1,0:T(8,128)(2,1)S(1)}, bf16[21,22,16,256]{3,2,1,0:T(8,128)(2,1)S(1)}, bf16[22,20,16,256]{3,2,1,0:T(8,128)(2,1)S(1)}, bf16[21,...) custom-call(bf16[22,22,16,256]{3,2,1,0:T(8,128)(2,1)S(1)} %get-tuple, ...), custom_call_target="tpu_custom_call", output_to_operand_aliasing={{0}: (0, {}), {1}: (1, {}), {2}: (2, {}), {3}: (3, {}), {4}... | custom-call | flops 3221225472 | bytes 1048576 | tf_op jit(solution)/shard_map/band/pallas_call | solution.py:295
  23.6 4.2 %outer.1 = (bf16[160,256]{1,0:T(8,128)(2,1)S(1)}, bf16[22,22,16,256]{3,2,1,0:T(8,128)(2,1)S(1)}, bf16[21,22,16,256]{3,2,1,0:T(8,128)(2,1)S(1)}, bf16[22,20,16,25...) custom-call(bf16[22,22,16,256]{3,2,1,0:T(8,128)(2,1)S(1)} %get-tuple, ...), custom_call_target="tpu_custom_call", output_to_operand_aliasing={{1}: (0, {}), {2}: (1, {}), {3}: (2, {}), {4}: (3, {}), {5}... | custom-call | flops 4294967296 | bytes 1048576 | tf_op jit(solution)/shard_map/outer/pallas_call | solution.py:295
  27.8 2.2 %collective-permute-start.3 = (bf16[160,256]{1,0:T(8,128)(2,1)S(1)}, bf16[160,256]{1,0:T(8,128)(2,1)S(1)}, u32[]{:S(2)}, u32[]{:S(2)}) collective-permute-start(bf16[160,256]{1,0:T(8,128)(2,1)S(1)} %get-tuple-element.68.y_ref.own_ref), channel_id=1, source_target_pairs={{0,2},{1,3},{2,0},{3,1},{4,6},{5,7},{6,4},{7,5},{8,10},{9,11},{10,... | collective-permute-start | bytes 245768 | tf_op jit(solution)/shard_map/ppermute | solution.py:287
  30.0 0.3 collective-permute-start.4
  30.3 0.5 %collective-permute-start.5 = (bf16[80,256]{1,0:T(8,128)(2,1)S(1)}, bf16[80,256]{1,0:T(8,128)(2,1)S(1)}, u32[]{:S(2)}, u32[]{:S(2)}) collective-permute-start(bf16[80,256]{1,0:T(8,128)(2,1)S(1)} %slice.4), channel_id=1, source_target_pairs={{0,4},{1,5},{2,6},{3,7},{4,8},{5,9},{6,10},{7,11},{8,12},{9,13},{1... | collective-permute-start | bytes 122888 | tf_op jit(solution)/shard_map/ppermute | solution.py:287
  30.7 1.5 %collective-permute-start.6 = (bf16[80,256]{1,0:T(8,128)(2,1)S(1)}, bf16[80,256]{1,0:T(8,128)(2,1)S(1)}, u32[]{:S(2)}, u32[]{:S(2)}) collective-permute-start(bf16[80,256]{1,0:T(8,128)(2,1)S(1)} %slice.4), channel_id=1, source_target_pairs={{0,6},{1,7},{2,4},{3,5},{4,10},{5,11},{6,8},{7,9},{8,14},{9,15},{1... | collective-permute-start | bytes 122888 | tf_op jit(solution)/shard_map/ppermute | solution.py:287
  32.2 0.4 late.1
  32.6 4.7 %collective-permute-done.5.halo_ref = bf16[80,256]{1,0:T(8,128)(2,1)S(1)} collective-permute-done((bf16[80,256]{1,0:T(8,128)(2,1)S(1)}, bf16[80,256]{1,0:T(8,128)(2,1)S(1)}, u32[]{:S(2)}, u32[]{:S(2)}) %collective-permute-start.5) | collective-permute-done | bytes 40992 | tf_op jit(solution)/shard_map/ppermute | solution.py:287
  37.3 1.7 %collective-permute-done.6.far_halo_ref = bf16[80,256]{1,0:T(8,128)(2,1)S(1)} collective-permute-done((bf16[80,256]{1,0:T(8,128)(2,1)S(1)}, bf16[80,256]{1,0:T(8,128)(2,1)S(1)}, u32[]{:S(2)}, u32[]{:S(2)}) %collective-permute-start.6) | collective-permute-done | bytes 40992 | tf_op jit(solution)/shard_map/ppermute | solution.py:287
  39.0 2.0 %collective-permute-start.7 = (bf16[320,256]{1,0:T(8,128)(2,1)S(1)}, bf16[320,256]{1,0:T(8,128)(2,1)S(1)}, u32[]{:S(2)}, u32[]{:S(2)}) collective-permute-start(bf16[320,256]{1,0:T(8,128)(2,1)S(1)} %pad_maximum_fusion), channel_id=1, source_target_pairs={{0,1},{1,0},{2,3},{3,2},{4,5},{5,4},{6,7},{7,6},{8,9},{9,8},{10,11... | collective-permute-start | bytes 491528 | tf_op jit(solution)/shard_map/ppermute | solution.py:287
  41.1 1.0 %collective-permute-done.7.last_ref = bf16[320,256]{1,0:T(8,128)(2,1)S(1)} collective-permute-done((bf16[320,256]{1,0:T(8,128)(2,1)S(1)}, bf16[320,256]{1,0:T(8,128)(2,1)S(1)}, u32[]{:S(2)}, u32[]{:S(2)}) %collective-permute-start.7) | collective-permute-done | bytes 163872 | tf_op jit(solution)/shard_map/ppermute | solution.py:287
  42.1 2.0 %coarse.1 = bf16[4,16,512]{2,1,0:T(8,128)(2,1)} custom-call(bf16[160,256]{1,0:T(8,128)(2,1)S(1)} %get-tuple-element.68.y_ref.own_ref, bf16[160,256]{1,0:T(8,128)(2,1)S(1)} %collective-permute-done.4.near_ref, bf16[80,256]{1,0:T(8,128)(2,1)S(1)} %collective-permute-done.5.halo_ref, bf16[160,256]{1,0:T(8,128)(2,1)S(1)} %collective-permute-done.3.far_ref, ...), custom_call_target="tpu_custom_call" | custom-call | flops 2147483648 | bytes 1048576 | tf_op jit(solution)/shard_map/coarse/pallas_call | solution.py:295
  (17 shorter events, 0.1 us)
Async XLA Ops:
  0.0 1.2 %copy-start.1 = (bf16[16,16,2048]{2,1,0:T(8,128)(2,1)S(1)}, bf16[16,16,2048]{2,1,0:T(8,128)(2,1)}, u32[]{:S(2)}) copy-start(bf16[16,16,2048]{2,1,0:T(8,128)(2,1)} %x_ref.5) | copy-start | bytes 3145732
  1.4 11.9 %copy-start.3 = (bf16[3,3,3,64,128]{4,3,2,1,0:T(8,128)(2,1)S(1)}, bf16[3,3,3,64,128]{4,3,2,1,0:T(8,128)(2,1)}, u32[]{:S(2)}) copy-start(bf16[3,3,3,64,128]{4,3,2,1,0:T(8,128)(2,1)} %w1_raw.1) | copy-start | bytes 1327108
  1.4 11.9 %copy-start.4 = (bf16[3,3,64,64]{3,2,1,0:T(8,128)(2,1)S(1)}, bf16[3,3,64,64]{3,2,1,0:T(8,128)(2,1)}, u32[]{:S(2)}) copy-start(bf16[3,3,64,64]{3,2,1,0:T(8,128)(2,1)} %wp_raw.1) | copy-start | bytes 221188
  1.4 11.9 %copy-start.5 = (bf16[3,3,64,64]{3,2,1,0:T(8,128)(2,1)S(1)}, bf16[3,3,64,64]{3,2,1,0:T(8,128)(2,1)}, u32[]{:S(2)}) copy-start(bf16[3,3,64,64]{3,2,1,0:T(8,128)(2,1)} %wp2_raw.1) | copy-start | bytes 221188
  1.4 11.9 %copy-start.6 = (bf16[3,3,64,64]{3,2,1,0:T(8,128)(2,1)S(1)}, bf16[3,3,64,64]{3,2,1,0:T(8,128)(2,1)}, u32[]{:S(2)}) copy-start(bf16[3,3,64,64]{3,2,1,0:T(8,128)(2,1)} %wq_raw.1) | copy-start | bytes 221188
  1.4 11.9 %copy-start.7 = (bf16[3,3,64,64]{3,2,1,0:T(8,128)(2,1)S(1)}, bf16[3,3,64,64]{3,2,1,0:T(8,128)(2,1)}, u32[]{:S(2)}) copy-start(bf16[3,3,64,64]{3,2,1,0:T(8,128)(2,1)} %wq2_raw.1) | copy-start | bytes 221188
  1.4 19.9 %collective-permute-start = (bf16[16,5,16,128]{3,2,1,0:T(8,128)(2,1)S(1)}, bf16[16,5,16,128]{3,2,1,0:T(8,128)(2,1)S(1)}, u32[]{:S(2)}, u32[]{:S(2)}) collective-permute-start(bf16[16,5,16,128]{3,2,1,0:T(8,128)(2,1)S(1)} %band_edge.1.band_ref), channel_id=1, source_target_pairs={{1,0},{2,1},{3,2},{5,4},{6,5},{7,6},{9,8},{10,9},{11,10},{13,12},{... | collective-permute-start | bytes 983048 | tf_op jit(solution)/shard_map/ppermute | solution.py:287
  5.0 18.6 %collective-permute-start.1 = (bf16[5,16,16,128]{3,2,1,0:T(8,128)(2,1)S(1)}, bf16[5,16,16,128]{3,2,1,0:T(8,128)(2,1)S(1)}, u32[]{:S(2)}, u32[]{:S(2)}) collective-permute-start(bf16[5,16,16,128]{3,2,1,0:T(8,128)(2,1)S(1)} %get-tuple-element.59), channel_id=1, source_target_pairs={{0,124},{1,125},{2,126},{3,127},{4,0},{5,1},{6,2},{7,3},{8,4},{9,5... | collective-permute-start | bytes 983048 | tf_op jit(solution)/shard_map/ppermute | solution.py:287
  11.4 12.1 %collective-permute-start.2 = (bf16[5,5,16,128]{3,2,1,0:T(8,128)(2,1)S(1)}, bf16[5,5,16,128]{3,2,1,0:T(8,128)(2,1)S(1)}, u32[]{:S(2)}, u32[]{:S(2)}) collective-permute-start(bf16[5,5,16,128]{3,2,1,0:T(8,128)(2,1)S(1)} %get-tuple-element.60), channel_id=1, source_target_pairs={{1,124},{2,125},{3,126},{5,0},{6,1},{7,2},{9,4},{10,5},{11,6},{13,... | collective-permute-start | bytes 307208 | tf_op jit(solution)/shard_map/ppermute | solution.py:287
  21.3 2.2 %copy-start = (bf16[3,3,3,128,256]{4,3,2,1,0:T(8,128)(2,1)S(1)}, bf16[3,3,3,128,256]{4,3,2,1,0:T(8,128)(2,1)}, u32[]{:S(2)}) copy-start(bf16[3,3,3,128,256]{4,3,2,1,0:T(8,128)(2,1)} %w2_ref.1) | copy-start | bytes 5308420
  23.6 8.6 %copy-start.2 = (bf16[3,3,3,256,64]{3,4,2,1,0:T(8,128)(2,1)S(1)}, bf16[3,3,3,256,64]{3,4,2,1,0:T(8,128)(2,1)}, u32[]{:S(2)}) copy-start(bf16[3,3,3,256,64]{3,4,2,1,0:T(8,128)(2,1)} %param.15) | copy-start | bytes 2654212
  27.8 11.3 %collective-permute-start.3 = (bf16[160,256]{1,0:T(8,128)(2,1)S(1)}, bf16[160,256]{1,0:T(8,128)(2,1)S(1)}, u32[]{:S(2)}, u32[]{:S(2)}) collective-permute-start(bf16[160,256]{1,0:T(8,128)(2,1)S(1)} %get-tuple-element.68.y_ref.own_ref), channel_id=1, source_target_pairs={{0,2},{1,3},{2,0},{3,1},{4,6},{5,7},{6,4},{7,5},{8,10},{9,11},{10,... | collective-permute-start | bytes 245768 | tf_op jit(solution)/shard_map/ppermute | solution.py:287
  30.0 9.0 %collective-permute-start.4 = (bf16[160,256]{1,0:T(8,128)(2,1)S(1)}, bf16[160,256]{1,0:T(8,128)(2,1)S(1)}, u32[]{:S(2)}, u32[]{:S(2)}) collective-permute-start(bf16[160,256]{1,0:T(8,128)(2,1)S(1)} %get-tuple-element.68.y_ref.own_ref), channel_id=1, source_target_pairs={{0,1},{1,0},{2,3},{3,2},{4,5},{5,4},{6,7},{7,6},{8,9},{9,8},{10,11... | collective-permute-start | bytes 245768 | tf_op jit(solution)/shard_map/ppermute | solution.py:287
  30.3 7.1 %collective-permute-start.5 = (bf16[80,256]{1,0:T(8,128)(2,1)S(1)}, bf16[80,256]{1,0:T(8,128)(2,1)S(1)}, u32[]{:S(2)}, u32[]{:S(2)}) collective-permute-start(bf16[80,256]{1,0:T(8,128)(2,1)S(1)} %slice.4), channel_id=1, source_target_pairs={{0,4},{1,5},{2,6},{3,7},{4,8},{5,9},{6,10},{7,11},{8,12},{9,13},{1... | collective-permute-start | bytes 122888 | tf_op jit(solution)/shard_map/ppermute | solution.py:287
  30.7 8.3 %collective-permute-start.6 = (bf16[80,256]{1,0:T(8,128)(2,1)S(1)}, bf16[80,256]{1,0:T(8,128)(2,1)S(1)}, u32[]{:S(2)}, u32[]{:S(2)}) collective-permute-start(bf16[80,256]{1,0:T(8,128)(2,1)S(1)} %slice.4), channel_id=1, source_target_pairs={{0,6},{1,7},{2,4},{3,5},{4,10},{5,11},{6,8},{7,9},{8,14},{9,15},{1... | collective-permute-start | bytes 122888 | tf_op jit(solution)/shard_map/ppermute | solution.py:287
  39.0 3.0 %collective-permute-start.7 = (bf16[320,256]{1,0:T(8,128)(2,1)S(1)}, bf16[320,256]{1,0:T(8,128)(2,1)S(1)}, u32[]{:S(2)}, u32[]{:S(2)}) collective-permute-start(bf16[320,256]{1,0:T(8,128)(2,1)S(1)} %pad_maximum_fusion), channel_id=1, source_target_pairs={{0,1},{1,0},{2,3},{3,2},{4,5},{5,4},{6,7},{7,6},{8,9},{9,8},{10,11... | collective-permute-start | bytes 491528 | tf_op jit(solution)/shard_map/ppermute | solution.py:287

commit v4 on v3

--- a/solution.py
+++ b/solution.py
@@ -7,6 +7,7 @@
 
 BF = jnp.bfloat16
 F32 = jnp.float32
+ROWS = 5
 EDGE = 5
 VMEM = pl.BlockSpec(memory_space=pltpu.VMEM)
 
@@ -66,17 +67,22 @@
 
 
 def fill_p(xx, pp, weights, a, pairs, r, count):
-    total = along_a(xx, weights, a, pairs, r + 1, count).astype(BF)
     for pair in range(pairs):
-        for side in range(2):
-            put(pp, (a + 2 * pair + side, slice(r + 1, r + 1 + count)), total[pair, :, :, 128 * side : 128 * side + 128])
-
-
-def fill_q(xx, qq, weights, a, count, r, pairs):
-    total = along_r(xx, weights, a, count, r, pairs).astype(BF)
-    for pair in range(pairs):
-        for side in range(2):
-            put(qq, (slice(a, a + count), r + 2 * pair + side), total[:, pair, :, 128 * side : 128 * side + 128])
+        for first in range(0, count, 8):
+            width = min(8, count - first)
+            total = along_a(xx, weights, a + 2 * pair, 1, r + 1 + first, width).astype(BF)[0]
+            at = slice(r + 1 + first, r + 1 + first + width)
+            for side in range(2):
+                put(pp, (a + 2 * pair + side, at), total[:, :, 128 * side : 128 * side + 128])
+
+
+def fill_q(xx, qq, weights, a, count, r, pairs, step):
+    for first in range(a, a + count, step):
+        rows = min(step, a + count - first)
+        total = along_r(xx, weights, first, rows, r, pairs).astype(BF)
+        for pair in range(pairs):
+            for side in range(2):
+                put(qq, (slice(first, first + rows), r + 2 * pair + side), total[:, pair, :, 128 * side : 128 * side + 128])
 
 
 def fill_f(pp, qq, ff, part, wp, wq, a, a_pairs, r, r_pairs):
@@ -115,7 +121,7 @@
 
 
 def sector_edge_kernel(x_ref, band_ref, sector_ref, corner_ref):
-    for a in range(EDGE):
+    for a in range(ROWS):
         sector_ref[a] = x_ref[a].reshape(x_ref.shape[1], 16, 128)
         corner_ref[a] = band_ref[a]
 
@@ -127,14 +133,14 @@
 ):
     own = x_ref.shape[0]
     blank = jnp.zeros((1, 16, 256), BF)
-    for a in range(own + EDGE):
+    for a in range(own + ROWS):
         xx[a, 0:1] = blank
         pp[a, 0:1] = blank
         ff[a, 0:1] = blank
     for a in range(9):
         gg[a, 0:1] = jnp.zeros((1, 16, 128), F32)
-    xx[own + EDGE] = jnp.zeros(xx.shape[1:], BF)
-    qq[own + EDGE] = jnp.zeros(qq.shape[1:], BF)
+    xx[own + ROWS] = jnp.zeros(xx.shape[1:], BF)
+    qq[own + ROWS] = jnp.zeros(qq.shape[1:], BF)
     for a in range(own):
         put(xx, (a, slice(1, own + 1)), x_ref[a].reshape(own, 16, 128))
 
@@ -164,8 +170,9 @@
             out[192:256, at] = w1_raw[i, j, 0]
 
     fill_p(xx, pp, wp, 1, 7, 0, 16)
-    fill_q(xx, qq, wq, 0, 16, 0, 7)
-    fill_f(pp, qq, ff, part, wp2, wq2, 1, 7, 0, 7)
+    fill_q(xx, qq, wq, 0, 16, 0, 7, 2)
+    for pair in range(7):
+        fill_f(pp, qq, ff, part, wp2, wq2, 1 + 2 * pair, 1, 0, 7)
     fill_g(ff, gg, w_oo, w_oe, w_eo, w_ee, 1, 6, 0, 7)
 
 
@@ -177,8 +184,11 @@
     own = band_ref.shape[0]
     for a in range(own):
         put(xx, (a, slice(own + 1, own + 1 + EDGE)), band_ref[a])
-    fill_p(xx, pp, wp, 1, 7, 16, 5)
-    fill_q(xx, qq, wq, 0, 16, 14, 3)
+    total = along_a(xx, wp, 1, 7, 17, EDGE).astype(BF)
+    for pair in range(7):
+        for side in range(2):
+            put(pp, (1 + 2 * pair + side, slice(17, 17 + EDGE)), total[pair, :, :, 128 * side : 128 * side + 128])
+    fill_q(xx, qq, wq, 0, 16, 14, 3, 8)
     fill_f(pp, qq, ff, part, wp2, wq2, 1, 7, 14, 3)
     fill_g(ff, gg, w_oo, w_oe, w_eo, w_ee, 1, 6, 7, 3)
 
@@ -189,14 +199,14 @@
     y_ref, xx, pp, qq, ff, gg, part, cells,
 ):
     own = sector_ref.shape[1]
-    for a in range(EDGE):
+    for a in range(ROWS):
         put(xx, (own + a, slice(1, own + 1)), sector_ref[a])
         put(xx, (own + a, slice(own + 1, own + 1 + EDGE)), corner_ref[a])
     fill_p(xx, pp, wp, 15, 3, 0, 21)
-    fill_q(xx, qq, wq, 16, 5, 0, 10)
-    fill_f(pp, qq, ff, part, wp2, wq2, 15, 3, 0, 10)
+    fill_q(xx, qq, wq, 16, 5, 0, 10, 1)
+    for pair in range(3):
+        fill_f(pp, qq, ff, part, wp2, wq2, 15 + 2 * pair, 1, 0, 10)
     fill_g(ff, gg, w_oo, w_oe, w_eo, w_ee, 7, 3, 0, 10)
-
     even = gg[:, :, pl.ds(0, 8, stride=2), :]
     odd = gg[:, :, pl.ds(1, 8, stride=2), :]
     cells[:, :, :, 0:128] = even
@@ -227,31 +237,24 @@
             coarse_out[i, k] = jnp.concatenate([raw[i, 0, k], raw[i, 1, k], raw[i, 2, k], last], axis=0).T
 
 
-def coarse_kernel_body(
-    own_ref, near_ref, halo_ref, far_ref, far_halo_ref, last_ref, wc_ref, spread_ref, out_ref, slab, moved,
-):
-    band = lax.axis_index("blk")
-    blocks = (
-        (0, 2, own_ref[...]), (0, 0, halo_ref[...]), (1, 2, near_ref[...]), (1, 0, last_ref[0:80]),
-        (2, 2, far_ref[...]), (2, 0, far_halo_ref[...]), (3, 2, last_ref[80:240]), (3, 0, last_ref[240:320]),
-    )
-    for place, first, block in blocks:
-        other = jnp.bitwise_xor(band, place)
-        block = block.astype(F32).reshape(-1, 5, 8, 256)
-        at = slice(first, first + block.shape[0])
-        slab[at, pl.ds(4 * other + 1, 4)] = block[:, 1:5]
-
-        @pl.when(other == 0)
-        def _():
-            slab[at, 0:1] = block[:, 0:1]
-
-    for a in range(4):
-        rows = [slab[a + i, 0:16].astype(BF).reshape(128, 256) for i in range(3)]
+def lay(slab, first, other, block):
+    block = block.astype(F32).reshape(-1, 5, 8, 256)
+    at = slice(first, first + block.shape[0])
+    slab[at, pl.ds(4 * other + 1, 4)] = block[:, 1:5]
+
+    @pl.when(other == 0)
+    def _():
+        slab[at, 0:1] = block[:, 0:1]
+
+
+def coarse_rows(slab, wc_ref, spread_ref, moved, first, count):
+    cast = [slab[a, 0:16].astype(BF).reshape(128, 256) for a in range(first, first + count + 2)]
+    for n in range(count):
         tall = None
         for k in range(3):
             total = None
             for i in range(3):
-                term = jnp.dot(rows[i], wc_ref[i, k], preferred_element_type=F32)
+                term = jnp.dot(cast[n + i], wc_ref[i, k], preferred_element_type=F32)
                 total = term if total is None else total + term
             total = total.reshape(16, 8, 256)
             gap = jnp.zeros((16, 1, 256), F32)
@@ -268,13 +271,24 @@
             + tall[:, :, 64:128]
             + jnp.concatenate([tall[1:, :, 128:192], gap], axis=0)
         )
-        moved[128 * a : 128 * a + 128, 0:64] = (kept + leaky_relu(total)).reshape(128, 64)
+        moved[128 * n : 128 * n + 128, 0:64] = (kept + leaky_relu(total)).reshape(128, 64)
     total = None
     for h in range(8):
-        rows = moved[pl.ds(h, 64, stride=8), :].astype(BF)
+        rows = moved[pl.ds(h, 16 * count, stride=8), :].astype(BF)
         term = jnp.dot(rows[:, 0:64], spread_ref[h], preferred_element_type=F32)
         total = term if total is None else total + term
-    out_ref[...] = total.astype(BF).reshape(4, 16, 512)
+    return total.astype(BF)
+
+
+def coarse_kernel_body(own_ref, near_ref, far_ref, halo_ref, last_ref, wc_ref, spread_ref, out_ref, slab, moved):
+    band = lax.axis_index("blk")
+    odd = 2 * jnp.bitwise_and(band, 1)
+    for place, block in enumerate((own_ref[...], near_ref[...], far_ref[...], last_ref[0:160])):
+        lay(slab, 2, jnp.bitwise_xor(band, place), block)
+    halves = (halo_ref[0:80], halo_ref[80:160], last_ref[240:320], last_ref[160:240])
+    for place, block in enumerate(halves):
+        lay(slab, 0, jnp.bitwise_xor(jnp.bitwise_xor(band, place), odd), block)
+    out_ref[...] = coarse_rows(slab, wc_ref, spread_ref, moved, 0, 4).reshape(4, 16, 512)
 
 
 def moved_by(x, sectors, band_of):
@@ -300,7 +314,7 @@
         scratch_shapes=scratch,
         input_output_aliases=aliases or {},
         compiler_params=pltpu.CompilerParams(vmem_limit_bytes=limit << 20),
-        cost_estimate=pl.CostEstimate(flops=flops, bytes_accessed=1 << 20, transcendentals=0),
+        cost_estimate=pl.CostEstimate(flops=flops, bytes_accessed=min(flops, 1 << 20), transcendentals=0),
         name=name,
     )(*args)
 
@@ -310,7 +324,7 @@
     own_band = run(band_edge_kernel, shaped(16, EDGE, 16, 128), (), 2 << 30, "band_edge", features)
     band_edge = moved_by(own_band, 0, lambda b: b - 1)
     sector_edge, corner = run(
-        sector_edge_kernel, (shaped(EDGE, 16, 16, 128), shaped(EDGE, EDGE, 16, 128)), (), 4 << 30,
+        sector_edge_kernel, (shaped(ROWS, 16, 16, 128), shaped(ROWS, EDGE, 16, 128)), (), 4 << 30,
         "sector_edge", features, own_band,
     )
     sector_edge = moved_by(sector_edge, -1, lambda b: b)
@@ -338,26 +352,25 @@
     y, *_ = run(
         outer_kernel,
         (shaped(160, 256),) + held,
-        (pltpu.VMEM((6, 20, 16, 128), F32), pltpu.VMEM((9, 11, 8, 384), F32)),
+        (pltpu.VMEM((2, 20, 16, 128), F32), pltpu.VMEM((9, 11, 8, 384), F32)),
         4 << 30, "outer", *levels, sector_edge, corner, *weights, second_reduce_weight,
         aliases={n: n + 1 for n in range(5)},
     )
+    near = moved_by(y, 0, lambda b: b ^ 1)
     far = moved_by(y, 0, lambda b: b ^ 2)
-    halo = moved_by(y[80:160], 1, lambda b: b)
-    far_halo = moved_by(y[80:160], 1, lambda b: b ^ 2)
-    near = moved_by(y, 0, lambda b: b ^ 1)
+    halo = moved_by(jnp.concatenate([y[80:160], near[80:160]], axis=0), 1, lambda b: b ^ 2 if b % 2 else b)
     wc, spread = run(
         late_kernel,
         (shaped(3, 3, 256, 256), shaped(8, 64, 512)),
         (), 4 << 30, "late", y, jnp.swapaxes(coarse_kernel, 3, 4), limit=8,
     )
-    far, near, halo, far_halo, wc, spread = lax.optimization_barrier((far, near, halo, far_halo, wc, spread))
-    last = moved_by(jnp.concatenate([halo, far, far_halo], axis=0), 0, lambda b: b ^ 1)
+    far, halo, wc, spread = lax.optimization_barrier((far, halo, wc, spread))
+    last = moved_by(jnp.concatenate([far, halo], axis=0), 0, lambda b: b ^ 1)
     return run(
         coarse_kernel_body,
         shaped(4, 16, 512),
         (pltpu.VMEM((6, 18, 8, 256), F32), pltpu.VMEM((512, 128), F32)),
-        2 << 30, "coarse", y, near, halo, far, far_halo, last, wc, spread, limit=16,
+        2 << 30, "coarse", y, near, far, halo, last, wc, spread, limit=16,
     )
 
 

time: 44.2 us -> 42.3 us (0.957)
  starting transfers between devices: 18.3 us -> 14.8 us
  waiting for transfers between devices: 9.08 us -> 11.2 us
  Pallas kernels: 15.3 us -> 14.6 us
    ppermute x8 -> x7, starting transfers between devices: 18.3 us -> 14.8 us  [moved_by(): return lax.ppermute(x, ('sector', 'blk'), pairs)]
    ppermute x8 -> x7, waiting for transfers between devices: 9.08 us -> 11.2 us  [moved_by(): return lax.ppermute(x, ('sector', 'blk'), pairs)]
    pallas_call x7, Pallas kernels: 15.3 us -> 14.6 us  [run(): pl.pallas_call(kernel, out_shape=outs, in_specs=[pl.BlockSpec(memory_spac...]
  transfers between devices with their start and end apart: 8 -> 7, of which waited for: 4 -> 4; matrix products, arithmetic and copies ran while one was open for 0% -> 0% of each run, Pallas kernels for 20% -> 20%
where the time goes in v4:
time: 42.3 us; the launch traced here: 42.1 us
  starting transfers between devices  14.8 us (35%)
  Pallas kernels  14.6 us (35%)
  waiting for transfers between devices  11.2 us (26%)
  local copies, waits for them, and re-layouts  1.27 us (3%)
    ppermute x7, starting transfers between devices, moved_by(): return lax.ppermute(x, ('sector', 'blk'), pairs)  14.8 us
    pallas_call x7, Pallas kernels, run(): pl.pallas_call(kernel, out_shape=outs, in_specs=[pl.BlockSpec(memory_spac...  14.6 us
    ppermute x7, waiting for transfers between devices, moved_by(): return lax.ppermute(x, ('sector', 'blk'), pairs)  11.2 us
    unnamed x16, local copies, waits for them, and re-layouts  1.27 us
  transfers between devices with their start and end apart: 7, of which 4 were waited for; matrix products, arithmetic and copies ran while one was open for 0% of the time, Pallas kernels for 20%

profile of v4, /device:TPU:1, one launch (start us, length us, event | category | flops | bytes accessed | tf_op | source)
XLA Modules:
  0.0 42.1 jit_solution(15797570269437791974)
XLA Ops:
  0.0 1.2 %copy-done.1 = bf16[16,16,2048]{2,1,0:T(8,128)(2,1)S(1)} copy-done((bf16[16,16,2048]{2,1,0:T(8,128)(2,1)S(1)}, bf16[16,16,2048]{2,1,0:T(8,128)(2,1)}, u32[]{:S(2)}) %copy-start.1) | copy-done | bytes 1048600
  1.2 0.1 band_edge.1.band_ref
  1.4 0.0 copy-start.3
  1.4 0.0 copy-start.4
  1.4 0.0 copy-start.5
  1.4 0.0 copy-start.6
  1.4 0.0 copy-start.7
  1.4 3.5 %collective-permute-start = (bf16[16,5,16,128]{3,2,1,0:T(8,128)(2,1)S(1)}, bf16[16,5,16,128]{3,2,1,0:T(8,128)(2,1)S(1)}, u32[]{:S(2)}, u32[]{:S(2)}) collective-permute-start(bf16[16,5,16,128]{3,2,1,0:T(8,128)(2,1)S(1)} %band_edge.1.band_ref), channel_id=1, source_target_pairs={{1,0},{2,1},{3,2},{5,4},{6,5},{7,6},{9,8},{10,9},{11,10},{13,12},{... | collective-permute-start | bytes 983048 | tf_op jit(solution)/shard_map/ppermute | solution.py:301
  4.9 0.1 sector_edge.1
  5.0 6.4 %collective-permute-start.1 = (bf16[5,16,16,128]{3,2,1,0:T(8,128)(2,1)S(1)}, bf16[5,16,16,128]{3,2,1,0:T(8,128)(2,1)S(1)}, u32[]{:S(2)}, u32[]{:S(2)}) collective-permute-start(bf16[5,16,16,128]{3,2,1,0:T(8,128)(2,1)S(1)} %get-tuple-element.57), channel_id=1, source_target_pairs={{0,124},{1,125},{2,126},{3,127},{4,0},{5,1},{6,2},{7,3},{8,4},{9,5... | collective-permute-start | bytes 983048 | tf_op jit(solution)/shard_map/ppermute | solution.py:301
  11.4 1.9 %collective-permute-start.2 = (bf16[5,5,16,128]{3,2,1,0:T(8,128)(2,1)S(1)}, bf16[5,5,16,128]{3,2,1,0:T(8,128)(2,1)S(1)}, u32[]{:S(2)}, u32[]{:S(2)}) collective-permute-start(bf16[5,5,16,128]{3,2,1,0:T(8,128)(2,1)S(1)} %get-tuple-element.58), channel_id=1, source_target_pairs={{1,124},{2,125},{3,126},{5,0},{6,1},{7,2},{9,4},{10,5},{11,6},{13,... | collective-permute-start | bytes 307208 | tf_op jit(solution)/shard_map/ppermute | solution.py:301
  13.4 5.7 %inner.1 = (bf16[4,256,256]{2,1,0:T(8,128)(2,1)S(1)}, bf16[4,256,256]{2,1,0:T(8,128)(2,1)S(1)}, bf16[4,256,256]{2,1,0:T(8,128)(2,1)S(1)}, bf16[4,256,256]{2,1,0:...) custom-call(bf16[16,16,2048]{2,1,0:T(8,128)(2,1)S(1)} %copy-done.1, ...), custom_call_target="tpu_custom_call" | custom-call | flops 6442450944 | bytes 1048576 | tf_op jit(solution)/shard_map/inner/pallas_call | solution.py:309
  19.0 2.3 %collective-permute-done.band_ref = bf16[16,5,16,128]{3,2,1,0:T(8,128)(2,1)S(1)} collective-permute-done((bf16[16,5,16,128]{3,2,1,0:T(8,128)(2,1)S(1)}, bf16[16,5,16,128]{3,2,1,0:T(8,128)(2,1)S(1)}, u32[]{:S(2)}, u32[]{:S(2)}) %collective-permute-start) | collective-permute-done | bytes 327712 | tf_op jit(solution)/shard_map/ppermute | solution.py:301
  21.3 2.2 %band.1 = (bf16[22,22,16,256]{3,2,1,0:T(8,128)(2,1)S(1)}, bf16[21,22,16,256]{3,2,1,0:T(8,128)(2,1)S(1)}, bf16[22,20,16,256]{3,2,1,0:T(8,128)(2,1)S(1)}, bf16[21,...) custom-call(bf16[22,22,16,256]{3,2,1,0:T(8,128)(2,1)S(1)} %get-tuple, ...), custom_call_target="tpu_custom_call", output_to_operand_aliasing={{0}: (0, {}), {1}: (1, {}), {2}: (2, {}), {3}: (3, {}), {4}... | custom-call | flops 3221225472 | bytes 1048576 | tf_op jit(solution)/shard_map/band/pallas_call | solution.py:309
  23.6 4.1 %outer.1 = (bf16[160,256]{1,0:T(8,128)(2,1)S(1)}, bf16[22,22,16,256]{3,2,1,0:T(8,128)(2,1)S(1)}, bf16[21,22,16,256]{3,2,1,0:T(8,128)(2,1)S(1)}, bf16[22,20,16,25...) custom-call(bf16[22,22,16,256]{3,2,1,0:T(8,128)(2,1)S(1)} %get-tuple, ...), custom_call_target="tpu_custom_call", output_to_operand_aliasing={{1}: (0, {}), {2}: (1, {}), {3}: (2, {}), {4}: (3, {}), {5}... | custom-call | flops 4294967296 | bytes 1048576 | tf_op jit(solution)/shard_map/outer/pallas_call | solution.py:309
  27.7 0.1 collective-permute-start.3
  27.8 1.4 %collective-permute-start.4 = (bf16[160,256]{1,0:T(8,128)(2,1)S(1)}, bf16[160,256]{1,0:T(8,128)(2,1)S(1)}, u32[]{:S(2)}, u32[]{:S(2)}) collective-permute-start(bf16[160,256]{1,0:T(8,128)(2,1)S(1)} %get-tuple-element.66.y_ref.own_ref), channel_id=1, source_target_pairs={{0,2},{1,3},{2,0},{3,1},{4,6},{5,7},{6,4},{7,5},{8,10},{9,11},{10,... | collective-permute-start | bytes 245768 | tf_op jit(solution)/shard_map/ppermute | solution.py:301
  29.3 1.4 %collective-permute-start.5 = (bf16[160,256]{1,0:T(8,128)(2,1)S(1)}, bf16[160,256]{1,0:T(8,128)(2,1)S(1)}, u32[]{:S(2)}, u32[]{:S(2)}) collective-permute-start(bf16[160,256]{1,0:T(8,128)(2,1)S(1)} %pad_maximum_fusion.1), channel_id=1, source_target_pairs={{0,4},{1,7},{2,6},{3,5},{4,8},{5,11},{6,10},{7,9},{8,12},{9,15},{1... | collective-permute-start | bytes 245768 | tf_op jit(solution)/shard_map/ppermute | solution.py:301
  30.7 0.4 late.1
  31.1 2.0 %collective-permute-done.4.far_ref = bf16[160,256]{1,0:T(8,128)(2,1)S(1)} collective-permute-done((bf16[160,256]{1,0:T(8,128)(2,1)S(1)}, bf16[160,256]{1,0:T(8,128)(2,1)S(1)}, u32[]{:S(2)}, u32[]{:S(2)}) %collective-permute-start.4) | collective-permute-done | bytes 81952 | tf_op jit(solution)/shard_map/ppermute | solution.py:301
  33.0 5.6 %collective-permute-done.5.halo_ref = bf16[160,256]{1,0:T(8,128)(2,1)S(1)} collective-permute-done((bf16[160,256]{1,0:T(8,128)(2,1)S(1)}, bf16[160,256]{1,0:T(8,128)(2,1)S(1)}, u32[]{:S(2)}, u32[]{:S(2)}) %collective-permute-start.5) | collective-permute-done | bytes 81952 | tf_op jit(solution)/shard_map/ppermute | solution.py:301
  38.6 0.1 collective-permute-start.6
  38.8 1.3 %collective-permute-done.6.last_ref = bf16[320,256]{1,0:T(8,128)(2,1)S(1)} collective-permute-done((bf16[320,256]{1,0:T(8,128)(2,1)S(1)}, bf16[320,256]{1,0:T(8,128)(2,1)S(1)}, u32[]{:S(2)}, u32[]{:S(2)}) %collective-permute-start.6) | collective-permute-done | bytes 163872 | tf_op jit(solution)/shard_map/ppermute | solution.py:301
  40.1 2.0 %coarse.1 = bf16[4,16,512]{2,1,0:T(8,128)(2,1)} custom-call(bf16[160,256]{1,0:T(8,128)(2,1)S(1)} %get-tuple-element.66.y_ref.own_ref, bf16[160,256]{1,0:T(8,128)(2,1)S(1)} %collective-permute-done.3.near_ref, bf16[160,256]{1,0:T(8,128)(2,1)S(1)} %collective-permute-done.4.far_ref, bf16[160,256]{1,0:T(8,128)(2,1)S(1)} %collective-permute-done.5.halo_ref, ...), custom_call_target="tpu_custom_call" | custom-call | flops 2147483648 | bytes 1048576 | tf_op jit(solution)/shard_map/coarse/pallas_call | solution.py:309
  (17 shorter events, 0.1 us)
Async XLA Ops:
  0.0 1.2 %copy-start.1 = (bf16[16,16,2048]{2,1,0:T(8,128)(2,1)S(1)}, bf16[16,16,2048]{2,1,0:T(8,128)(2,1)}, u32[]{:S(2)}) copy-start(bf16[16,16,2048]{2,1,0:T(8,128)(2,1)} %x_ref.5) | copy-start | bytes 3145732
  1.4 11.9 %copy-start.3 = (bf16[3,3,3,64,128]{4,3,2,1,0:T(8,128)(2,1)S(1)}, bf16[3,3,3,64,128]{4,3,2,1,0:T(8,128)(2,1)}, u32[]{:S(2)}) copy-start(bf16[3,3,3,64,128]{4,3,2,1,0:T(8,128)(2,1)} %w1_raw.1) | copy-start | bytes 1327108
  1.4 11.9 %copy-start.4 = (bf16[3,3,64,64]{3,2,1,0:T(8,128)(2,1)S(1)}, bf16[3,3,64,64]{3,2,1,0:T(8,128)(2,1)}, u32[]{:S(2)}) copy-start(bf16[3,3,64,64]{3,2,1,0:T(8,128)(2,1)} %wp_raw.1) | copy-start | bytes 221188
  1.4 11.9 %copy-start.5 = (bf16[3,3,64,64]{3,2,1,0:T(8,128)(2,1)S(1)}, bf16[3,3,64,64]{3,2,1,0:T(8,128)(2,1)}, u32[]{:S(2)}) copy-start(bf16[3,3,64,64]{3,2,1,0:T(8,128)(2,1)} %wp2_raw.1) | copy-start | bytes 221188
  1.4 11.9 %copy-start.6 = (bf16[3,3,64,64]{3,2,1,0:T(8,128)(2,1)S(1)}, bf16[3,3,64,64]{3,2,1,0:T(8,128)(2,1)}, u32[]{:S(2)}) copy-start(bf16[3,3,64,64]{3,2,1,0:T(8,128)(2,1)} %wq_raw.1) | copy-start | bytes 221188
  1.4 11.9 %copy-start.7 = (bf16[3,3,64,64]{3,2,1,0:T(8,128)(2,1)S(1)}, bf16[3,3,64,64]{3,2,1,0:T(8,128)(2,1)}, u32[]{:S(2)}) copy-start(bf16[3,3,64,64]{3,2,1,0:T(8,128)(2,1)} %wq2_raw.1) | copy-start | bytes 221188
  1.4 19.9 %collective-permute-start = (bf16[16,5,16,128]{3,2,1,0:T(8,128)(2,1)S(1)}, bf16[16,5,16,128]{3,2,1,0:T(8,128)(2,1)S(1)}, u32[]{:S(2)}, u32[]{:S(2)}) collective-permute-start(bf16[16,5,16,128]{3,2,1,0:T(8,128)(2,1)S(1)} %band_edge.1.band_ref), channel_id=1, source_target_pairs={{1,0},{2,1},{3,2},{5,4},{6,5},{7,6},{9,8},{10,9},{11,10},{13,12},{... | collective-permute-start | bytes 983048 | tf_op jit(solution)/shard_map/ppermute | solution.py:301
  5.0 18.6 %collective-permute-start.1 = (bf16[5,16,16,128]{3,2,1,0:T(8,128)(2,1)S(1)}, bf16[5,16,16,128]{3,2,1,0:T(8,128)(2,1)S(1)}, u32[]{:S(2)}, u32[]{:S(2)}) collective-permute-start(bf16[5,16,16,128]{3,2,1,0:T(8,128)(2,1)S(1)} %get-tuple-element.57), channel_id=1, source_target_pairs={{0,124},{1,125},{2,126},{3,127},{4,0},{5,1},{6,2},{7,3},{8,4},{9,5... | collective-permute-start | bytes 983048 | tf_op jit(solution)/shard_map/ppermute | solution.py:301
  11.4 12.2 %collective-permute-start.2 = (bf16[5,5,16,128]{3,2,1,0:T(8,128)(2,1)S(1)}, bf16[5,5,16,128]{3,2,1,0:T(8,128)(2,1)S(1)}, u32[]{:S(2)}, u32[]{:S(2)}) collective-permute-start(bf16[5,5,16,128]{3,2,1,0:T(8,128)(2,1)S(1)} %get-tuple-element.58), channel_id=1, source_target_pairs={{1,124},{2,125},{3,126},{5,0},{6,1},{7,2},{9,4},{10,5},{11,6},{13,... | collective-permute-start | bytes 307208 | tf_op jit(solution)/shard_map/ppermute | solution.py:301
  21.3 2.3 %copy-start = (bf16[3,3,3,128,256]{4,3,2,1,0:T(8,128)(2,1)S(1)}, bf16[3,3,3,128,256]{4,3,2,1,0:T(8,128)(2,1)}, u32[]{:S(2)}) copy-start(bf16[3,3,3,128,256]{4,3,2,1,0:T(8,128)(2,1)} %w2_ref.1) | copy-start | bytes 5308420
  23.6 7.0 %copy-start.2 = (bf16[3,3,3,256,64]{3,4,2,1,0:T(8,128)(2,1)S(1)}, bf16[3,3,3,256,64]{3,4,2,1,0:T(8,128)(2,1)}, u32[]{:S(2)}) copy-start(bf16[3,3,3,256,64]{3,4,2,1,0:T(8,128)(2,1)} %param.15) | copy-start | bytes 2654212
  27.7 1.5 %collective-permute-start.3 = (bf16[160,256]{1,0:T(8,128)(2,1)S(1)}, bf16[160,256]{1,0:T(8,128)(2,1)S(1)}, u32[]{:S(2)}, u32[]{:S(2)}) collective-permute-start(bf16[160,256]{1,0:T(8,128)(2,1)S(1)} %get-tuple-element.66.y_ref.own_ref), channel_id=1, source_target_pairs={{0,1},{1,0},{2,3},{3,2},{4,5},{5,4},{6,7},{7,6},{8,9},{9,8},{10,11... | collective-permute-start | bytes 245768 | tf_op jit(solution)/shard_map/ppermute | solution.py:301
  27.8 5.2 %collective-permute-start.4 = (bf16[160,256]{1,0:T(8,128)(2,1)S(1)}, bf16[160,256]{1,0:T(8,128)(2,1)S(1)}, u32[]{:S(2)}, u32[]{:S(2)}) collective-permute-start(bf16[160,256]{1,0:T(8,128)(2,1)S(1)} %get-tuple-element.66.y_ref.own_ref), channel_id=1, source_target_pairs={{0,2},{1,3},{2,0},{3,1},{4,6},{5,7},{6,4},{7,5},{8,10},{9,11},{10,... | collective-permute-start | bytes 245768 | tf_op jit(solution)/shard_map/ppermute | solution.py:301
  29.3 9.4 %collective-permute-start.5 = (bf16[160,256]{1,0:T(8,128)(2,1)S(1)}, bf16[160,256]{1,0:T(8,128)(2,1)S(1)}, u32[]{:S(2)}, u32[]{:S(2)}) collective-permute-start(bf16[160,256]{1,0:T(8,128)(2,1)S(1)} %pad_maximum_fusion.1), channel_id=1, source_target_pairs={{0,4},{1,7},{2,6},{3,5},{4,8},{5,11},{6,10},{7,9},{8,12},{9,15},{1... | collective-permute-start | bytes 245768 | tf_op jit(solution)/shard_map/ppermute | solution.py:301
  38.6 1.5 %collective-permute-start.6 = (bf16[320,256]{1,0:T(8,128)(2,1)S(1)}, bf16[320,256]{1,0:T(8,128)(2,1)S(1)}, u32[]{:S(2)}, u32[]{:S(2)}) collective-permute-start(bf16[320,256]{1,0:T(8,128)(2,1)S(1)} %pad_maximum_fusion), channel_id=1, source_target_pairs={{0,1},{1,0},{2,3},{3,2},{4,5},{5,4},{6,7},{7,6},{8,9},{9,8},{10,11... | collective-permute-start | bytes 491528 | tf_op jit(solution)/shard_map/ppermute | solution.py:301

commit v5 on v4

--- a/solution.py
+++ b/solution.py
@@ -115,15 +115,17 @@
     gg[a - 1 : a - 1 + rows, r + 1 : r + 1 + cols] = leaky_relu(total).astype(BF).astype(F32)
 
 
-def band_edge_kernel(x_ref, band_ref):
-    for a in range(x_ref.shape[0]):
-        band_ref[a] = x_ref[a, 0:8].reshape(8, 16, 128)[:EDGE]
-
-
-def sector_edge_kernel(x_ref, band_ref, sector_ref, corner_ref):
+def sector_edge_kernel(x_ref, sector_ref):
     for a in range(ROWS):
         sector_ref[a] = x_ref[a].reshape(x_ref.shape[1], 16, 128)
-        corner_ref[a] = band_ref[a]
+
+
+def band_edge_kernel(x_ref, sector_ref, band_ref, corner_ref):
+    for a in range(ROWS):
+        corner_ref[a] = sector_ref[a, 0:EDGE]
+        band_ref[a] = sector_ref[a, 0:EDGE]
+    for a in range(ROWS, x_ref.shape[0]):
+        band_ref[a] = x_ref[a, 0:8].reshape(8, 16, 128)[:EDGE]
 
 
 def inner_kernel(
@@ -280,14 +282,16 @@
     return total.astype(BF)
 
 
-def coarse_kernel_body(own_ref, near_ref, far_ref, halo_ref, last_ref, wc_ref, spread_ref, out_ref, slab, moved):
+def coarse_kernel_body(
+    own_ref, near_ref, halo_ref, far_ref, far_halo_ref, last_ref, wc_ref, spread_ref, out_ref, slab, moved,
+):
     band = lax.axis_index("blk")
-    odd = 2 * jnp.bitwise_and(band, 1)
-    for place, block in enumerate((own_ref[...], near_ref[...], far_ref[...], last_ref[0:160])):
-        lay(slab, 2, jnp.bitwise_xor(band, place), block)
-    halves = (halo_ref[0:80], halo_ref[80:160], last_ref[240:320], last_ref[160:240])
-    for place, block in enumerate(halves):
-        lay(slab, 0, jnp.bitwise_xor(jnp.bitwise_xor(band, place), odd), block)
+    blocks = (
+        (0, 2, own_ref[...]), (0, 0, halo_ref[...]), (1, 2, near_ref[...]), (1, 0, last_ref[0:80]),
+        (2, 2, far_ref[...]), (2, 0, far_halo_ref[...]), (3, 2, last_ref[80:240]), (3, 0, last_ref[240:320]),
+    )
+    for place, first, block in blocks:
+        lay(slab, first, jnp.bitwise_xor(band, place), block)
     out_ref[...] = coarse_rows(slab, wc_ref, spread_ref, moved, 0, 4).reshape(4, 16, 512)
 
 
@@ -321,13 +325,12 @@
 
 def per_device(features, residual_first, residual_second, shortcut_first, shortcut_second,
                first_reduce_weight, second_reduce_weight, coarse_kernel):
-    own_band = run(band_edge_kernel, shaped(16, EDGE, 16, 128), (), 2 << 30, "band_edge", features)
-    band_edge = moved_by(own_band, 0, lambda b: b - 1)
-    sector_edge, corner = run(
-        sector_edge_kernel, (shaped(ROWS, 16, 16, 128), shaped(ROWS, EDGE, 16, 128)), (), 4 << 30,
-        "sector_edge", features, own_band,
-    )
-    sector_edge = moved_by(sector_edge, -1, lambda b: b)
+    own_sector = run(sector_edge_kernel, shaped(ROWS, 16, 16, 128), (), 2 << 30, "sector_edge", features)
+    sector_edge = moved_by(own_sector, -1, lambda b: b)
+    band_edge, corner = run(
+        band_edge_kernel, (shaped(16, EDGE, 16, 128), shaped(ROWS, EDGE, 16, 128)), (), 4 << 30, "band_edge", features, own_sector
+    )
+    band_edge = moved_by(band_edge, 0, lambda b: b - 1)
     corner = moved_by(corner, -1, lambda b: b - 1)
     held = (
         shaped(22, 22, 16, 256), shaped(21, 22, 16, 256), shaped(22, 20, 16, 256), shaped(21, 21, 16, 256),
@@ -339,13 +342,13 @@
         (
             pltpu.VMEM((14, 14, 16, 128), F32),
         ),
-        6 << 30, "inner", features,
+        1 << 20, "inner", features,
         residual_first, residual_second, shortcut_first, shortcut_second, first_reduce_weight,
     )
     weights, levels = made[:8], made[8:]
     levels = run(
         band_kernel, held, (pltpu.VMEM((14, 6, 16, 128), F32),),
-        3 << 30, "band", *levels, band_edge, *weights,
+        1 << 20, "band", *levels, band_edge, *weights,
         aliases={n: n for n in range(5)},
     )
     *levels, sector_edge, corner = lax.optimization_barrier((*levels, sector_edge, corner))
@@ -356,21 +359,22 @@
         4 << 30, "outer", *levels, sector_edge, corner, *weights, second_reduce_weight,
         aliases={n: n + 1 for n in range(5)},
     )
+    halo = moved_by(y[80:160], 1, lambda b: b)
+    far_halo = moved_by(y[80:160], 1, lambda b: b ^ 2)
+    far = moved_by(y, 0, lambda b: b ^ 2)
     near = moved_by(y, 0, lambda b: b ^ 1)
-    far = moved_by(y, 0, lambda b: b ^ 2)
-    halo = moved_by(jnp.concatenate([y[80:160], near[80:160]], axis=0), 1, lambda b: b ^ 2 if b % 2 else b)
     wc, spread = run(
         late_kernel,
         (shaped(3, 3, 256, 256), shaped(8, 64, 512)),
         (), 4 << 30, "late", y, jnp.swapaxes(coarse_kernel, 3, 4), limit=8,
     )
-    far, halo, wc, spread = lax.optimization_barrier((far, halo, wc, spread))
-    last = moved_by(jnp.concatenate([far, halo], axis=0), 0, lambda b: b ^ 1)
+    halo, far_halo, far, near, wc, spread = lax.optimization_barrier((halo, far_halo, far, near, wc, spread))
+    last = moved_by(jnp.concatenate([halo, far, far_halo], axis=0), 0, lambda b: b ^ 1)
     return run(
         coarse_kernel_body,
         shaped(4, 16, 512),
         (pltpu.VMEM((6, 18, 8, 256), F32), pltpu.VMEM((512, 128), F32)),
-        2 << 30, "coarse", y, near, far, halo, last, wc, spread, limit=16,
+        2 << 30, "coarse", y, near, halo, far, far_halo, last, wc, spread, limit=16,
     )
 
 

time: 42.3 us -> 40.8 us (0.965)
  waiting for transfers between devices: 11.2 us -> 7.36 us
  starting transfers between devices: 14.8 us -> 17.2 us
    ppermute x7 -> x8, waiting for transfers between devices: 11.2 us -> 7.36 us  [moved_by(): return lax.ppermute(x, ('sector', 'blk'), pairs)]
    ppermute x7 -> x8, starting transfers between devices: 14.8 us -> 17.2 us  [moved_by(): return lax.ppermute(x, ('sector', 'blk'), pairs)]
  transfers between devices with their start and end apart: 7 -> 8, of which waited for: 4 -> 4; matrix products, arithmetic and copies ran while one was open for 0% -> 0% of each run, Pallas kernels for 20% -> 20%
where the time goes in v5:
time: 40.8 us; the launch traced here: 40.6 us
  starting transfers between devices  17.2 us (42%)
  Pallas kernels  14.5 us (36%)
  waiting for transfers between devices  7.36 us (18%)
  local copies, waits for them, and re-layouts  1.27 us (3%)
    ppermute x8, starting transfers between devices, moved_by(): return lax.ppermute(x, ('sector', 'blk'), pairs)  17.2 us
    pallas_call x7, Pallas kernels, run(): pl.pallas_call(kernel, out_shape=outs, in_specs=[pl.BlockSpec(memory_spac...  14.5 us
    ppermute x8, waiting for transfers between devices, moved_by(): return lax.ppermute(x, ('sector', 'blk'), pairs)  7.36 us
    unnamed x16, local copies, waits for them, and re-layouts  1.27 us
  transfers between devices with their start and end apart: 8, of which 4 were waited for; matrix products, arithmetic and copies ran while one was open for 0% of the time, Pallas kernels for 20%

profile of v5, /device:TPU:1, one launch (start us, length us, event | category | flops | bytes accessed | tf_op | source)
XLA Modules:
  0.0 40.6 jit_solution(18063168456176226607)
XLA Ops:
  0.0 1.2 %copy-done.1 = bf16[16,16,2048]{2,1,0:T(8,128)(2,1)S(1)} copy-done((bf16[16,16,2048]{2,1,0:T(8,128)(2,1)S(1)}, bf16[16,16,2048]{2,1,0:T(8,128)(2,1)}, u32[]{:S(2)}) %copy-start.1) | copy-done | bytes 1048600
  1.2 0.1 sector_edge.1.sector_ref
  1.3 0.0 copy-start.2
  1.3 0.0 copy-start.3
  1.3 0.0 copy-start.4
  1.3 0.0 copy-start.5
  1.3 0.0 copy-start.6
  1.3 0.1 band_edge.1
  1.5 3.5 %collective-permute-start = (bf16[16,5,16,128]{3,2,1,0:T(8,128)(2,1)S(1)}, bf16[16,5,16,128]{3,2,1,0:T(8,128)(2,1)S(1)}, u32[]{:S(2)}, u32[]{:S(2)}) collective-permute-start(bf16[16,5,16,128]{3,2,1,0:T(8,128)(2,1)S(1)} %get-tuple-element.46), channel_id=1, source_target_pairs={{1,0},{2,1},{3,2},{5,4},{6,5},{7,6},{9,8},{10,9},{11,10},{13,12},{... | collective-permute-start | bytes 983048 | tf_op jit(solution)/shard_map/ppermute | solution.py:305
  4.9 6.4 %collective-permute-start.1 = (bf16[5,16,16,128]{3,2,1,0:T(8,128)(2,1)S(1)}, bf16[5,16,16,128]{3,2,1,0:T(8,128)(2,1)S(1)}, u32[]{:S(2)}, u32[]{:S(2)}) collective-permute-start(bf16[5,16,16,128]{3,2,1,0:T(8,128)(2,1)S(1)} %sector_edge.1.sector_ref), channel_id=1, source_target_pairs={{0,124},{1,125},{2,126},{3,127},{4,0},{5,1},{6,2},{7,3},{8,4},{9,5... | collective-permute-start | bytes 983048 | tf_op jit(solution)/shard_map/ppermute | solution.py:305
  11.4 1.9 %collective-permute-start.2 = (bf16[5,5,16,128]{3,2,1,0:T(8,128)(2,1)S(1)}, bf16[5,5,16,128]{3,2,1,0:T(8,128)(2,1)S(1)}, u32[]{:S(2)}, u32[]{:S(2)}) collective-permute-start(bf16[5,5,16,128]{3,2,1,0:T(8,128)(2,1)S(1)} %get-tuple-element.60), channel_id=1, source_target_pairs={{1,124},{2,125},{3,126},{5,0},{6,1},{7,2},{9,4},{10,5},{11,6},{13,... | collective-permute-start | bytes 307208 | tf_op jit(solution)/shard_map/ppermute | solution.py:305
  13.3 5.7 %inner.1 = (bf16[4,256,256]{2,1,0:T(8,128)(2,1)S(1)}, bf16[4,256,256]{2,1,0:T(8,128)(2,1)S(1)}, bf16[4,256,256]{2,1,0:T(8,128)(2,1)S(1)}, bf16[4,256,256]{2,1,0:...) custom-call(bf16[16,16,2048]{2,1,0:T(8,128)(2,1)S(1)} %copy-done.1, ...), custom_call_target="tpu_custom_call" | custom-call | flops 1048576 | bytes 1048576 | tf_op jit(solution)/shard_map/inner/pallas_call | solution.py:313
  19.0 2.4 %collective-permute-done.band_ref = bf16[16,5,16,128]{3,2,1,0:T(8,128)(2,1)S(1)} collective-permute-done((bf16[16,5,16,128]{3,2,1,0:T(8,128)(2,1)S(1)}, bf16[16,5,16,128]{3,2,1,0:T(8,128)(2,1)S(1)}, u32[]{:S(2)}, u32[]{:S(2)}) %collective-permute-start) | collective-permute-done | bytes 327712 | tf_op jit(solution)/shard_map/ppermute | solution.py:305
  21.4 2.2 %band.1 = (bf16[22,22,16,256]{3,2,1,0:T(8,128)(2,1)S(1)}, bf16[21,22,16,256]{3,2,1,0:T(8,128)(2,1)S(1)}, bf16[22,20,16,256]{3,2,1,0:T(8,128)(2,1)S(1)}, bf16[21,...) custom-call(bf16[22,22,16,256]{3,2,1,0:T(8,128)(2,1)S(1)} %get-tuple, ...), custom_call_target="tpu_custom_call", output_to_operand_aliasing={{0}: (0, {}), {1}: (1, {}), {2}: (2, {}), {3}: (3, {}), {4}... | custom-call | flops 1048576 | bytes 1048576 | tf_op jit(solution)/shard_map/band/pallas_call | solution.py:313
  23.7 0.0 copy-start.7
  23.7 4.1 %outer.1 = (bf16[160,256]{1,0:T(8,128)(2,1)S(1)}, bf16[22,22,16,256]{3,2,1,0:T(8,128)(2,1)S(1)}, bf16[21,22,16,256]{3,2,1,0:T(8,128)(2,1)S(1)}, bf16[22,20,16,25...) custom-call(bf16[22,22,16,256]{3,2,1,0:T(8,128)(2,1)S(1)} %get-tuple, ...), custom_call_target="tpu_custom_call", output_to_operand_aliasing={{1}: (0, {}), {2}: (1, {}), {3}: (2, {}), {4}: (3, {}), {5}... | custom-call | flops 4294967296 | bytes 1048576 | tf_op jit(solution)/shard_map/outer/pallas_call | solution.py:313
  27.8 1.5 %collective-permute-start.4 = (bf16[80,256]{1,0:T(8,128)(2,1)S(1)}, bf16[80,256]{1,0:T(8,128)(2,1)S(1)}, u32[]{:S(2)}, u32[]{:S(2)}) collective-permute-start(bf16[80,256]{1,0:T(8,128)(2,1)S(1)} %slice.4), channel_id=1, source_target_pairs={{0,6},{1,7},{2,4},{3,5},{4,10},{5,11},{6,8},{7,9},{8,14},{9,15},{1... | collective-permute-start | bytes 122888 | tf_op jit(solution)/shard_map/ppermute | solution.py:305
  29.3 3.4 %collective-permute-start.5 = (bf16[160,256]{1,0:T(8,128)(2,1)S(1)}, bf16[160,256]{1,0:T(8,128)(2,1)S(1)}, u32[]{:S(2)}, u32[]{:S(2)}) collective-permute-start(bf16[160,256]{1,0:T(8,128)(2,1)S(1)} %get-tuple-element.68.y_ref.own_ref), channel_id=1, source_target_pairs={{0,2},{1,3},{2,0},{3,1},{4,6},{5,7},{6,4},{7,5},{8,10},{9,11},{10,... | collective-permute-start | bytes 245768 | tf_op jit(solution)/shard_map/ppermute | solution.py:305
  32.6 0.4 late.1
  33.0 3.6 %collective-permute-done.4.far_halo_ref = bf16[80,256]{1,0:T(8,128)(2,1)S(1)} collective-permute-done((bf16[80,256]{1,0:T(8,128)(2,1)S(1)}, bf16[80,256]{1,0:T(8,128)(2,1)S(1)}, u32[]{:S(2)}, u32[]{:S(2)}) %collective-permute-start.4) | collective-permute-done | bytes 40992 | tf_op jit(solution)/shard_map/ppermute | solution.py:305
  36.7 0.4 collective-permute-done.3.halo_ref
  37.0 0.5 %collective-permute-start.7 = (bf16[320,256]{1,0:T(8,128)(2,1)S(1)}, bf16[320,256]{1,0:T(8,128)(2,1)S(1)}, u32[]{:S(2)}, u32[]{:S(2)}) collective-permute-start(bf16[320,256]{1,0:T(8,128)(2,1)S(1)} %pad_maximum_fusion), channel_id=1, source_target_pairs={{0,1},{1,0},{2,3},{3,2},{4,5},{5,4},{6,7},{7,6},{8,9},{9,8},{10,11... | collective-permute-start | bytes 491528 | tf_op jit(solution)/shard_map/ppermute | solution.py:305
  37.6 1.0 %collective-permute-done.7.last_ref = bf16[320,256]{1,0:T(8,128)(2,1)S(1)} collective-permute-done((bf16[320,256]{1,0:T(8,128)(2,1)S(1)}, bf16[320,256]{1,0:T(8,128)(2,1)S(1)}, u32[]{:S(2)}, u32[]{:S(2)}) %collective-permute-start.7) | collective-permute-done | bytes 163872 | tf_op jit(solution)/shard_map/ppermute | solution.py:305
  38.6 2.0 %coarse.1 = bf16[4,16,512]{2,1,0:T(8,128)(2,1)} custom-call(bf16[160,256]{1,0:T(8,128)(2,1)S(1)} %get-tuple-element.68.y_ref.own_ref, bf16[160,256]{1,0:T(8,128)(2,1)S(1)} %collective-permute-done.6.near_ref, bf16[80,256]{1,0:T(8,128)(2,1)S(1)} %collective-permute-done.3.halo_ref, bf16[160,256]{1,0:T(8,128)(2,1)S(1)} %collective-permute-done.5.far_ref, ...), custom_call_target="tpu_custom_call" | custom-call | flops 2147483648 | bytes 1048576 | tf_op jit(solution)/shard_map/coarse/pallas_call | solution.py:313
  (17 shorter events, 0.1 us)
Async XLA Ops:
  0.0 1.2 %copy-start.1 = (bf16[16,16,2048]{2,1,0:T(8,128)(2,1)S(1)}, bf16[16,16,2048]{2,1,0:T(8,128)(2,1)}, u32[]{:S(2)}) copy-start(bf16[16,16,2048]{2,1,0:T(8,128)(2,1)} %x_ref.5) | copy-start | bytes 3145732
  1.3 12.0 %copy-start.2 = (bf16[3,3,3,64,128]{4,3,2,1,0:T(8,128)(2,1)S(1)}, bf16[3,3,3,64,128]{4,3,2,1,0:T(8,128)(2,1)}, u32[]{:S(2)}) copy-start(bf16[3,3,3,64,128]{4,3,2,1,0:T(8,128)(2,1)} %w1_raw.1) | copy-start | bytes 1327108
  1.3 12.0 %copy-start.3 = (bf16[3,3,64,64]{3,2,1,0:T(8,128)(2,1)S(1)}, bf16[3,3,64,64]{3,2,1,0:T(8,128)(2,1)}, u32[]{:S(2)}) copy-start(bf16[3,3,64,64]{3,2,1,0:T(8,128)(2,1)} %wp_raw.1) | copy-start | bytes 221188
  1.3 12.0 %copy-start.4 = (bf16[3,3,64,64]{3,2,1,0:T(8,128)(2,1)S(1)}, bf16[3,3,64,64]{3,2,1,0:T(8,128)(2,1)}, u32[]{:S(2)}) copy-start(bf16[3,3,64,64]{3,2,1,0:T(8,128)(2,1)} %wp2_raw.1) | copy-start | bytes 221188
  1.3 12.0 %copy-start.5 = (bf16[3,3,64,64]{3,2,1,0:T(8,128)(2,1)S(1)}, bf16[3,3,64,64]{3,2,1,0:T(8,128)(2,1)}, u32[]{:S(2)}) copy-start(bf16[3,3,64,64]{3,2,1,0:T(8,128)(2,1)} %wq_raw.1) | copy-start | bytes 221188
  1.3 12.0 %copy-start.6 = (bf16[3,3,64,64]{3,2,1,0:T(8,128)(2,1)S(1)}, bf16[3,3,64,64]{3,2,1,0:T(8,128)(2,1)}, u32[]{:S(2)}) copy-start(bf16[3,3,64,64]{3,2,1,0:T(8,128)(2,1)} %wq2_raw.1) | copy-start | bytes 221188
  1.5 19.9 %collective-permute-start = (bf16[16,5,16,128]{3,2,1,0:T(8,128)(2,1)S(1)}, bf16[16,5,16,128]{3,2,1,0:T(8,128)(2,1)S(1)}, u32[]{:S(2)}, u32[]{:S(2)}) collective-permute-start(bf16[16,5,16,128]{3,2,1,0:T(8,128)(2,1)S(1)} %get-tuple-element.46), channel_id=1, source_target_pairs={{1,0},{2,1},{3,2},{5,4},{6,5},{7,6},{9,8},{10,9},{11,10},{13,12},{... | collective-permute-start | bytes 983048 | tf_op jit(solution)/shard_map/ppermute | solution.py:305
  4.9 18.7 %collective-permute-start.1 = (bf16[5,16,16,128]{3,2,1,0:T(8,128)(2,1)S(1)}, bf16[5,16,16,128]{3,2,1,0:T(8,128)(2,1)S(1)}, u32[]{:S(2)}, u32[]{:S(2)}) collective-permute-start(bf16[5,16,16,128]{3,2,1,0:T(8,128)(2,1)S(1)} %sector_edge.1.sector_ref), channel_id=1, source_target_pairs={{0,124},{1,125},{2,126},{3,127},{4,0},{5,1},{6,2},{7,3},{8,4},{9,5... | collective-permute-start | bytes 983048 | tf_op jit(solution)/shard_map/ppermute | solution.py:305
  11.4 12.3 %collective-permute-start.2 = (bf16[5,5,16,128]{3,2,1,0:T(8,128)(2,1)S(1)}, bf16[5,5,16,128]{3,2,1,0:T(8,128)(2,1)S(1)}, u32[]{:S(2)}, u32[]{:S(2)}) collective-permute-start(bf16[5,5,16,128]{3,2,1,0:T(8,128)(2,1)S(1)} %get-tuple-element.60), channel_id=1, source_target_pairs={{1,124},{2,125},{3,126},{5,0},{6,1},{7,2},{9,4},{10,5},{11,6},{13,... | collective-permute-start | bytes 307208 | tf_op jit(solution)/shard_map/ppermute | solution.py:305
  21.4 2.3 %copy-start = (bf16[3,3,3,128,256]{4,3,2,1,0:T(8,128)(2,1)S(1)}, bf16[3,3,3,128,256]{4,3,2,1,0:T(8,128)(2,1)}, u32[]{:S(2)}) copy-start(bf16[3,3,3,128,256]{4,3,2,1,0:T(8,128)(2,1)} %w2_ref.1) | copy-start | bytes 5308420
  23.7 9.0 %copy-start.7 = (bf16[3,3,3,256,64]{3,4,2,1,0:T(8,128)(2,1)S(1)}, bf16[3,3,3,256,64]{3,4,2,1,0:T(8,128)(2,1)}, u32[]{:S(2)}) copy-start(bf16[3,3,3,256,64]{3,4,2,1,0:T(8,128)(2,1)} %param.15) | copy-start | bytes 2654212
  27.8 8.9 %collective-permute-start.4 = (bf16[80,256]{1,0:T(8,128)(2,1)S(1)}, bf16[80,256]{1,0:T(8,128)(2,1)S(1)}, u32[]{:S(2)}, u32[]{:S(2)}) collective-permute-start(bf16[80,256]{1,0:T(8,128)(2,1)S(1)} %slice.4), channel_id=1, source_target_pairs={{0,6},{1,7},{2,4},{3,5},{4,10},{5,11},{6,8},{7,9},{8,14},{9,15},{1... | collective-permute-start | bytes 122888 | tf_op jit(solution)/shard_map/ppermute | solution.py:305
  29.3 7.8 %collective-permute-start.3 = (bf16[80,256]{1,0:T(8,128)(2,1)S(1)}, bf16[80,256]{1,0:T(8,128)(2,1)S(1)}, u32[]{:S(2)}, u32[]{:S(2)}) collective-permute-start(bf16[80,256]{1,0:T(8,128)(2,1)S(1)} %slice.4), channel_id=1, source_target_pairs={{0,4},{1,5},{2,6},{3,7},{4,8},{5,9},{6,10},{7,11},{8,12},{9,13},{1... | collective-permute-start | bytes 122888 | tf_op jit(solution)/shard_map/ppermute | solution.py:305
  29.3 7.8 %collective-permute-start.6 = (bf16[160,256]{1,0:T(8,128)(2,1)S(1)}, bf16[160,256]{1,0:T(8,128)(2,1)S(1)}, u32[]{:S(2)}, u32[]{:S(2)}) collective-permute-start(bf16[160,256]{1,0:T(8,128)(2,1)S(1)} %get-tuple-element.68.y_ref.own_ref), channel_id=1, source_target_pairs={{0,1},{1,0},{2,3},{3,2},{4,5},{5,4},{6,7},{7,6},{8,9},{9,8},{10,11... | collective-permute-start | bytes 245768 | tf_op jit(solution)/shard_map/ppermute | solution.py:305
  29.3 7.8 %collective-permute-start.5 = (bf16[160,256]{1,0:T(8,128)(2,1)S(1)}, bf16[160,256]{1,0:T(8,128)(2,1)S(1)}, u32[]{:S(2)}, u32[]{:S(2)}) collective-permute-start(bf16[160,256]{1,0:T(8,128)(2,1)S(1)} %get-tuple-element.68.y_ref.own_ref), channel_id=1, source_target_pairs={{0,2},{1,3},{2,0},{3,1},{4,6},{5,7},{6,4},{7,5},{8,10},{9,11},{10,... | collective-permute-start | bytes 245768 | tf_op jit(solution)/shard_map/ppermute | solution.py:305
  37.0 1.6 %collective-permute-start.7 = (bf16[320,256]{1,0:T(8,128)(2,1)S(1)}, bf16[320,256]{1,0:T(8,128)(2,1)S(1)}, u32[]{:S(2)}, u32[]{:S(2)}) collective-permute-start(bf16[320,256]{1,0:T(8,128)(2,1)S(1)} %pad_maximum_fusion), channel_id=1, source_target_pairs={{0,1},{1,0},{2,3},{3,2},{4,5},{5,4},{6,7},{7,6},{8,9},{9,8},{10,11... | collective-permute-start | bytes 491528 | tf_op jit(solution)/shard_map/ppermute | solution.py:305

commit v6 on v5

--- a/solution.py
+++ b/solution.py
@@ -115,17 +115,17 @@
     gg[a - 1 : a - 1 + rows, r + 1 : r + 1 + cols] = leaky_relu(total).astype(BF).astype(F32)
 
 
-def sector_edge_kernel(x_ref, sector_ref):
+def sector_edge_kernel(x_ref, sector_ref, corner_ref):
     for a in range(ROWS):
-        sector_ref[a] = x_ref[a].reshape(x_ref.shape[1], 16, 128)
-
-
-def band_edge_kernel(x_ref, sector_ref, band_ref, corner_ref):
-    for a in range(ROWS):
-        corner_ref[a] = sector_ref[a, 0:EDGE]
-        band_ref[a] = sector_ref[a, 0:EDGE]
+        tiles = x_ref[a].reshape(x_ref.shape[1], 16, 128)
+        sector_ref[a] = tiles
+        corner_ref[a] = tiles[:EDGE]
+
+
+def band_edge_kernel(x_ref, corner_ref, band_ref):
+    band_ref[0:ROWS] = corner_ref[...]
     for a in range(ROWS, x_ref.shape[0]):
-        band_ref[a] = x_ref[a, 0:8].reshape(8, 16, 128)[:EDGE]
+        band_ref[a] = x_ref[a].reshape(8, 16, 128)[:EDGE]
 
 
 def inner_kernel(
@@ -178,37 +178,42 @@
     fill_g(ff, gg, w_oo, w_oe, w_eo, w_ee, 1, 6, 0, 7)
 
 
-def band_kernel(
-    xx_in, pp_in, qq_in, ff_in, gg_in, band_ref,
+def rows_kernel(
+    xx_in, pp_in, qq_in, ff_in, gg_in, sector_ref,
     wp, wp2, wq, wq2, w_oo, w_oe, w_eo, w_ee,
     xx, pp, qq, ff, gg, part,
+):
+    own = sector_ref.shape[1]
+    for a in range(ROWS):
+        put(xx, (own + a, slice(1, own + 1)), sector_ref[a])
+    fill_p(xx, pp, wp, 15, 3, 0, 16)
+    fill_q(xx, qq, wq, 16, 5, 0, 7, 1)
+    for pair in range(3):
+        fill_f(pp, qq, ff, part, wp2, wq2, 15 + 2 * pair, 1, 0, 7)
+    fill_g(ff, gg, w_oo, w_oe, w_eo, w_ee, 7, 3, 0, 7)
+
+
+def columns_kernel(
+    xx_in, pp_in, qq_in, ff_in, gg_in, band_ref, corner_ref,
+    wp, wp2, wq, wq2, w_oo, w_oe, w_eo, w_ee, w2_ref,
+    y_ref, xx, pp, qq, ff, gg, part, cells,
 ):
     own = band_ref.shape[0]
     for a in range(own):
         put(xx, (a, slice(own + 1, own + 1 + EDGE)), band_ref[a])
-    total = along_a(xx, wp, 1, 7, 17, EDGE).astype(BF)
-    for pair in range(7):
-        for side in range(2):
-            put(pp, (1 + 2 * pair + side, slice(17, 17 + EDGE)), total[pair, :, :, 128 * side : 128 * side + 128])
-    fill_q(xx, qq, wq, 0, 16, 14, 3, 8)
-    fill_f(pp, qq, ff, part, wp2, wq2, 1, 7, 14, 3)
-    fill_g(ff, gg, w_oo, w_oe, w_eo, w_ee, 1, 6, 7, 3)
-
-
-def outer_kernel(
-    xx_in, pp_in, qq_in, ff_in, gg_in, sector_ref, corner_ref,
-    wp, wp2, wq, wq2, w_oo, w_oe, w_eo, w_ee, w2_ref,
-    y_ref, xx, pp, qq, ff, gg, part, cells,
-):
-    own = sector_ref.shape[1]
     for a in range(ROWS):
-        put(xx, (own + a, slice(1, own + 1)), sector_ref[a])
         put(xx, (own + a, slice(own + 1, own + 1 + EDGE)), corner_ref[a])
-    fill_p(xx, pp, wp, 15, 3, 0, 21)
-    fill_q(xx, qq, wq, 16, 5, 0, 10, 1)
-    for pair in range(3):
-        fill_f(pp, qq, ff, part, wp2, wq2, 15 + 2 * pair, 1, 0, 10)
-    fill_g(ff, gg, w_oo, w_oe, w_eo, w_ee, 7, 3, 0, 10)
+    for first in (1, 11):
+        total = along_a(xx, wp, first, 5, 17, EDGE).astype(BF)
+        for pair in range(5):
+            for side in range(2):
+                tiles = total[pair, :, :, 128 * side : 128 * side + 128]
+                put(pp, (first + 2 * pair + side, slice(17, 17 + EDGE)), tiles)
+    fill_q(xx, qq, wq, 0, 21, 14, 3, 7)
+    for first in (1, 11):
+        fill_f(pp, qq, ff, part, wp2, wq2, first, 5, 14, 3)
+    fill_g(ff, gg, w_oo, w_oe, w_eo, w_ee, 1, 9, 7, 3)
+
     even = gg[:, :, pl.ds(0, 8, stride=2), :]
     odd = gg[:, :, pl.ds(1, 8, stride=2), :]
     cells[:, :, :, 0:128] = even
@@ -325,11 +330,11 @@
 
 def per_device(features, residual_first, residual_second, shortcut_first, shortcut_second,
                first_reduce_weight, second_reduce_weight, coarse_kernel):
-    own_sector = run(sector_edge_kernel, shaped(ROWS, 16, 16, 128), (), 2 << 30, "sector_edge", features)
-    sector_edge = moved_by(own_sector, -1, lambda b: b)
-    band_edge, corner = run(
-        band_edge_kernel, (shaped(16, EDGE, 16, 128), shaped(ROWS, EDGE, 16, 128)), (), 4 << 30, "band_edge", features, own_sector
-    )
+    sector_edge, corner = run(
+        sector_edge_kernel, (shaped(ROWS, 16, 16, 128), shaped(ROWS, EDGE, 16, 128)), (), 2 << 30, "sector_edge", features[0:ROWS]
+    )
+    band_edge = run(band_edge_kernel, shaped(16, EDGE, 16, 128), (), 4 << 30, "band_edge", features[:, 0:8], corner)
+    sector_edge = moved_by(sector_edge, -1, lambda b: b)
     band_edge = moved_by(band_edge, 0, lambda b: b - 1)
     corner = moved_by(corner, -1, lambda b: b - 1)
     held = (
@@ -347,16 +352,16 @@
     )
     weights, levels = made[:8], made[8:]
     levels = run(
-        band_kernel, held, (pltpu.VMEM((14, 6, 16, 128), F32),),
-        1 << 20, "band", *levels, band_edge, *weights,
+        rows_kernel, held, (pltpu.VMEM((2, 14, 16, 128), F32),),
+        1 << 20, "rows", *levels, sector_edge, *weights,
         aliases={n: n for n in range(5)},
     )
-    *levels, sector_edge, corner = lax.optimization_barrier((*levels, sector_edge, corner))
+    *levels, band_edge, corner = lax.optimization_barrier((*levels, band_edge, corner))
     y, *_ = run(
-        outer_kernel,
+        columns_kernel,
         (shaped(160, 256),) + held,
-        (pltpu.VMEM((2, 20, 16, 128), F32), pltpu.VMEM((9, 11, 8, 384), F32)),
-        4 << 30, "outer", *levels, sector_edge, corner, *weights, second_reduce_weight,
+        (pltpu.VMEM((10, 6, 16, 128), F32), pltpu.VMEM((9, 11, 8, 384), F32)),
+        4 << 30, "columns", *levels, band_edge, corner, *weights, second_reduce_weight,
         aliases={n: n + 1 for n in range(5)},
     )
     halo = moved_by(y[80:160], 1, lambda b: b)

time: 40.8 us -> 40.3 us (0.988)
  waiting for transfers between devices: 7.36 us -> 6.91 us
    unnamed x16, local copies, waits for them, and re-layouts: 1.27 us -> 0.05 us
    slice x0 -> x2, local copies, waits for them, and re-layouts: none -> 1.03 us  [the longest x1 0.99 us: per_device(): features[0:ROWS]]
    ppermute x8, waiting for transfers between devices: 7.36 us -> 6.91 us  [moved_by(): return lax.ppermute(x, ('sector', 'blk'), pairs)]
  transfers between devices with their start and end apart: 8 -> 8, of which waited for: 4 -> 3; matrix products, arithmetic and copies ran while one was open for 0% -> 0% of each run, Pallas kernels for 20% -> 21%
where the time goes in v6:
time: 40.3 us; the launch traced here: 40.1 us
  starting transfers between devices  17.4 us (43%)
  Pallas kernels  14.5 us (36%)
  waiting for transfers between devices  6.91 us (17%)
  local copies, waits for them, and re-layouts  1.08 us (3%)
    ppermute x8, starting transfers between devices, moved_by(): return lax.ppermute(x, ('sector', 'blk'), pairs)  17.4 us
    pallas_call x7, Pallas kernels, run(): pl.pallas_call(kernel, out_shape=outs, in_specs=[pl.BlockSpec(memory_spac...  14.5 us
    ppermute x8, waiting for transfers between devices, moved_by(): return lax.ppermute(x, ('sector', 'blk'), pairs)  6.91 us
    slice x1, local copies, waits for them, and re-layouts, per_device(): features[0:ROWS]  0.99 us
  transfers between devices with their start and end apart: 8, of which 3 were waited for; matrix products, arithmetic and copies ran while one was open for 0% of the time, Pallas kernels for 21%

profile of v6, /device:TPU:1, one launch (start us, length us, event | category | flops | bytes accessed | tf_op | source)
XLA Modules:
  0.0 40.1 jit_solution(10227871381712461690)
XLA Ops:
  0.0 1.0 %slice.10.x_ref = bf16[5,16,2048]{2,1,0:T(8,128)(2,1)S(1)} slice(bf16[16,16,2048]{2,1,0:T(8,128)(2,1)} %x_ref.1), slice={[0:5], [0:16], [0:2048]} | slice | bytes 655360 | tf_op jit(solution)/shard_map/slice | solution.py:334
  1.0 0.0 copy-start
  1.0 0.1 sector_edge.1
  1.1 7.2 %collective-permute-start = (bf16[5,16,16,128]{3,2,1,0:T(8,128)(2,1)S(1)}, bf16[5,16,16,128]{3,2,1,0:T(8,128)(2,1)S(1)}, u32[]{:S(2)}, u32[]{:S(2)}) collective-permute-start(bf16[5,16,16,128]{3,2,1,0:T(8,128)(2,1)S(1)} %get-tuple-element.46), channel_id=1, source_target_pairs={{0,124},{1,125},{2,126},{3,127},{4,0},{5,1},{6,2},{7,3},{8,4},{9,5... | collective-permute-start | bytes 983048 | tf_op jit(solution)/shard_map/ppermute | solution.py:310
  8.3 0.0 copy-start.2
  8.3 0.0 copy-start.4
  8.4 0.0 copy-start.5
  8.4 0.1 band_edge.1
  8.5 3.0 %collective-permute-start.1 = (bf16[16,5,16,128]{3,2,1,0:T(8,128)(2,1)S(1)}, bf16[16,5,16,128]{3,2,1,0:T(8,128)(2,1)S(1)}, u32[]{:S(2)}, u32[]{:S(2)}) collective-permute-start(bf16[16,5,16,128]{3,2,1,0:T(8,128)(2,1)S(1)} %band_edge.1), channel_id=1, source_target_pairs={{1,0},{2,1},{3,2},{5,4},{6,5},{7,6},{9,8},{10,9},{11,10},{13,12},{... | collective-permute-start | bytes 983048 | tf_op jit(solution)/shard_map/ppermute | solution.py:310
  11.5 2.0 %collective-permute-start.2 = (bf16[5,5,16,128]{3,2,1,0:T(8,128)(2,1)S(1)}, bf16[5,5,16,128]{3,2,1,0:T(8,128)(2,1)S(1)}, u32[]{:S(2)}, u32[]{:S(2)}) collective-permute-start(bf16[5,5,16,128]{3,2,1,0:T(8,128)(2,1)S(1)} %get-tuple-element.60.corner_ref), channel_id=1, source_target_pairs={{1,124},{2,125},{3,126},{5,0},{6,1},{7,2},{9,4},{10,5},{11,6},{13,... | collective-permute-start | bytes 307208 | tf_op jit(solution)/shard_map/ppermute | solution.py:310
  13.5 5.7 %inner.1 = (bf16[4,256,256]{2,1,0:T(8,128)(2,1)S(1)}, bf16[4,256,256]{2,1,0:T(8,128)(2,1)S(1)}, bf16[4,256,256]{2,1,0:T(8,128)(2,1)S(1)}, bf16[4,256,256]{2,1,0:...) custom-call(bf16[16,16,2048]{2,1,0:T(8,128)(2,1)S(1)} %copy-done, ...), custom_call_target="tpu_custom_call" | custom-call | flops 1048576 | bytes 1048576 | tf_op jit(solution)/shard_map/inner/pallas_call | solution.py:318
  19.2 0.0 copy-start.1
  19.2 2.3 %rows.1 = (bf16[22,22,16,256]{3,2,1,0:T(8,128)(2,1)S(1)}, bf16[21,22,16,256]{3,2,1,0:T(8,128)(2,1)S(1)}, bf16[22,20,16,256]{3,2,1,0:T(8,128)(2,1)S(1)}, bf16[21,...) custom-call(bf16[22,22,16,256]{3,2,1,0:T(8,128)(2,1)S(1)} %get-tuple, ...), custom_call_target="tpu_custom_call", output_to_operand_aliasing={{0}: (0, {}), {1}: (1, {}), {2}: (2, {}), {3}: (3, {}), {4}... | custom-call | flops 1048576 | bytes 1048576 | tf_op jit(solution)/shard_map/rows/pallas_call | solution.py:318
  21.6 3.9 %columns.1 = (bf16[160,256]{1,0:T(8,128)(2,1)S(1)}, bf16[22,22,16,256]{3,2,1,0:T(8,128)(2,1)S(1)}, bf16[21,22,16,256]{3,2,1,0:T(8,128)(2,1)S(1)}, bf16[22,20,16,...) custom-call(bf16[22,22,16,256]{3,2,1,0:T(8,128)(2,1)S(1)} %get-tuple, ...), custom_call_target="tpu_custom_call", output_to_operand_aliasing={{1}: (0, {}), {2}: (1, {}), {3}: (2, {}), {4}: (3, {}), {5}... | custom-call | flops 4294967296 | bytes 1048576 | tf_op jit(solution)/shard_map/columns/pallas_call | solution.py:318
  25.5 0.8 %collective-permute-start.3 = (bf16[80,256]{1,0:T(8,128)(2,1)S(1)}, bf16[80,256]{1,0:T(8,128)(2,1)S(1)}, u32[]{:S(2)}, u32[]{:S(2)}) collective-permute-start(bf16[80,256]{1,0:T(8,128)(2,1)S(1)} %slice.12), channel_id=1, source_target_pairs={{0,4},{1,5},{2,6},{3,7},{4,8},{5,9},{6,10},{7,11},{8,12},{9,13},{1... | collective-permute-start | bytes 122888 | tf_op jit(solution)/shard_map/ppermute | solution.py:310
  26.2 2.8 %collective-permute-start.4 = (bf16[80,256]{1,0:T(8,128)(2,1)S(1)}, bf16[80,256]{1,0:T(8,128)(2,1)S(1)}, u32[]{:S(2)}, u32[]{:S(2)}) collective-permute-start(bf16[80,256]{1,0:T(8,128)(2,1)S(1)} %slice.12), channel_id=1, source_target_pairs={{0,6},{1,7},{2,4},{3,5},{4,10},{5,11},{6,8},{7,9},{8,14},{9,15},{1... | collective-permute-start | bytes 122888 | tf_op jit(solution)/shard_map/ppermute | solution.py:310
  29.1 1.1 %collective-permute-start.5 = (bf16[160,256]{1,0:T(8,128)(2,1)S(1)}, bf16[160,256]{1,0:T(8,128)(2,1)S(1)}, u32[]{:S(2)}, u32[]{:S(2)}) collective-permute-start(bf16[160,256]{1,0:T(8,128)(2,1)S(1)} %get-tuple-element.68.y_ref.own_ref), channel_id=1, source_target_pairs={{0,2},{1,3},{2,0},{3,1},{4,6},{5,7},{6,4},{7,5},{8,10},{9,11},{10,... | collective-permute-start | bytes 245768 | tf_op jit(solution)/shard_map/ppermute | solution.py:310
  30.2 0.1 collective-permute-start.6
  30.3 0.4 late.1
  30.7 1.9 %collective-permute-done.3.halo_ref = bf16[80,256]{1,0:T(8,128)(2,1)S(1)} collective-permute-done((bf16[80,256]{1,0:T(8,128)(2,1)S(1)}, bf16[80,256]{1,0:T(8,128)(2,1)S(1)}, u32[]{:S(2)}, u32[]{:S(2)}) %collective-permute-start.3) | collective-permute-done | bytes 40992 | tf_op jit(solution)/shard_map/ppermute | solution.py:310
  32.6 4.0 %collective-permute-done.4.far_halo_ref = bf16[80,256]{1,0:T(8,128)(2,1)S(1)} collective-permute-done((bf16[80,256]{1,0:T(8,128)(2,1)S(1)}, bf16[80,256]{1,0:T(8,128)(2,1)S(1)}, u32[]{:S(2)}, u32[]{:S(2)}) %collective-permute-start.4) | collective-permute-done | bytes 40992 | tf_op jit(solution)/shard_map/ppermute | solution.py:310
  36.6 0.5 %collective-permute-start.7 = (bf16[320,256]{1,0:T(8,128)(2,1)S(1)}, bf16[320,256]{1,0:T(8,128)(2,1)S(1)}, u32[]{:S(2)}, u32[]{:S(2)}) collective-permute-start(bf16[320,256]{1,0:T(8,128)(2,1)S(1)} %pad_maximum_fusion), channel_id=1, source_target_pairs={{0,1},{1,0},{2,3},{3,2},{4,5},{5,4},{6,7},{7,6},{8,9},{9,8},{10,11... | collective-permute-start | bytes 491528 | tf_op jit(solution)/shard_map/ppermute | solution.py:310
  37.1 1.0 %collective-permute-done.7.last_ref = bf16[320,256]{1,0:T(8,128)(2,1)S(1)} collective-permute-done((bf16[320,256]{1,0:T(8,128)(2,1)S(1)}, bf16[320,256]{1,0:T(8,128)(2,1)S(1)}, u32[]{:S(2)}, u32[]{:S(2)}) %collective-permute-start.7) | collective-permute-done | bytes 163872 | tf_op jit(solution)/shard_map/ppermute | solution.py:310
  38.1 2.0 %coarse.1 = bf16[4,16,512]{2,1,0:T(8,128)(2,1)} custom-call(bf16[160,256]{1,0:T(8,128)(2,1)S(1)} %get-tuple-element.68.y_ref.own_ref, bf16[160,256]{1,0:T(8,128)(2,1)S(1)} %collective-permute-done.6.near_ref, bf16[80,256]{1,0:T(8,128)(2,1)S(1)} %collective-permute-done.3.halo_ref, bf16[160,256]{1,0:T(8,128)(2,1)S(1)} %collective-permute-done.5.far_ref, ...), custom_call_target="tpu_custom_call" | custom-call | flops 2147483648 | bytes 1048576 | tf_op jit(solution)/shard_map/coarse/pallas_call | solution.py:318
  (19 shorter events, 0.1 us)
Async XLA Ops:
  1.0 7.3 %copy-start = (bf16[16,16,2048]{2,1,0:T(8,128)(2,1)S(1)}, bf16[16,16,2048]{2,1,0:T(8,128)(2,1)}, u32[]{:S(2)}) copy-start(bf16[16,16,2048]{2,1,0:T(8,128)(2,1)} %x_ref.1) | copy-start | bytes 3145732
  1.1 18.1 %collective-permute-start = (bf16[5,16,16,128]{3,2,1,0:T(8,128)(2,1)S(1)}, bf16[5,16,16,128]{3,2,1,0:T(8,128)(2,1)S(1)}, u32[]{:S(2)}, u32[]{:S(2)}) collective-permute-start(bf16[5,16,16,128]{3,2,1,0:T(8,128)(2,1)S(1)} %get-tuple-element.46), channel_id=1, source_target_pairs={{0,124},{1,125},{2,126},{3,127},{4,0},{5,1},{6,2},{7,3},{8,4},{9,5... | collective-permute-start | bytes 983048 | tf_op jit(solution)/shard_map/ppermute | solution.py:310
  8.3 5.1 %copy-start.2 = (bf16[3,3,3,64,128]{4,3,2,1,0:T(8,128)(2,1)S(1)}, bf16[3,3,3,64,128]{4,3,2,1,0:T(8,128)(2,1)}, u32[]{:S(2)}) copy-start(bf16[3,3,3,64,128]{4,3,2,1,0:T(8,128)(2,1)} %w1_raw.1) | copy-start | bytes 1327108
  8.3 5.1 %copy-start.3 = (bf16[3,3,64,64]{3,2,1,0:T(8,128)(2,1)S(1)}, bf16[3,3,64,64]{3,2,1,0:T(8,128)(2,1)}, u32[]{:S(2)}) copy-start(bf16[3,3,64,64]{3,2,1,0:T(8,128)(2,1)} %wp_raw.1) | copy-start | bytes 221188
  8.3 5.1 %copy-start.4 = (bf16[3,3,64,64]{3,2,1,0:T(8,128)(2,1)S(1)}, bf16[3,3,64,64]{3,2,1,0:T(8,128)(2,1)}, u32[]{:S(2)}) copy-start(bf16[3,3,64,64]{3,2,1,0:T(8,128)(2,1)} %wp2_raw.1) | copy-start | bytes 221188
  8.4 5.1 %copy-start.5 = (bf16[3,3,64,64]{3,2,1,0:T(8,128)(2,1)S(1)}, bf16[3,3,64,64]{3,2,1,0:T(8,128)(2,1)}, u32[]{:S(2)}) copy-start(bf16[3,3,64,64]{3,2,1,0:T(8,128)(2,1)} %wq_raw.1) | copy-start | bytes 221188
  8.4 5.1 %copy-start.6 = (bf16[3,3,64,64]{3,2,1,0:T(8,128)(2,1)S(1)}, bf16[3,3,64,64]{3,2,1,0:T(8,128)(2,1)}, u32[]{:S(2)}) copy-start(bf16[3,3,64,64]{3,2,1,0:T(8,128)(2,1)} %wq2_raw.1) | copy-start | bytes 221188
  8.5 13.0 %collective-permute-start.1 = (bf16[16,5,16,128]{3,2,1,0:T(8,128)(2,1)S(1)}, bf16[16,5,16,128]{3,2,1,0:T(8,128)(2,1)S(1)}, u32[]{:S(2)}, u32[]{:S(2)}) collective-permute-start(bf16[16,5,16,128]{3,2,1,0:T(8,128)(2,1)S(1)} %band_edge.1), channel_id=1, source_target_pairs={{1,0},{2,1},{3,2},{5,4},{6,5},{7,6},{9,8},{10,9},{11,10},{13,12},{... | collective-permute-start | bytes 983048 | tf_op jit(solution)/shard_map/ppermute | solution.py:310
  11.5 10.0 %collective-permute-start.2 = (bf16[5,5,16,128]{3,2,1,0:T(8,128)(2,1)S(1)}, bf16[5,5,16,128]{3,2,1,0:T(8,128)(2,1)S(1)}, u32[]{:S(2)}, u32[]{:S(2)}) collective-permute-start(bf16[5,5,16,128]{3,2,1,0:T(8,128)(2,1)S(1)} %get-tuple-element.60.corner_ref), channel_id=1, source_target_pairs={{1,124},{2,125},{3,126},{5,0},{6,1},{7,2},{9,4},{10,5},{11,6},{13,... | collective-permute-start | bytes 307208 | tf_op jit(solution)/shard_map/ppermute | solution.py:310
  19.2 2.4 %copy-start.1 = (bf16[3,3,3,128,256]{4,3,2,1,0:T(8,128)(2,1)S(1)}, bf16[3,3,3,128,256]{4,3,2,1,0:T(8,128)(2,1)}, u32[]{:S(2)}) copy-start(bf16[3,3,3,128,256]{4,3,2,1,0:T(8,128)(2,1)} %w2_ref.1) | copy-start | bytes 5308420
  21.5 8.8 %copy-start.7 = (bf16[3,3,3,256,64]{3,4,2,1,0:T(8,128)(2,1)S(1)}, bf16[3,3,3,256,64]{3,4,2,1,0:T(8,128)(2,1)}, u32[]{:S(2)}) copy-start(bf16[3,3,3,256,64]{3,4,2,1,0:T(8,128)(2,1)} %param.15) | copy-start | bytes 2654212
  25.5 7.1 %collective-permute-start.3 = (bf16[80,256]{1,0:T(8,128)(2,1)S(1)}, bf16[80,256]{1,0:T(8,128)(2,1)S(1)}, u32[]{:S(2)}, u32[]{:S(2)}) collective-permute-start(bf16[80,256]{1,0:T(8,128)(2,1)S(1)} %slice.12), channel_id=1, source_target_pairs={{0,4},{1,5},{2,6},{3,7},{4,8},{5,9},{6,10},{7,11},{8,12},{9,13},{1... | collective-permute-start | bytes 122888 | tf_op jit(solution)/shard_map/ppermute | solution.py:310
  26.2 10.4 %collective-permute-start.4 = (bf16[80,256]{1,0:T(8,128)(2,1)S(1)}, bf16[80,256]{1,0:T(8,128)(2,1)S(1)}, u32[]{:S(2)}, u32[]{:S(2)}) collective-permute-start(bf16[80,256]{1,0:T(8,128)(2,1)S(1)} %slice.12), channel_id=1, source_target_pairs={{0,6},{1,7},{2,4},{3,5},{4,10},{5,11},{6,8},{7,9},{8,14},{9,15},{1... | collective-permute-start | bytes 122888 | tf_op jit(solution)/shard_map/ppermute | solution.py:310
  29.1 7.5 %collective-permute-start.5 = (bf16[160,256]{1,0:T(8,128)(2,1)S(1)}, bf16[160,256]{1,0:T(8,128)(2,1)S(1)}, u32[]{:S(2)}, u32[]{:S(2)}) collective-permute-start(bf16[160,256]{1,0:T(8,128)(2,1)S(1)} %get-tuple-element.68.y_ref.own_ref), channel_id=1, source_target_pairs={{0,2},{1,3},{2,0},{3,1},{4,6},{5,7},{6,4},{7,5},{8,10},{9,11},{10,... | collective-permute-start | bytes 245768 | tf_op jit(solution)/shard_map/ppermute | solution.py:310
  30.2 6.4 %collective-permute-start.6 = (bf16[160,256]{1,0:T(8,128)(2,1)S(1)}, bf16[160,256]{1,0:T(8,128)(2,1)S(1)}, u32[]{:S(2)}, u32[]{:S(2)}) collective-permute-start(bf16[160,256]{1,0:T(8,128)(2,1)S(1)} %get-tuple-element.68.y_ref.own_ref), channel_id=1, source_target_pairs={{0,1},{1,0},{2,3},{3,2},{4,5},{5,4},{6,7},{7,6},{8,9},{9,8},{10,11... | collective-permute-start | bytes 245768 | tf_op jit(solution)/shard_map/ppermute | solution.py:310
  36.6 1.5 %collective-permute-start.7 = (bf16[320,256]{1,0:T(8,128)(2,1)S(1)}, bf16[320,256]{1,0:T(8,128)(2,1)S(1)}, u32[]{:S(2)}, u32[]{:S(2)}) collective-permute-start(bf16[320,256]{1,0:T(8,128)(2,1)S(1)} %pad_maximum_fusion), channel_id=1, source_target_pairs={{0,1},{1,0},{2,3},{3,2},{4,5},{5,4},{6,7},{7,6},{8,9},{9,8},{10,11... | collective-permute-start | bytes 491528 | tf_op jit(solution)/shard_map/ppermute | solution.py:310

commit v7 on v6

--- a/solution.py
+++ b/solution.py
@@ -172,7 +172,7 @@
             out[192:256, at] = w1_raw[i, j, 0]
 
     fill_p(xx, pp, wp, 1, 7, 0, 16)
-    fill_q(xx, qq, wq, 0, 16, 0, 7, 2)
+    fill_q(xx, qq, wq, 0, 16, 0, 7, 1)
     for pair in range(7):
         fill_f(pp, qq, ff, part, wp2, wq2, 1 + 2 * pair, 1, 0, 7)
     fill_g(ff, gg, w_oo, w_oe, w_eo, w_ee, 1, 6, 0, 7)
@@ -373,7 +373,7 @@
         (shaped(3, 3, 256, 256), shaped(8, 64, 512)),
         (), 4 << 30, "late", y, jnp.swapaxes(coarse_kernel, 3, 4), limit=8,
     )
-    halo, far_halo, far, near, wc, spread = lax.optimization_barrier((halo, far_halo, far, near, wc, spread))
+    halo, far_halo, near, far, wc, spread = lax.optimization_barrier((halo, far_halo, near, far, wc, spread))
     last = moved_by(jnp.concatenate([halo, far, far_halo], axis=0), 0, lambda b: b ^ 1)
     return run(
         coarse_kernel_body,

time: 40.3 us -> 40.3 us (level)
  no operation moved by 1% of the time
where the time goes in v7:
time: 40.3 us; the launch traced here: 40.1 us
  starting transfers between devices  17.3 us (43%)
  Pallas kernels  14.4 us (36%)
  waiting for transfers between devices  7.07 us (18%)
  local copies, waits for them, and re-layouts  1.08 us (3%)
    ppermute x8, starting transfers between devices, moved_by(): return lax.ppermute(x, ('sector', 'blk'), pairs)  17.3 us
    pallas_call x7, Pallas kernels, run(): pl.pallas_call(kernel, out_shape=outs, in_specs=[pl.BlockSpec(memory_spac...  14.4 us
    ppermute x8, waiting for transfers between devices, moved_by(): return lax.ppermute(x, ('sector', 'blk'), pairs)  7.07 us
    slice x1, local copies, waits for them, and re-layouts, per_device(): features[0:ROWS]  0.99 us
  transfers between devices with their start and end apart: 8, of which 3 were waited for; matrix products, arithmetic and copies ran while one was open for 0% of the time, Pallas kernels for 21%

profile of v7, /device:TPU:1, one launch (start us, length us, event | category | flops | bytes accessed | tf_op | source)
XLA Modules:
  0.0 40.1 jit_solution(7229724718927380050)
XLA Ops:
  0.0 1.0 %slice.10.x_ref = bf16[5,16,2048]{2,1,0:T(8,128)(2,1)S(1)} slice(bf16[16,16,2048]{2,1,0:T(8,128)(2,1)} %x_ref.1), slice={[0:5], [0:16], [0:2048]} | slice | bytes 655360 | tf_op jit(solution)/shard_map/slice | solution.py:334
  1.0 0.0 copy-start
  1.0 0.1 sector_edge.1
  1.1 7.2 %collective-permute-start = (bf16[5,16,16,128]{3,2,1,0:T(8,128)(2,1)S(1)}, bf16[5,16,16,128]{3,2,1,0:T(8,128)(2,1)S(1)}, u32[]{:S(2)}, u32[]{:S(2)}) collective-permute-start(bf16[5,16,16,128]{3,2,1,0:T(8,128)(2,1)S(1)} %get-tuple-element.46), channel_id=1, source_target_pairs={{0,124},{1,125},{2,126},{3,127},{4,0},{5,1},{6,2},{7,3},{8,4},{9,5... | collective-permute-start | bytes 983048 | tf_op jit(solution)/shard_map/ppermute | solution.py:310
  8.3 0.0 copy-start.2
  8.3 0.0 copy-start.4
  8.4 0.0 copy-start.5
  8.4 0.1 band_edge.1
  8.5 3.0 %collective-permute-start.1 = (bf16[16,5,16,128]{3,2,1,0:T(8,128)(2,1)S(1)}, bf16[16,5,16,128]{3,2,1,0:T(8,128)(2,1)S(1)}, u32[]{:S(2)}, u32[]{:S(2)}) collective-permute-start(bf16[16,5,16,128]{3,2,1,0:T(8,128)(2,1)S(1)} %band_edge.1), channel_id=1, source_target_pairs={{1,0},{2,1},{3,2},{5,4},{6,5},{7,6},{9,8},{10,9},{11,10},{13,12},{... | collective-permute-start | bytes 983048 | tf_op jit(solution)/shard_map/ppermute | solution.py:310
  11.5 2.0 %collective-permute-start.2 = (bf16[5,5,16,128]{3,2,1,0:T(8,128)(2,1)S(1)}, bf16[5,5,16,128]{3,2,1,0:T(8,128)(2,1)S(1)}, u32[]{:S(2)}, u32[]{:S(2)}) collective-permute-start(bf16[5,5,16,128]{3,2,1,0:T(8,128)(2,1)S(1)} %get-tuple-element.60.corner_ref), channel_id=1, source_target_pairs={{1,124},{2,125},{3,126},{5,0},{6,1},{7,2},{9,4},{10,5},{11,6},{13,... | collective-permute-start | bytes 307208 | tf_op jit(solution)/shard_map/ppermute | solution.py:310
  13.5 5.6 %inner.1 = (bf16[4,256,256]{2,1,0:T(8,128)(2,1)S(1)}, bf16[4,256,256]{2,1,0:T(8,128)(2,1)S(1)}, bf16[4,256,256]{2,1,0:T(8,128)(2,1)S(1)}, bf16[4,256,256]{2,1,0:...) custom-call(bf16[16,16,2048]{2,1,0:T(8,128)(2,1)S(1)} %copy-done, ...), custom_call_target="tpu_custom_call" | custom-call | flops 1048576 | bytes 1048576 | tf_op jit(solution)/shard_map/inner/pallas_call | solution.py:318
  19.2 2.3 %rows.1 = (bf16[22,22,16,256]{3,2,1,0:T(8,128)(2,1)S(1)}, bf16[21,22,16,256]{3,2,1,0:T(8,128)(2,1)S(1)}, bf16[22,20,16,256]{3,2,1,0:T(8,128)(2,1)S(1)}, bf16[21,...) custom-call(bf16[22,22,16,256]{3,2,1,0:T(8,128)(2,1)S(1)} %get-tuple, ...), custom_call_target="tpu_custom_call", output_to_operand_aliasing={{0}: (0, {}), {1}: (1, {}), {2}: (2, {}), {3}: (3, {}), {4}... | custom-call | flops 1048576 | bytes 1048576 | tf_op jit(solution)/shard_map/rows/pallas_call | solution.py:318
  21.5 0.0 collective-permute-done.2.corner_ref
  21.5 0.0 copy-start.7
  21.5 3.9 %columns.1 = (bf16[160,256]{1,0:T(8,128)(2,1)S(1)}, bf16[22,22,16,256]{3,2,1,0:T(8,128)(2,1)S(1)}, bf16[21,22,16,256]{3,2,1,0:T(8,128)(2,1)S(1)}, bf16[22,20,16,...) custom-call(bf16[22,22,16,256]{3,2,1,0:T(8,128)(2,1)S(1)} %get-tuple, ...), custom_call_target="tpu_custom_call", output_to_operand_aliasing={{1}: (0, {}), {2}: (1, {}), {3}: (2, {}), {4}: (3, {}), {5}... | custom-call | flops 4294967296 | bytes 1048576 | tf_op jit(solution)/shard_map/columns/pallas_call | solution.py:318
  25.5 0.8 %collective-permute-start.3 = (bf16[80,256]{1,0:T(8,128)(2,1)S(1)}, bf16[80,256]{1,0:T(8,128)(2,1)S(1)}, u32[]{:S(2)}, u32[]{:S(2)}) collective-permute-start(bf16[80,256]{1,0:T(8,128)(2,1)S(1)} %slice.12), channel_id=1, source_target_pairs={{0,4},{1,5},{2,6},{3,7},{4,8},{5,9},{6,10},{7,11},{8,12},{9,13},{1... | collective-permute-start | bytes 122888 | tf_op jit(solution)/shard_map/ppermute | solution.py:310
  26.2 2.8 %collective-permute-start.4 = (bf16[80,256]{1,0:T(8,128)(2,1)S(1)}, bf16[80,256]{1,0:T(8,128)(2,1)S(1)}, u32[]{:S(2)}, u32[]{:S(2)}) collective-permute-start(bf16[80,256]{1,0:T(8,128)(2,1)S(1)} %slice.12), channel_id=1, source_target_pairs={{0,6},{1,7},{2,4},{3,5},{4,10},{5,11},{6,8},{7,9},{8,14},{9,15},{1... | collective-permute-start | bytes 122888 | tf_op jit(solution)/shard_map/ppermute | solution.py:310
  29.1 1.1 %collective-permute-start.6 = (bf16[160,256]{1,0:T(8,128)(2,1)S(1)}, bf16[160,256]{1,0:T(8,128)(2,1)S(1)}, u32[]{:S(2)}, u32[]{:S(2)}) collective-permute-start(bf16[160,256]{1,0:T(8,128)(2,1)S(1)} %get-tuple-element.68.y_ref.own_ref), channel_id=1, source_target_pairs={{0,2},{1,3},{2,0},{3,1},{4,6},{5,7},{6,4},{7,5},{8,10},{9,11},{10,... | collective-permute-start | bytes 245768 | tf_op jit(solution)/shard_map/ppermute | solution.py:310
  30.2 0.4 late.1
  30.6 2.0 %collective-permute-done.3.halo_ref = bf16[80,256]{1,0:T(8,128)(2,1)S(1)} collective-permute-done((bf16[80,256]{1,0:T(8,128)(2,1)S(1)}, bf16[80,256]{1,0:T(8,128)(2,1)S(1)}, u32[]{:S(2)}, u32[]{:S(2)}) %collective-permute-start.3) | collective-permute-done | bytes 40992 | tf_op jit(solution)/shard_map/ppermute | solution.py:310
  32.6 4.0 %collective-permute-done.4.far_halo_ref = bf16[80,256]{1,0:T(8,128)(2,1)S(1)} collective-permute-done((bf16[80,256]{1,0:T(8,128)(2,1)S(1)}, bf16[80,256]{1,0:T(8,128)(2,1)S(1)}, u32[]{:S(2)}, u32[]{:S(2)}) %collective-permute-start.4) | collective-permute-done | bytes 40992 | tf_op jit(solution)/shard_map/ppermute | solution.py:310
  36.6 0.5 %collective-permute-start.7 = (bf16[320,256]{1,0:T(8,128)(2,1)S(1)}, bf16[320,256]{1,0:T(8,128)(2,1)S(1)}, u32[]{:S(2)}, u32[]{:S(2)}) collective-permute-start(bf16[320,256]{1,0:T(8,128)(2,1)S(1)} %pad_maximum_fusion), channel_id=1, source_target_pairs={{0,1},{1,0},{2,3},{3,2},{4,5},{5,4},{6,7},{7,6},{8,9},{9,8},{10,11... | collective-permute-start | bytes 491528 | tf_op jit(solution)/shard_map/ppermute | solution.py:310
  37.1 1.0 %collective-permute-done.7.last_ref = bf16[320,256]{1,0:T(8,128)(2,1)S(1)} collective-permute-done((bf16[320,256]{1,0:T(8,128)(2,1)S(1)}, bf16[320,256]{1,0:T(8,128)(2,1)S(1)}, u32[]{:S(2)}, u32[]{:S(2)}) %collective-permute-start.7) | collective-permute-done | bytes 163872 | tf_op jit(solution)/shard_map/ppermute | solution.py:310
  38.1 2.0 %coarse.1 = bf16[4,16,512]{2,1,0:T(8,128)(2,1)} custom-call(bf16[160,256]{1,0:T(8,128)(2,1)S(1)} %get-tuple-element.68.y_ref.own_ref, bf16[160,256]{1,0:T(8,128)(2,1)S(1)} %collective-permute-done.5.near_ref, bf16[80,256]{1,0:T(8,128)(2,1)S(1)} %collective-permute-done.3.halo_ref, bf16[160,256]{1,0:T(8,128)(2,1)S(1)} %collective-permute-done.6.far_ref, ...), custom_call_target="tpu_custom_call" | custom-call | flops 2147483648 | bytes 1048576 | tf_op jit(solution)/shard_map/coarse/pallas_call | solution.py:318
  (19 shorter events, 0.1 us)
Async XLA Ops:
  1.0 7.3 %copy-start = (bf16[16,16,2048]{2,1,0:T(8,128)(2,1)S(1)}, bf16[16,16,2048]{2,1,0:T(8,128)(2,1)}, u32[]{:S(2)}) copy-start(bf16[16,16,2048]{2,1,0:T(8,128)(2,1)} %x_ref.1) | copy-start | bytes 3145732
  1.1 18.1 %collective-permute-start = (bf16[5,16,16,128]{3,2,1,0:T(8,128)(2,1)S(1)}, bf16[5,16,16,128]{3,2,1,0:T(8,128)(2,1)S(1)}, u32[]{:S(2)}, u32[]{:S(2)}) collective-permute-start(bf16[5,16,16,128]{3,2,1,0:T(8,128)(2,1)S(1)} %get-tuple-element.46), channel_id=1, source_target_pairs={{0,124},{1,125},{2,126},{3,127},{4,0},{5,1},{6,2},{7,3},{8,4},{9,5... | collective-permute-start | bytes 983048 | tf_op jit(solution)/shard_map/ppermute | solution.py:310
  8.3 5.1 %copy-start.2 = (bf16[3,3,3,64,128]{4,3,2,1,0:T(8,128)(2,1)S(1)}, bf16[3,3,3,64,128]{4,3,2,1,0:T(8,128)(2,1)}, u32[]{:S(2)}) copy-start(bf16[3,3,3,64,128]{4,3,2,1,0:T(8,128)(2,1)} %w1_raw.1) | copy-start | bytes 1327108
  8.3 5.1 %copy-start.3 = (bf16[3,3,64,64]{3,2,1,0:T(8,128)(2,1)S(1)}, bf16[3,3,64,64]{3,2,1,0:T(8,128)(2,1)}, u32[]{:S(2)}) copy-start(bf16[3,3,64,64]{3,2,1,0:T(8,128)(2,1)} %wp_raw.1) | copy-start | bytes 221188
  8.3 5.1 %copy-start.4 = (bf16[3,3,64,64]{3,2,1,0:T(8,128)(2,1)S(1)}, bf16[3,3,64,64]{3,2,1,0:T(8,128)(2,1)}, u32[]{:S(2)}) copy-start(bf16[3,3,64,64]{3,2,1,0:T(8,128)(2,1)} %wp2_raw.1) | copy-start | bytes 221188
  8.4 5.1 %copy-start.5 = (bf16[3,3,64,64]{3,2,1,0:T(8,128)(2,1)S(1)}, bf16[3,3,64,64]{3,2,1,0:T(8,128)(2,1)}, u32[]{:S(2)}) copy-start(bf16[3,3,64,64]{3,2,1,0:T(8,128)(2,1)} %wq_raw.1) | copy-start | bytes 221188
  8.4 5.1 %copy-start.6 = (bf16[3,3,64,64]{3,2,1,0:T(8,128)(2,1)S(1)}, bf16[3,3,64,64]{3,2,1,0:T(8,128)(2,1)}, u32[]{:S(2)}) copy-start(bf16[3,3,64,64]{3,2,1,0:T(8,128)(2,1)} %wq2_raw.1) | copy-start | bytes 221188
  8.5 13.0 %collective-permute-start.1 = (bf16[16,5,16,128]{3,2,1,0:T(8,128)(2,1)S(1)}, bf16[16,5,16,128]{3,2,1,0:T(8,128)(2,1)S(1)}, u32[]{:S(2)}, u32[]{:S(2)}) collective-permute-start(bf16[16,5,16,128]{3,2,1,0:T(8,128)(2,1)S(1)} %band_edge.1), channel_id=1, source_target_pairs={{1,0},{2,1},{3,2},{5,4},{6,5},{7,6},{9,8},{10,9},{11,10},{13,12},{... | collective-permute-start | bytes 983048 | tf_op jit(solution)/shard_map/ppermute | solution.py:310
  11.5 10.0 %collective-permute-start.2 = (bf16[5,5,16,128]{3,2,1,0:T(8,128)(2,1)S(1)}, bf16[5,5,16,128]{3,2,1,0:T(8,128)(2,1)S(1)}, u32[]{:S(2)}, u32[]{:S(2)}) collective-permute-start(bf16[5,5,16,128]{3,2,1,0:T(8,128)(2,1)S(1)} %get-tuple-element.60.corner_ref), channel_id=1, source_target_pairs={{1,124},{2,125},{3,126},{5,0},{6,1},{7,2},{9,4},{10,5},{11,6},{13,... | collective-permute-start | bytes 307208 | tf_op jit(solution)/shard_map/ppermute | solution.py:310
  19.2 2.4 %copy-start.1 = (bf16[3,3,3,128,256]{4,3,2,1,0:T(8,128)(2,1)S(1)}, bf16[3,3,3,128,256]{4,3,2,1,0:T(8,128)(2,1)}, u32[]{:S(2)}) copy-start(bf16[3,3,3,128,256]{4,3,2,1,0:T(8,128)(2,1)} %w2_ref.1) | copy-start | bytes 5308420
  21.5 8.6 %copy-start.7 = (bf16[3,3,3,256,64]{3,4,2,1,0:T(8,128)(2,1)S(1)}, bf16[3,3,3,256,64]{3,4,2,1,0:T(8,128)(2,1)}, u32[]{:S(2)}) copy-start(bf16[3,3,3,256,64]{3,4,2,1,0:T(8,128)(2,1)} %param.15) | copy-start | bytes 2654212
  25.5 7.1 %collective-permute-start.3 = (bf16[80,256]{1,0:T(8,128)(2,1)S(1)}, bf16[80,256]{1,0:T(8,128)(2,1)S(1)}, u32[]{:S(2)}, u32[]{:S(2)}) collective-permute-start(bf16[80,256]{1,0:T(8,128)(2,1)S(1)} %slice.12), channel_id=1, source_target_pairs={{0,4},{1,5},{2,6},{3,7},{4,8},{5,9},{6,10},{7,11},{8,12},{9,13},{1... | collective-permute-start | bytes 122888 | tf_op jit(solution)/shard_map/ppermute | solution.py:310
  26.2 10.4 %collective-permute-start.4 = (bf16[80,256]{1,0:T(8,128)(2,1)S(1)}, bf16[80,256]{1,0:T(8,128)(2,1)S(1)}, u32[]{:S(2)}, u32[]{:S(2)}) collective-permute-start(bf16[80,256]{1,0:T(8,128)(2,1)S(1)} %slice.12), channel_id=1, source_target_pairs={{0,6},{1,7},{2,4},{3,5},{4,10},{5,11},{6,8},{7,9},{8,14},{9,15},{1... | collective-permute-start | bytes 122888 | tf_op jit(solution)/shard_map/ppermute | solution.py:310
  29.1 7.5 %collective-permute-start.5 = (bf16[160,256]{1,0:T(8,128)(2,1)S(1)}, bf16[160,256]{1,0:T(8,128)(2,1)S(1)}, u32[]{:S(2)}, u32[]{:S(2)}) collective-permute-start(bf16[160,256]{1,0:T(8,128)(2,1)S(1)} %get-tuple-element.68.y_ref.own_ref), channel_id=1, source_target_pairs={{0,1},{1,0},{2,3},{3,2},{4,5},{5,4},{6,7},{7,6},{8,9},{9,8},{10,11... | collective-permute-start | bytes 245768 | tf_op jit(solution)/shard_map/ppermute | solution.py:310
  29.1 7.5 %collective-permute-start.6 = (bf16[160,256]{1,0:T(8,128)(2,1)S(1)}, bf16[160,256]{1,0:T(8,128)(2,1)S(1)}, u32[]{:S(2)}, u32[]{:S(2)}) collective-permute-start(bf16[160,256]{1,0:T(8,128)(2,1)S(1)} %get-tuple-element.68.y_ref.own_ref), channel_id=1, source_target_pairs={{0,2},{1,3},{2,0},{3,1},{4,6},{5,7},{6,4},{7,5},{8,10},{9,11},{10,... | collective-permute-start | bytes 245768 | tf_op jit(solution)/shard_map/ppermute | solution.py:310
  36.6 1.5 %collective-permute-start.7 = (bf16[320,256]{1,0:T(8,128)(2,1)S(1)}, bf16[320,256]{1,0:T(8,128)(2,1)S(1)}, u32[]{:S(2)}, u32[]{:S(2)}) collective-permute-start(bf16[320,256]{1,0:T(8,128)(2,1)S(1)} %pad_maximum_fusion), channel_id=1, source_target_pairs={{0,1},{1,0},{2,3},{3,2},{4,5},{5,4},{6,7},{7,6},{8,9},{9,8},{10,11... | collective-permute-start | bytes 491528 | tf_op jit(solution)/shard_map/ppermute | solution.py:310

commit v8 on v7

--- a/solution.py
+++ b/solution.py
@@ -287,16 +287,14 @@
     return total.astype(BF)
 
 
-def coarse_kernel_body(
-    own_ref, near_ref, halo_ref, far_ref, far_halo_ref, last_ref, wc_ref, spread_ref, out_ref, slab, moved,
-):
+def coarse_kernel_body(own_ref, near_ref, far_ref, halo_ref, last_ref, wc_ref, spread_ref, out_ref, slab, moved):
     band = lax.axis_index("blk")
-    blocks = (
-        (0, 2, own_ref[...]), (0, 0, halo_ref[...]), (1, 2, near_ref[...]), (1, 0, last_ref[0:80]),
-        (2, 2, far_ref[...]), (2, 0, far_halo_ref[...]), (3, 2, last_ref[80:240]), (3, 0, last_ref[240:320]),
-    )
-    for place, first, block in blocks:
-        lay(slab, first, jnp.bitwise_xor(band, place), block)
+    odd = 2 * jnp.bitwise_and(band, 1)
+    for place, block in enumerate((own_ref[...], near_ref[...], far_ref[...], last_ref[0:160])):
+        lay(slab, 2, jnp.bitwise_xor(band, place), block)
+    halves = (halo_ref[0:80], halo_ref[80:160], last_ref[240:320], last_ref[160:240])
+    for place, block in enumerate(halves):
+        lay(slab, 0, jnp.bitwise_xor(jnp.bitwise_xor(band, place), odd), block)
     out_ref[...] = coarse_rows(slab, wc_ref, spread_ref, moved, 0, 4).reshape(4, 16, 512)
 
 
@@ -364,22 +362,22 @@
         4 << 30, "columns", *levels, band_edge, corner, *weights, second_reduce_weight,
         aliases={n: n + 1 for n in range(5)},
     )
-    halo = moved_by(y[80:160], 1, lambda b: b)
-    far_halo = moved_by(y[80:160], 1, lambda b: b ^ 2)
-    far = moved_by(y, 0, lambda b: b ^ 2)
     near = moved_by(y, 0, lambda b: b ^ 1)
+    kept, both = lax.optimization_barrier((y, jnp.concatenate([y[80:160], near[80:160]], axis=0)))
+    halo = moved_by(both, 1, lambda b: b ^ 2 if b % 2 else b)
+    far = moved_by(kept, 0, lambda b: b ^ 2)
     wc, spread = run(
         late_kernel,
         (shaped(3, 3, 256, 256), shaped(8, 64, 512)),
         (), 4 << 30, "late", y, jnp.swapaxes(coarse_kernel, 3, 4), limit=8,
     )
-    halo, far_halo, near, far, wc, spread = lax.optimization_barrier((halo, far_halo, near, far, wc, spread))
-    last = moved_by(jnp.concatenate([halo, far, far_halo], axis=0), 0, lambda b: b ^ 1)
+    halo, far, wc, spread = lax.optimization_barrier((halo, far, wc, spread))
+    last = moved_by(jnp.concatenate([far, halo], axis=0), 0, lambda b: b ^ 1)
     return run(
         coarse_kernel_body,
         shaped(4, 16, 512),
         (pltpu.VMEM((6, 18, 8, 256), F32), pltpu.VMEM((512, 128), F32)),
-        2 << 30, "coarse", y, near, halo, far, far_halo, last, wc, spread, limit=16,
+        2 << 30, "coarse", y, near, far, halo, last, wc, spread, limit=16,
     )
 
 

time: 40.3 us -> 40.3 us (level)
  starting transfers between devices: 17.3 us -> 16.5 us
  waiting for transfers between devices: 7.07 us -> 7.79 us
    ppermute x8 -> x7, starting transfers between devices: 17.3 us -> 16.5 us  [moved_by(): return lax.ppermute(x, ('sector', 'blk'), pairs)]
    ppermute x8 -> x7, waiting for transfers between devices: 7.07 us -> 7.79 us  [moved_by(): return lax.ppermute(x, ('sector', 'blk'), pairs)]
  transfers between devices with their start and end apart: 8 -> 7, of which waited for: 3 -> 4; matrix products, arithmetic and copies ran while one was open for 0% -> 0% of each run, Pallas kernels for 21% -> 21%
where the time goes in v8:
time: 40.3 us; the launch traced here: 40.1 us
  starting transfers between devices  16.5 us (41%)
  Pallas kernels  14.4 us (36%)
  waiting for transfers between devices  7.79 us (19%)
  local copies, waits for them, and re-layouts  1.09 us (3%)
    ppermute x7, starting transfers between devices, moved_by(): return lax.ppermute(x, ('sector', 'blk'), pairs)  16.5 us
    pallas_call x7, Pallas kernels, run(): pl.pallas_call(kernel, out_shape=outs, in_specs=[pl.BlockSpec(memory_spac...  14.4 us
    ppermute x7, waiting for transfers between devices, moved_by(): return lax.ppermute(x, ('sector', 'blk'), pairs)  7.79 us
    slice x1, local copies, waits for them, and re-layouts, per_device(): features[0:ROWS]  0.99 us
  transfers between devices with their start and end apart: 7, of which 4 were waited for; matrix products, arithmetic and copies ran while one was open for 0% of the time, Pallas kernels for 21%

profile of v8, /device:TPU:1, one launch (start us, length us, event | category | flops | bytes accessed | tf_op | source)
XLA Modules:
  0.0 40.1 jit_solution(2431068267714283316)
XLA Ops:
  0.0 1.0 %slice.12.x_ref = bf16[5,16,2048]{2,1,0:T(8,128)(2,1)S(1)} slice(bf16[16,16,2048]{2,1,0:T(8,128)(2,1)} %x_ref.1), slice={[0:5], [0:16], [0:2048]} | slice | bytes 655360 | tf_op jit(solution)/shard_map/slice | solution.py:332
  1.0 0.1 sector_edge.1
  1.1 7.2 %collective-permute-start = (bf16[5,16,16,128]{3,2,1,0:T(8,128)(2,1)S(1)}, bf16[5,16,16,128]{3,2,1,0:T(8,128)(2,1)S(1)}, u32[]{:S(2)}, u32[]{:S(2)}) collective-permute-start(bf16[5,16,16,128]{3,2,1,0:T(8,128)(2,1)S(1)} %get-tuple-element.46), channel_id=1, source_target_pairs={{0,124},{1,125},{2,126},{3,127},{4,0},{5,1},{6,2},{7,3},{8,4},{9,5... | collective-permute-start | bytes 983048 | tf_op jit(solution)/shard_map/ppermute | solution.py:308
  8.3 0.0 copy-start.2
  8.3 0.0 copy-start.4
  8.4 0.0 copy-start.5
  8.4 0.1 band_edge.1
  8.5 3.0 %collective-permute-start.1 = (bf16[16,5,16,128]{3,2,1,0:T(8,128)(2,1)S(1)}, bf16[16,5,16,128]{3,2,1,0:T(8,128)(2,1)S(1)}, u32[]{:S(2)}, u32[]{:S(2)}) collective-permute-start(bf16[16,5,16,128]{3,2,1,0:T(8,128)(2,1)S(1)} %band_edge.1), channel_id=1, source_target_pairs={{1,0},{2,1},{3,2},{5,4},{6,5},{7,6},{9,8},{10,9},{11,10},{13,12},{... | collective-permute-start | bytes 983048 | tf_op jit(solution)/shard_map/ppermute | solution.py:308
  11.5 2.0 %collective-permute-start.2 = (bf16[5,5,16,128]{3,2,1,0:T(8,128)(2,1)S(1)}, bf16[5,5,16,128]{3,2,1,0:T(8,128)(2,1)S(1)}, u32[]{:S(2)}, u32[]{:S(2)}) collective-permute-start(bf16[5,5,16,128]{3,2,1,0:T(8,128)(2,1)S(1)} %get-tuple-element.60.corner_ref), channel_id=1, source_target_pairs={{1,124},{2,125},{3,126},{5,0},{6,1},{7,2},{9,4},{10,5},{11,6},{13,... | collective-permute-start | bytes 307208 | tf_op jit(solution)/shard_map/ppermute | solution.py:308
  13.5 5.6 %inner.1 = (bf16[4,256,256]{2,1,0:T(8,128)(2,1)S(1)}, bf16[4,256,256]{2,1,0:T(8,128)(2,1)S(1)}, bf16[4,256,256]{2,1,0:T(8,128)(2,1)S(1)}, bf16[4,256,256]{2,1,0:...) custom-call(bf16[16,16,2048]{2,1,0:T(8,128)(2,1)S(1)} %copy-done, ...), custom_call_target="tpu_custom_call" | custom-call | flops 1048576 | bytes 1048576 | tf_op jit(solution)/shard_map/inner/pallas_call | solution.py:316
  19.2 2.3 %rows.1 = (bf16[22,22,16,256]{3,2,1,0:T(8,128)(2,1)S(1)}, bf16[21,22,16,256]{3,2,1,0:T(8,128)(2,1)S(1)}, bf16[22,20,16,256]{3,2,1,0:T(8,128)(2,1)S(1)}, bf16[21,...) custom-call(bf16[22,22,16,256]{3,2,1,0:T(8,128)(2,1)S(1)} %get-tuple, ...), custom_call_target="tpu_custom_call", output_to_operand_aliasing={{0}: (0, {}), {1}: (1, {}), {2}: (2, {}), {3}: (3, {}), {4}... | custom-call | flops 1048576 | bytes 1048576 | tf_op jit(solution)/shard_map/rows/pallas_call | solution.py:316
  21.5 0.0 collective-permute-done.2.corner_ref
  21.5 0.0 copy-start.7
  21.5 3.9 %columns.1 = (bf16[160,256]{1,0:T(8,128)(2,1)S(1)}, bf16[22,22,16,256]{3,2,1,0:T(8,128)(2,1)S(1)}, bf16[21,22,16,256]{3,2,1,0:T(8,128)(2,1)S(1)}, bf16[22,20,16,...) custom-call(bf16[22,22,16,256]{3,2,1,0:T(8,128)(2,1)S(1)} %get-tuple, ...), custom_call_target="tpu_custom_call", output_to_operand_aliasing={{1}: (0, {}), {2}: (1, {}), {3}: (2, {}), {4}: (3, {}), {5}... | custom-call | flops 4294967296 | bytes 1048576 | tf_op jit(solution)/shard_map/columns/pallas_call | solution.py:316
  25.5 0.1 collective-permute-start.3
  25.6 1.3 %collective-permute-done.3.near_ref = bf16[160,256]{1,0:T(8,128)(2,1)S(1)} collective-permute-done((bf16[160,256]{1,0:T(8,128)(2,1)S(1)}, bf16[160,256]{1,0:T(8,128)(2,1)S(1)}, u32[]{:S(2)}, u32[]{:S(2)}) %collective-permute-start.3) | collective-permute-done | bytes 81952 | tf_op jit(solution)/shard_map/ppermute | solution.py:308
  26.8 3.5 %collective-permute-start.4 = (bf16[160,256]{1,0:T(8,128)(2,1)S(1)}, bf16[160,256]{1,0:T(8,128)(2,1)S(1)}, u32[]{:S(2)}, u32[]{:S(2)}) collective-permute-start(bf16[160,256]{1,0:T(8,128)(2,1)S(1)} %pad_maximum_fusion.1), channel_id=1, source_target_pairs={{0,4},{1,7},{2,6},{3,5},{4,8},{5,11},{6,10},{7,9},{8,12},{9,15},{1... | collective-permute-start | bytes 245768 | tf_op jit(solution)/shard_map/ppermute | solution.py:308
  30.3 0.6 %collective-permute-start.5 = (bf16[160,256]{1,0:T(8,128)(2,1)S(1)}, bf16[160,256]{1,0:T(8,128)(2,1)S(1)}, u32[]{:S(2)}, u32[]{:S(2)}) collective-permute-start(bf16[160,256]{1,0:T(8,128)(2,1)S(1)} %get-tuple-element.70.y_ref.own_ref), channel_id=1, source_target_pairs={{0,2},{1,3},{2,0},{3,1},{4,6},{5,7},{6,4},{7,5},{8,10},{9,11},{10,... | collective-permute-start | bytes 245768 | tf_op jit(solution)/shard_map/ppermute | solution.py:308
  30.9 0.4 late.1
  31.3 5.2 %collective-permute-done.4.halo_ref = bf16[160,256]{1,0:T(8,128)(2,1)S(1)} collective-permute-done((bf16[160,256]{1,0:T(8,128)(2,1)S(1)}, bf16[160,256]{1,0:T(8,128)(2,1)S(1)}, u32[]{:S(2)}, u32[]{:S(2)}) %collective-permute-start.4) | collective-permute-done | bytes 81952 | tf_op jit(solution)/shard_map/ppermute | solution.py:308
  36.5 0.1 collective-permute-done.5.far_ref
  36.6 0.2 collective-permute-start.6
  36.8 1.3 %collective-permute-done.6.last_ref = bf16[320,256]{1,0:T(8,128)(2,1)S(1)} collective-permute-done((bf16[320,256]{1,0:T(8,128)(2,1)S(1)}, bf16[320,256]{1,0:T(8,128)(2,1)S(1)}, u32[]{:S(2)}, u32[]{:S(2)}) %collective-permute-start.6) | collective-permute-done | bytes 163872 | tf_op jit(solution)/shard_map/ppermute | solution.py:308
  38.1 2.0 %coarse.1 = bf16[4,16,512]{2,1,0:T(8,128)(2,1)} custom-call(bf16[160,256]{1,0:T(8,128)(2,1)S(1)} %get-tuple-element.70.y_ref.own_ref, bf16[160,256]{1,0:T(8,128)(2,1)S(1)} %collective-permute-done.3.near_ref, bf16[160,256]{1,0:T(8,128)(2,1)S(1)} %collective-permute-done.5.far_ref, bf16[160,256]{1,0:T(8,128)(2,1)S(1)} %collective-permute-done.4.halo_ref, ...), custom_call_target="tpu_custom_call" | custom-call | flops 2147483648 | bytes 1048576 | tf_op jit(solution)/shard_map/coarse/pallas_call | solution.py:316
  (19 shorter events, 0.1 us)
Async XLA Ops:
  1.0 7.3 %copy-start = (bf16[16,16,2048]{2,1,0:T(8,128)(2,1)S(1)}, bf16[16,16,2048]{2,1,0:T(8,128)(2,1)}, u32[]{:S(2)}) copy-start(bf16[16,16,2048]{2,1,0:T(8,128)(2,1)} %x_ref.1) | copy-start | bytes 3145732
  1.1 18.1 %collective-permute-start = (bf16[5,16,16,128]{3,2,1,0:T(8,128)(2,1)S(1)}, bf16[5,16,16,128]{3,2,1,0:T(8,128)(2,1)S(1)}, u32[]{:S(2)}, u32[]{:S(2)}) collective-permute-start(bf16[5,16,16,128]{3,2,1,0:T(8,128)(2,1)S(1)} %get-tuple-element.46), channel_id=1, source_target_pairs={{0,124},{1,125},{2,126},{3,127},{4,0},{5,1},{6,2},{7,3},{8,4},{9,5... | collective-permute-start | bytes 983048 | tf_op jit(solution)/shard_map/ppermute | solution.py:308
  8.3 5.1 %copy-start.2 = (bf16[3,3,3,64,128]{4,3,2,1,0:T(8,128)(2,1)S(1)}, bf16[3,3,3,64,128]{4,3,2,1,0:T(8,128)(2,1)}, u32[]{:S(2)}) copy-start(bf16[3,3,3,64,128]{4,3,2,1,0:T(8,128)(2,1)} %w1_raw.1) | copy-start | bytes 1327108
  8.3 5.1 %copy-start.3 = (bf16[3,3,64,64]{3,2,1,0:T(8,128)(2,1)S(1)}, bf16[3,3,64,64]{3,2,1,0:T(8,128)(2,1)}, u32[]{:S(2)}) copy-start(bf16[3,3,64,64]{3,2,1,0:T(8,128)(2,1)} %wp_raw.1) | copy-start | bytes 221188
  8.3 5.1 %copy-start.4 = (bf16[3,3,64,64]{3,2,1,0:T(8,128)(2,1)S(1)}, bf16[3,3,64,64]{3,2,1,0:T(8,128)(2,1)}, u32[]{:S(2)}) copy-start(bf16[3,3,64,64]{3,2,1,0:T(8,128)(2,1)} %wp2_raw.1) | copy-start | bytes 221188
  8.4 5.1 %copy-start.5 = (bf16[3,3,64,64]{3,2,1,0:T(8,128)(2,1)S(1)}, bf16[3,3,64,64]{3,2,1,0:T(8,128)(2,1)}, u32[]{:S(2)}) copy-start(bf16[3,3,64,64]{3,2,1,0:T(8,128)(2,1)} %wq_raw.1) | copy-start | bytes 221188
  8.4 5.1 %copy-start.6 = (bf16[3,3,64,64]{3,2,1,0:T(8,128)(2,1)S(1)}, bf16[3,3,64,64]{3,2,1,0:T(8,128)(2,1)}, u32[]{:S(2)}) copy-start(bf16[3,3,64,64]{3,2,1,0:T(8,128)(2,1)} %wq2_raw.1) | copy-start | bytes 221188
  8.5 13.0 %collective-permute-start.1 = (bf16[16,5,16,128]{3,2,1,0:T(8,128)(2,1)S(1)}, bf16[16,5,16,128]{3,2,1,0:T(8,128)(2,1)S(1)}, u32[]{:S(2)}, u32[]{:S(2)}) collective-permute-start(bf16[16,5,16,128]{3,2,1,0:T(8,128)(2,1)S(1)} %band_edge.1), channel_id=1, source_target_pairs={{1,0},{2,1},{3,2},{5,4},{6,5},{7,6},{9,8},{10,9},{11,10},{13,12},{... | collective-permute-start | bytes 983048 | tf_op jit(solution)/shard_map/ppermute | solution.py:308
  11.5 10.0 %collective-permute-start.2 = (bf16[5,5,16,128]{3,2,1,0:T(8,128)(2,1)S(1)}, bf16[5,5,16,128]{3,2,1,0:T(8,128)(2,1)S(1)}, u32[]{:S(2)}, u32[]{:S(2)}) collective-permute-start(bf16[5,5,16,128]{3,2,1,0:T(8,128)(2,1)S(1)} %get-tuple-element.60.corner_ref), channel_id=1, source_target_pairs={{1,124},{2,125},{3,126},{5,0},{6,1},{7,2},{9,4},{10,5},{11,6},{13,... | collective-permute-start | bytes 307208 | tf_op jit(solution)/shard_map/ppermute | solution.py:308
  19.2 2.4 %copy-start.1 = (bf16[3,3,3,128,256]{4,3,2,1,0:T(8,128)(2,1)S(1)}, bf16[3,3,3,128,256]{4,3,2,1,0:T(8,128)(2,1)}, u32[]{:S(2)}) copy-start(bf16[3,3,3,128,256]{4,3,2,1,0:T(8,128)(2,1)} %w2_ref.1) | copy-start | bytes 5308420
  21.5 9.4 %copy-start.7 = (bf16[3,3,3,256,64]{3,4,2,1,0:T(8,128)(2,1)S(1)}, bf16[3,3,3,256,64]{3,4,2,1,0:T(8,128)(2,1)}, u32[]{:S(2)}) copy-start(bf16[3,3,3,256,64]{3,4,2,1,0:T(8,128)(2,1)} %param.15) | copy-start | bytes 2654212
  25.5 1.4 %collective-permute-start.3 = (bf16[160,256]{1,0:T(8,128)(2,1)S(1)}, bf16[160,256]{1,0:T(8,128)(2,1)S(1)}, u32[]{:S(2)}, u32[]{:S(2)}) collective-permute-start(bf16[160,256]{1,0:T(8,128)(2,1)S(1)} %get-tuple-element.70.y_ref.own_ref), channel_id=1, source_target_pairs={{0,1},{1,0},{2,3},{3,2},{4,5},{5,4},{6,7},{7,6},{8,9},{9,8},{10,11... | collective-permute-start | bytes 245768 | tf_op jit(solution)/shard_map/ppermute | solution.py:308
  26.8 9.7 %collective-permute-start.4 = (bf16[160,256]{1,0:T(8,128)(2,1)S(1)}, bf16[160,256]{1,0:T(8,128)(2,1)S(1)}, u32[]{:S(2)}, u32[]{:S(2)}) collective-permute-start(bf16[160,256]{1,0:T(8,128)(2,1)S(1)} %pad_maximum_fusion.1), channel_id=1, source_target_pairs={{0,4},{1,7},{2,6},{3,5},{4,8},{5,11},{6,10},{7,9},{8,12},{9,15},{1... | collective-permute-start | bytes 245768 | tf_op jit(solution)/shard_map/ppermute | solution.py:308
  30.3 6.3 %collective-permute-start.5 = (bf16[160,256]{1,0:T(8,128)(2,1)S(1)}, bf16[160,256]{1,0:T(8,128)(2,1)S(1)}, u32[]{:S(2)}, u32[]{:S(2)}) collective-permute-start(bf16[160,256]{1,0:T(8,128)(2,1)S(1)} %get-tuple-element.70.y_ref.own_ref), channel_id=1, source_target_pairs={{0,2},{1,3},{2,0},{3,1},{4,6},{5,7},{6,4},{7,5},{8,10},{9,11},{10,... | collective-permute-start | bytes 245768 | tf_op jit(solution)/shard_map/ppermute | solution.py:308
  36.6 1.5 %collective-permute-start.6 = (bf16[320,256]{1,0:T(8,128)(2,1)S(1)}, bf16[320,256]{1,0:T(8,128)(2,1)S(1)}, u32[]{:S(2)}, u32[]{:S(2)}) collective-permute-start(bf16[320,256]{1,0:T(8,128)(2,1)S(1)} %pad_maximum_fusion), channel_id=1, source_target_pairs={{0,1},{1,0},{2,3},{3,2},{4,5},{5,4},{6,7},{7,6},{8,9},{9,8},{10,11... | collective-permute-start | bytes 491528 | tf_op jit(solution)/shard_map/ppermute | solution.py:308
